TPU v7x, 256 devices: a whole 4x4x8 slice. The times are simulated.
256 devices in a mesh: gx: 16 (over x_lo, y, core), gy: 8 (over z), gz: 2 (over x_hi).
Axes of the slice: x: 4 (x_hi: 2, x_lo: 2; x = x_hi * 2 + x_lo), y: 4, z: 8, core: 2. Of those that a mesh axis runs over, the one named last changes fastest.
Arguments:
- sections: bfloat16 [12, 1024, 2048], P('gz', 'gy', 'gx'), may hold values from -12 to 12
Outputs:
- corr_maps: bfloat16 [12, 2, 32, 64, 4096], P('gz', None, 'gy', 'gx')
All inputs are finite; a program needn't handle non-finite values.
Results may differ from a plain program's by a relative error of at most 0.011.
Values may be sent and summed in bfloat16 or wider, within the bound.
No kernel may reach another device: no remote copies, remote signals or barrier semaphores. Data moves between devices by JAX's collectives and lax.ppermute only.
A program may use at most 64 MiB of HBM per device.

v0:
```python
import math

import jax
import jax.numpy as jnp
from jax import lax
from jax.sharding import PartitionSpec as P

PATCH = 64
STRIDE = 32


def with_halo(block, sides, width):
    for axis, dim in sides:
        count = lax.axis_size(axis)
        forward = [(i, i + 1) for i in range(count - 1)]
        backward = [(target, source) for source, target in forward]
        low = lax.ppermute(
            lax.slice_in_dim(block, block.shape[dim] - width, None, axis=dim), axis, forward
        )
        high = lax.ppermute(lax.slice_in_dim(block, 0, width, axis=dim), axis, backward)
        block = jnp.concatenate([low, block, high], axis=dim)
    return block


def passed_along(value, axis, steps):
    count = lax.axis_size(axis)
    first, last = (max(0, -steps), min(count, count - steps))
    return lax.ppermute(value, axis, [(source, source + steps) for source in range(first, last)])


def tables():
    indices = jnp.arange(PATCH, dtype=jnp.int32)
    product = indices[:, None] * indices[None, :] % PATCH
    angles = product.astype(jnp.float32) * (2.0 * math.pi / PATCH)
    cosine = jnp.cos(angles).astype(jnp.bfloat16)
    sine_table = jnp.sin(angles).astype(jnp.bfloat16)
    first_table = jnp.concatenate([cosine, -sine_table], 1)
    inverse = jnp.concatenate(
        [jnp.concatenate([cosine, sine_table], 1), jnp.concatenate([-sine_table, cosine], 1)], 0
    )
    last_table = jnp.stack([cosine, -sine_table], 2)
    return (first_table, cosine, sine_table, inverse, last_table)


def cut_patches(padded):
    count, rows, cols = padded.shape
    n_rows = rows // STRIDE - 1
    n_cols = cols // STRIDE - 1
    blocks = padded.reshape(count, n_rows + 1, STRIDE, cols)
    row_pairs = jnp.concatenate([blocks[:, :-1], blocks[:, 1:]], axis=2)
    col_blocks = row_pairs.reshape(count, n_rows, PATCH, n_cols + 1, STRIDE)
    both = jnp.concatenate([col_blocks[:, :, :, :-1], col_blocks[:, :, :, 1:]], axis=4)
    return both.transpose(0, 1, 3, 2, 4)


def forward(pixels, first_table, cosine, sine_table):
    pixels = pixels.astype(jnp.float32)
    centre = jnp.mean(pixels, axis=(-2, -1), keepdims=True)
    centered = pixels - centre
    spread = jnp.mean(centered * centered, axis=(-2, -1), keepdims=True)
    normed = (centered * lax.rsqrt(spread + 1e-05) * (1.0 / PATCH)).astype(jnp.bfloat16)
    g_cat = jnp.einsum(
        "...xy,yc->...xc", normed, first_table, preferred_element_type=jnp.float32
    ).astype(jnp.bfloat16)
    along_cos = jnp.einsum("ux,...xc->...uc", cosine, g_cat, preferred_element_type=jnp.float32)
    along_sin = jnp.einsum("ux,...xc->...uc", sine_table, g_cat, preferred_element_type=jnp.float32)
    f_re = along_cos[..., :PATCH] + along_sin[..., PATCH:]
    f_im = along_cos[..., PATCH:] - along_sin[..., :PATCH]
    return jnp.concatenate([f_re, f_im], -1).astype(jnp.bfloat16)


def correlate(spec_here, spec_next, inverse, last_table):
    here = spec_here.astype(jnp.float32)
    there = spec_next.astype(jnp.float32)
    q_re = here[..., :PATCH] * there[..., :PATCH] + here[..., PATCH:] * there[..., PATCH:]
    q_im = here[..., PATCH:] * there[..., :PATCH] - here[..., :PATCH] * there[..., PATCH:]
    q_cat = jnp.concatenate([q_re, q_im], -1).astype(jnp.bfloat16)
    h_cat = jnp.einsum(
        "...uc,cd->...ud", q_cat, inverse, preferred_element_type=jnp.float32
    ).astype(jnp.bfloat16)
    h_split = h_cat.reshape(h_cat.shape[:-1] + (2, PATCH))
    maps = jnp.einsum("xuk,...uky->...xy", last_table, h_split, preferred_element_type=jnp.float32)
    maps = maps * (1.0 / (PATCH * PATCH))
    return maps.reshape(maps.shape[:-2] + (PATCH * PATCH,)).astype(jnp.bfloat16)


def local(sections):
    count = sections.shape[0]
    first_table, cosine, sine_table, inverse, last_table = tables()
    padded = with_halo(sections, (("gx", 2), ("gy", 1)), STRIDE // 2)
    spectra = forward(cut_patches(padded), first_table, cosine, sine_table)
    following = passed_along(spectra[:2], "gz", -1)
    extended = jnp.concatenate([spectra, following], 0)
    results = []
    for lag in (1, 2):
        results.append(correlate(spectra, extended[lag : lag + count], inverse, last_table))
    return jnp.stack(results, 1)


def solution(mesh):
    return jax.shard_map(
        local,
        mesh=mesh,
        in_specs=(P("gz", "gy", "gx"),),
        out_specs=P("gz", None, "gy", "gx", None),
        check_vma=False,
    )
```

profile of v0, /device:TPU:98, one launch (start us, length us, event | category | flops | bytes accessed | tf_op | source)
XLA Modules:
  0.0 82.3 jit_solution(898938034497075359)
XLA Ops:
  0.0 1.1 %fusion.56 = (bf16[6,128,16]{2,1,0:T(8,128)(2,1)S(1)}, bf16[6,128,16]{2,1,0:T(8,128)(2,1)S(1)}) fusion(bf16[6,128,128]{2,1,0:T(8,128)(2,1)} %param.1), kind=kLoop, calls=%fused_computation.98 | loop fusion | bytes 98304 | tf_op jit(solution)/shard_map/slice | solution.py:18
  1.1 1.9 %collective-permute-start = (bf16[6,128,16]{2,1,0:T(8,128)(2,1)S(1)}, bf16[6,128,16]{2,1,0:T(8,128)(2,1)S(1)}, u32[]{:S(2)}, u32[]{:S(2)}) collective-permute-start(bf16[6,128,16]{2,1,0:T(8,128)(2,1)S(1)} %get-tuple-element.21), channel_id=1, source_target_pairs={{0,16},{16,32},{32,48},{48,64},{64,80},{80,96},{96,112},{112,128},... | collective-permute-start | bytes 73736 | tf_op jit(solution)/shard_map/ppermute | solution.py:17
  3.1 5.8 %collective-permute-start.1 = (bf16[6,128,16]{2,1,0:T(8,128)(2,1)S(1)}, bf16[6,128,16]{2,1,0:T(8,128)(2,1)S(1)}, u32[]{:S(2)}, u32[]{:S(2)}) collective-permute-start(bf16[6,128,16]{2,1,0:T(8,128)(2,1)S(1)} %get-tuple-element.22), channel_id=1, source_target_pairs={{16,0},{32,16},{48,32},{64,48},{80,64},{96,80},{112,96},{128,112},... | collective-permute-start | bytes 73736 | tf_op jit(solution)/shard_map/ppermute | solution.py:20
  8.8 0.2 sine_convert_fusion.1
  9.0 1.3 %collective-permute-done = bf16[6,128,16]{2,1,0:T(8,128)(2,1)S(1)} collective-permute-done((bf16[6,128,16]{2,1,0:T(8,128)(2,1)S(1)}, bf16[6,128,16]{2,1,0:T(8,128)(2,1)S(1)}, u32[]{:S(2)}, u32[]{:S(2)}) %collective-permute-start) | collective-permute-done | bytes 24608 | tf_op jit(solution)/shard_map/ppermute | solution.py:17
  10.2 1.8 %collective-permute-done.1 = bf16[6,128,16]{2,1,0:T(8,128)(2,1)S(1)} collective-permute-done((bf16[6,128,16]{2,1,0:T(8,128)(2,1)S(1)}, bf16[6,128,16]{2,1,0:T(8,128)(2,1)S(1)}, u32[]{:S(2)}, u32[]{:S(2)}) %collective-permute-start.1) | collective-permute-done | bytes 24608 | tf_op jit(solution)/shard_map/ppermute | solution.py:20
  12.0 0.9 %pad_maximum_fusion.8 = (bf16[6,16,160]{2,1,0:T(8,128)(2,1)S(1)}, bf16[6,16,160]{2,1,0:T(8,128)(2,1)S(1)}) fusion(bf16[6,128,16]{2,1,0:T(8,128)(2,1)S(1)} %collective-permute-done.1, bf16[6,128,128]{2,1,0:T(8,128)(2,1)} %param.1, bf16[6,128,16]{2,1,0:T(8,128)(2,1)S(1)} %collective-permute-done), kind=kLoop, calls=%fused_computation.48 | loop fusion | flops 184320 | bytes 307200 | tf_op jit(solution)/shard_map/slice | solution.py:18
  12.9 5.0 %collective-permute-start.2 = (bf16[6,16,160]{2,1,0:T(8,128)(2,1)S(1)}, bf16[6,16,160]{2,1,0:T(8,128)(2,1)S(1)}, u32[]{:S(2)}, u32[]{:S(2)}) collective-permute-start(bf16[6,16,160]{2,1,0:T(8,128)(2,1)S(1)} %get-tuple-element.17), channel_id=1, source_target_pairs={{0,2},{2,4},{4,6},{6,8},{8,10},{10,12},{12,14},{1,3},{3,5},{5,7},{... | collective-permute-start | bytes 92168 | tf_op jit(solution)/shard_map/ppermute | solution.py:17
  17.9 1.9 %collective-permute-start.3 = (bf16[6,16,160]{2,1,0:T(8,128)(2,1)S(1)}, bf16[6,16,160]{2,1,0:T(8,128)(2,1)S(1)}, u32[]{:S(2)}, u32[]{:S(2)}) collective-permute-start(bf16[6,16,160]{2,1,0:T(8,128)(2,1)S(1)} %get-tuple-element.18), channel_id=1, source_target_pairs={{2,0},{4,2},{6,4},{8,6},{10,8},{12,10},{14,12},{3,1},{5,3},{7,5},{... | collective-permute-start | bytes 92168 | tf_op jit(solution)/shard_map/ppermute | solution.py:20
  19.8 0.1 fusion.39
  20.0 0.0 collective-permute-done.2
  20.0 5.1 %collective-permute-done.3 = bf16[6,16,160]{2,1,0:T(8,128)(2,1)S(1)} collective-permute-done((bf16[6,16,160]{2,1,0:T(8,128)(2,1)S(1)}, bf16[6,16,160]{2,1,0:T(8,128)(2,1)S(1)}, u32[]{:S(2)}, u32[]{:S(2)}) %collective-permute-start.3) | collective-permute-done | bytes 30752 | tf_op jit(solution)/shard_map/ppermute | solution.py:20
  25.1 1.2 %pad_maximum_fusion.4 = bf16[6,160,160]{2,1,0:T(8,128)(2,1)S(1)} fusion(bf16[6,16,160]{2,1,0:T(8,128)(2,1)S(1)} %collective-permute-done.3, bf16[6,128,16]{2,1,0:T(8,128)(2,1)S(1)} %collective-permute-done.1, bf16[6,128,128]{2,1,0:T(8,128)(2,1)} %param.1, bf16[6,128,16]{2,1,0:T(8,128)(2,1)S(1)} %collective-permute-done, ...), kind=kLoop, calls=%fused_computation.45 | loop fusion | flops 1536000 | bytes 614400 | tf_op jit(solution)/shard_map/concatenate | solution.py:21
  26.3 0.1 fusion.55
  26.4 0.1 pad_maximum_fusion.3
  26.5 0.7 copy.10
  27.2 0.3 fusion.54
  27.5 0.6 bitcast_reduce_fusion
  28.1 0.9 %fusion.6 = f32[6,4,4]{2,1,0:T(4,128)S(1)} fusion(f32[6,4,4]{2,1,0:T(4,128)S(1)} %broadcast_multiply_fusion, bf16[6,4,64,4,32]{2,4,3,1,0:T(8,128)(2,1)S(1)} %get-tuple-element.16, bf16[6,4,64,4,32]{2,4,3,1,0:T(8,128)(2,1)S(1)} %get-tuple-element.15), kind=kLoop, calls=%fused_computation.12 | loop fusion | flops 2752416 | bytes 787200 | tf_op jit(solution)/shard_map/reduce_sum | solution.py:60
  29.0 1.4 %convolution_convert_fusion.2 = bf16[6,4,4,64,128]{4,3,2,1,0:T(8,128)(2,1)S(1)} fusion(f32[6,4,4]{2,1,0:T(4,128)S(1)} %add_rsqrt_fusion, f32[6,4,4]{2,1,0:T(4,128)S(1)} %broadcast_multiply_fusion, bf16[6,4,64,4,32]{2,4,3,1,0:T(8,128)(2,1)S(1)} %get-tuple-element.16, bf16[6,4,64,4,32]{2,4,3,1,0:T(8,128)(2,1)S(1)} %get-tuple-element.15, ...), kind=kOutput, calls=%fused_computation.24 | convolution fusion | flops 104628224 | bytes 2376448 | tf_op jit(solution)/shard_map/...xy,yc->...xc/dot_general | solution.py:62
  30.4 0.7 convolution_bitcast_fusion
  31.1 0.7 convolution_bitcast_fusion.1
  31.7 1.7 %fusion = (bf16[6,4,4,64,64]{4,3,2,1,0:T(8,128)(2,1)S(1)}, bf16[6,4,4,64,64]{4,3,2,1,0:T(8,128)(2,1)S(1)}) fusion(f32[6,4,4,64,128]{4,3,2,1,0:T(8,128)S(1)} %convolution_bitcast_fusion, f32[6,4,4,64,128]{4,3,2,1,0:T(8,128)S(1)} %convolution_bitcast_fusion.1), kind=kLoop, calls=%fused_computation.1 | loop fusion | flops 1572864 | bytes 7864320 | tf_op jit(solution)/shard_map/convert.6
  33.5 0.3 fusion.21
  33.8 1.3 %collective-permute-start.4 = (bf16[2,4,4,64,128]{4,3,2,1,0:T(8,128)(2,1)S(1)}, bf16[2,4,4,64,128]{4,3,2,1,0:T(8,128)(2,1)S(1)}, u32[]{:S(2)}, u32[]{:S(2)}) collective-permute-start(bf16[2,4,4,64,128]{4,3,2,1,0:T(8,128)(2,1)S(1)} %fusion.21), channel_id=1, source_target_pairs={{1,0},{3,2},{5,4},{7,6},{9,8},{11,10},{13,12},{15,14},{17,16},{19,... | collective-permute-start | bytes 1572872 | tf_op jit(solution)/shard_map/ppermute | solution.py:28
  35.1 0.1 cosine_convert_fusion
  35.2 0.1 fusion.34
  35.4 0.8 maximum_convert_fusion
  36.1 13.2 %collective-permute-done.4 = bf16[2,4,4,64,128]{4,3,2,1,0:T(8,128)(2,1)S(1)} collective-permute-done((bf16[2,4,4,64,128]{4,3,2,1,0:T(8,128)(2,1)S(1)}, bf16[2,4,4,64,128]{4,3,2,1,0:T(8,128)(2,1)S(1)}, u32[]{:S(2)}, u32[]{:S(2)}) %collective-permute-start.4) | collective-permute-done | bytes 524320 | tf_op jit(solution)/shard_map/ppermute | solution.py:28
  49.3 0.9 %pad_maximum_fusion = bf16[8,4,4,64,128]{4,3,2,1,0:T(8,128)(2,1)S(1)} fusion(bf16[2,4,4,64,128]{4,3,2,1,0:T(8,128)(2,1)S(1)} %collective-permute-done.4, bf16[6,4,4,64,64]{4,3,2,1,0:T(8,128)(2,1)S(1)} %get-tuple-element.9, bf16[6,4,4,64,64]{4,3,2,1,0:T(8,128)(2,1)S(1)} %get-tuple-element.10), kind=kLoop, calls=%fused_computation.19 | loop fusion | flops 6291456 | bytes 4194304 | tf_op jit(solution)/shard_map/concatenate | solution.py:93
  50.2 0.8 %slice_convert_fusion.1 = (f32[6,4,4,64,128]{4,3,2,1,0:T(8,128)S(1)}, f32[6,4,4,64,128]{4,3,2,1,0:T(8,128)S(1)}) fusion(bf16[8,4,4,64,128]{4,3,2,1,0:T(8,128)(2,1)S(1)} %pad_maximum_fusion), kind=kLoop, calls=%fused_computation.26 | loop fusion | flops 1572864 | bytes 9437184 | tf_op jit(solution)/shard_map/convert_element_type | solution.py:74
  51.1 4.0 %add_convert_fusion.1 = (bf16[6,4,4,64,64]{4,3,2,1,0:T(8,128)(2,1)S(1)}, bf16[6,4,4,64,64]{4,3,2,1,0:T(8,128)(2,1)S(1)}, bf16[6,4,4,64,64]{4,3,2,1,0:T(8,128)(2,1)}, bf16[6,4,4,64,64]{4,3,2,1,0:T(8,128)(2,1)}) fusion(f32[6,4,4,64,128]{4,3,2,1,0:T(8,128)S(1)} %get-tuple-element.13, f32[6,4,4,64,128]{4,3,2,1,0:T(8,128)S(1)} %maximum_convert_fusion, ...), kind=kLoop, calls=%fused_computation.18 | loop fusion | flops 6291456 | bytes 12582912 | tf_op jit(solution)/shard_map/convert.3
  55.1 2.2 %convolution_convert_fusion.1 = bf16[6,4,4,64,128]{4,3,2,1,0:T(8,128)(2,1)} fusion(bf16[6,4,4,64,64]{4,3,2,1,0:T(8,128)(2,1)S(1)} %get-tuple-element.6, bf16[6,4,4,64,64]{4,3,2,1,0:T(8,128)(2,1)S(1)} %get-tuple-element.5, bf16[64,64]{1,0:T(8,128)(2,1)S(1)} %get-tuple-element.24, bf16[64,64]{1,0:T(8,128)(2,1)S(1)} %fusion.39, ...), kind=kOutput, calls=%fused_computation.23 | convolution fusion | flops 205389824 | bytes 3170304 | tf_op jit(solution)/shard_map/...uc,cd->...ud/dot_general | solution.py:78
  57.3 3.1 %copy.25 = bf16[6,4,4,64,128]{3,4,2,1,0:T(8,128)(2,1)S(1)} copy(bf16[6,4,4,64,128]{4,3,2,1,0:T(8,128)(2,1)} %convolution_convert_fusion.1) | data formatting | bytes 3145728 | tf_op jit(solution)/shard_map/reshape | solution.py:81
  60.4 2.1 %fusion.19 = bf16[6,4,4,64,64]{3,4,2,1,0:T(8,128)(2,1)} fusion(bf16[6,4,4,64,2,64]{3,5,4,2,1,0:T(8,128)(2,1)S(1)} %bitcast.76, bf16[64,64,1]{1,0,2:T(8,128)(2,1)S(1)} %fusion.34, bf16[64,64,1]{1,0,2:T(8,128)(2,1)S(1)} %cosine_convert_fusion), kind=kOutput, calls=%fused_computation.39 | convolution fusion | flops 101457920 | bytes 2375680 | tf_op jit(solution)/shard_map/xuk,...uky->...xy/dot_general | solution.py:82
  62.5 0.0 copy-start
  62.5 2.7 %copy.13 = bf16[6,4,4,64,64]{4,3,2,1,0:T(8,128)(2,1)} copy(bf16[6,4,4,64,64]{3,4,2,1,0:T(8,128)(2,1)} %fusion.19) | data formatting | bytes 1572864 | tf_op jit(solution)/shard_map/convert_element_type | solution.py:84
  65.2 3.7 %convert_element_type.146 = bf16[6,1,4,4,4096]{4,3,2,0,1:T(4,128)(2,1)} reshape(bf16[6,4,4,64,64]{4,3,2,1,0:T(8,128)(2,1)} %copy.13) | data formatting | bytes 1572864 | tf_op jit(solution)/shard_map/convert_element_type | solution.py:84
  68.9 0.0 copy-done
  68.9 0.0 copy-done.1
  68.9 2.2 %convolution_convert_fusion = bf16[6,4,4,64,128]{4,3,2,1,0:T(8,128)(2,1)} fusion(bf16[6,4,4,64,64]{4,3,2,1,0:T(8,128)(2,1)S(1)} %copy-done, bf16[6,4,4,64,64]{4,3,2,1,0:T(8,128)(2,1)S(1)} %copy-done.1, bf16[64,64]{1,0:T(8,128)(2,1)S(1)} %get-tuple-element.24, bf16[64,64]{1,0:T(8,128)(2,1)S(1)} %fusion.39, bf16[64,64]{1,0:T(8,128)(2,1)S(1)} %get-tuple-element.23), kind=kOutput, calls=%fused_computation.22 | convolution fusion | flops 205389824 | bytes 3170304 | tf_op jit(solution)/shard_map/...uc,cd->...ud/dot_general | solution.py:78
  71.1 3.1 %copy.26 = bf16[6,4,4,64,128]{3,4,2,1,0:T(8,128)(2,1)S(1)} copy(bf16[6,4,4,64,128]{4,3,2,1,0:T(8,128)(2,1)} %convolution_convert_fusion) | data formatting | bytes 3145728 | tf_op jit(solution)/shard_map/reshape | solution.py:81
  74.2 2.1 %fusion.20 = bf16[6,4,4,64,64]{3,4,2,1,0:T(8,128)(2,1)} fusion(bf16[6,4,4,64,2,64]{3,5,4,2,1,0:T(8,128)(2,1)S(1)} %bitcast.75, bf16[64,64,1]{1,0,2:T(8,128)(2,1)S(1)} %fusion.34, bf16[64,64,1]{1,0,2:T(8,128)(2,1)S(1)} %cosine_convert_fusion), kind=kOutput, calls=%fused_computation.40 | convolution fusion | flops 101457920 | bytes 2375680 | tf_op jit(solution)/shard_map/xuk,...uky->...xy/dot_general | solution.py:82
  76.3 2.0 %copy.15 = bf16[6,4,4,64,64]{4,3,2,1,0:T(8,128)(2,1)S(1)} copy(bf16[6,4,4,64,64]{3,4,2,1,0:T(8,128)(2,1)} %fusion.20) | data formatting | bytes 1572864 | tf_op jit(solution)/shard_map/convert_element_type | solution.py:84
  78.2 1.1 %convert_element_type.151 = bf16[6,1,4,4,4096]{4,3,2,0,1:T(4,128)(2,1)S(1)} reshape(bf16[6,4,4,64,64]{4,3,2,1,0:T(8,128)(2,1)S(1)} %copy.15) | data formatting | bytes 1572864 | tf_op jit(solution)/shard_map/convert_element_type | solution.py:84
  79.4 0.0 copy-done.2
  79.4 1.1 %pad_maximum_fusion.2 = bf16[6,2,4,4,4096]{4,3,2,0,1:T(4,128)(2,1)S(1)} fusion(bf16[6,1,4,4,4096]{4,3,2,0,1:T(4,128)(2,1)S(1)} %convert_element_type.151, bf16[6,1,4,4,4096]{4,3,2,0,1:T(4,128)(2,1)S(1)} %copy-done.2), kind=kLoop, calls=%fused_computation.35 | loop fusion | flops 786432 | bytes 3145728 | tf_op jit(solution)/shard_map/stack | solution.py:97
  80.5 1.8 %copy.16 = bf16[6,2,4,4,4096]{4,3,2,1,0:T(4,128)(2,1)} copy(bf16[6,2,4,4,4096]{4,3,2,0,1:T(4,128)(2,1)S(1)} %pad_maximum_fusion.2) | data formatting | bytes 3145728 | tf_op jit(solution)/shard_map/stack | solution.py:97
  (4 shorter events, 0.0 us)
Async XLA Ops:
  1.1 9.1 %collective-permute-start = (bf16[6,128,16]{2,1,0:T(8,128)(2,1)S(1)}, bf16[6,128,16]{2,1,0:T(8,128)(2,1)S(1)}, u32[]{:S(2)}, u32[]{:S(2)}) collective-permute-start(bf16[6,128,16]{2,1,0:T(8,128)(2,1)S(1)} %get-tuple-element.21), channel_id=1, source_target_pairs={{0,16},{16,32},{32,48},{48,64},{64,80},{80,96},{96,112},{112,128},... | collective-permute-start | bytes 73736 | tf_op jit(solution)/shard_map/ppermute | solution.py:17
  3.1 8.9 %collective-permute-start.1 = (bf16[6,128,16]{2,1,0:T(8,128)(2,1)S(1)}, bf16[6,128,16]{2,1,0:T(8,128)(2,1)S(1)}, u32[]{:S(2)}, u32[]{:S(2)}) collective-permute-start(bf16[6,128,16]{2,1,0:T(8,128)(2,1)S(1)} %get-tuple-element.22), channel_id=1, source_target_pairs={{16,0},{32,16},{48,32},{64,48},{80,64},{96,80},{112,96},{128,112},... | collective-permute-start | bytes 73736 | tf_op jit(solution)/shard_map/ppermute | solution.py:20
  12.9 7.1 %collective-permute-start.2 = (bf16[6,16,160]{2,1,0:T(8,128)(2,1)S(1)}, bf16[6,16,160]{2,1,0:T(8,128)(2,1)S(1)}, u32[]{:S(2)}, u32[]{:S(2)}) collective-permute-start(bf16[6,16,160]{2,1,0:T(8,128)(2,1)S(1)} %get-tuple-element.17), channel_id=1, source_target_pairs={{0,2},{2,4},{4,6},{6,8},{8,10},{10,12},{12,14},{1,3},{3,5},{5,7},{... | collective-permute-start | bytes 92168 | tf_op jit(solution)/shard_map/ppermute | solution.py:17
  17.9 7.2 %collective-permute-start.3 = (bf16[6,16,160]{2,1,0:T(8,128)(2,1)S(1)}, bf16[6,16,160]{2,1,0:T(8,128)(2,1)S(1)}, u32[]{:S(2)}, u32[]{:S(2)}) collective-permute-start(bf16[6,16,160]{2,1,0:T(8,128)(2,1)S(1)} %get-tuple-element.18), channel_id=1, source_target_pairs={{2,0},{4,2},{6,4},{8,6},{10,8},{12,10},{14,12},{3,1},{5,3},{7,5},{... | collective-permute-start | bytes 92168 | tf_op jit(solution)/shard_map/ppermute | solution.py:20
  33.8 15.5 %collective-permute-start.4 = (bf16[2,4,4,64,128]{4,3,2,1,0:T(8,128)(2,1)S(1)}, bf16[2,4,4,64,128]{4,3,2,1,0:T(8,128)(2,1)S(1)}, u32[]{:S(2)}, u32[]{:S(2)}) collective-permute-start(bf16[2,4,4,64,128]{4,3,2,1,0:T(8,128)(2,1)S(1)} %fusion.21), channel_id=1, source_target_pairs={{1,0},{3,2},{5,4},{7,6},{9,8},{11,10},{13,12},{15,14},{17,16},{19,... | collective-permute-start | bytes 1572872 | tf_op jit(solution)/shard_map/ppermute | solution.py:28
  62.5 6.4 %copy-start = (bf16[6,4,4,64,64]{4,3,2,1,0:T(8,128)(2,1)S(1)}, bf16[6,4,4,64,64]{4,3,2,1,0:T(8,128)(2,1)}, u32[]{:S(2)}) copy-start(bf16[6,4,4,64,64]{4,3,2,1,0:T(8,128)(2,1)} %get-tuple-element.11) | copy-start | bytes 2359300
  62.5 6.4 %copy-start.1 = (bf16[6,4,4,64,64]{4,3,2,1,0:T(8,128)(2,1)S(1)}, bf16[6,4,4,64,64]{4,3,2,1,0:T(8,128)(2,1)}, u32[]{:S(2)}) copy-start(bf16[6,4,4,64,64]{4,3,2,1,0:T(8,128)(2,1)} %get-tuple-element.12) | copy-start | bytes 2359300
  76.3 3.1 %copy-start.2 = (bf16[6,1,4,4,4096]{4,3,2,0,1:T(4,128)(2,1)S(1)}, bf16[6,1,4,4,4096]{4,3,2,0,1:T(4,128)(2,1)}, u32[]{:S(2)}) copy-start(bf16[6,1,4,4,4096]{4,3,2,0,1:T(4,128)(2,1)} %convert_element_type.146) | copy-start | bytes 2359300
where the time goes:
time: 83.3 us; the launch traced here: 82.3 us
  waiting for transfers between devices  21.3 us (26%)
  local copies, waits for them, and re-layouts  19.6 us (24%)
  starting transfers between devices  15.9 us (19%)
  other arithmetic  14 us (17%)
  matrix products  11.4 us (14%)
    ppermute x1, waiting for transfers between devices, passed_along(): lax.ppermute(value, axis, [(source, source + steps) for source in range(f...  13.2 us
    convert_element_type x4, local copies, waits for them, and re-layouts, correlate(): return maps.reshape(maps.shape[:-2] + (PATCH * PATCH,)).astype(jnp.bfloat16)  9.46 us
    ppermute x2, starting transfers between devices, with_halo(): lax.ppermute(lax.slice_in_dim(block, 0, width, axis=dim), axis, backward)  7.67 us
    ppermute x2, starting transfers between devices, with_halo(): lax.ppermute(lax.slice_in_dim(block, block.shape[dim] - width, None, axis...  6.96 us
    ppermute x2, waiting for transfers between devices, with_halo(): lax.ppermute(lax.slice_in_dim(block, 0, width, axis=dim), axis, backward)  6.86 us
    reshape x2, local copies, waits for them, and re-layouts, correlate(): h_split = h_cat.reshape(h_cat.shape[:-1] + (2, PATCH))  6.12 us
    another operation x2, other arithmetic  5.77 us
    dot_general x2, matrix products, correlate(): jnp.einsum('...uc,cd->...ud', q_cat, inverse, preferred_element_type=jnp....  4.38 us
  transfers between devices with their start and end apart: 5, of which 4 were waited for; matrix products, arithmetic and copies ran while one was open for 2% of the time, Pallas kernels for 0%

commit v1 on v0

v1 whole, which is shorter than its diff:
```python
import functools
import math

import jax
import jax.numpy as jnp
import ml_dtypes
import numpy as np
from jax import lax
from jax.experimental import pallas as pl
from jax.experimental.pallas import tpu as pltpu
from jax.sharding import PartitionSpec as P

PATCH = 64
F32 = jnp.float32
BF16 = jnp.bfloat16
VMEM = pl.BlockSpec(memory_space=pltpu.VMEM)
ANY = pl.BlockSpec(memory_space=pl.ANY)


def rounded(values):
    return values.astype(np.float32).astype(ml_dtypes.bfloat16)


@functools.cache
def constants():
    index = np.arange(PATCH)
    angle = (index[:, None] * index[None, :] % PATCH) * (2.0 * math.pi / PATCH)
    cos = rounded(np.cos(angle)).astype(np.float64)
    sin = rounded(np.sin(angle)).astype(np.float64)
    sign = 1.0 - 2.0 * (index % 2)

    rows = np.zeros((160, 2, 4, 32))
    for j in range(4):
        rows[32 * j : 32 * j + 64, 0, j] = cos[:, :32]
        rows[32 * j : 32 * j + 64, 1, j] = -sin[:, :32]
        rows[32 * j : 32 * j + 64, 1, j, 0] = sign
    rows = rows.reshape(160, 256)

    forward = np.block([[cos, sin], [-sin, cos]])
    order = np.concatenate([index[0::2], index[1::2]])
    inverse = np.block([[cos[order], -sin[order]], [sin[order], cos[order]]])

    last = np.zeros((2, 4, 32, 4, 64))
    weight = np.where(index[:32] == 0, 1.0, 2.0)[:, None] / 4096.0
    for j in range(4):
        last[0, j, :, j] = weight * cos[:32]
        last[1, j, :, j] = -weight * sin[:32]
        last[1, j, 0, j] = sign / 4096.0
    even = last.reshape(256, 256)
    odd = last[:, :, :, [1, 0, 3, 2]].reshape(256, 256)

    column = np.full(256, -1000)
    column[:128] = np.arange(128) + 16
    column[128:144] = np.arange(16)
    column[192:208] = np.arange(16) + 144
    inside = np.stack([(column >= 32 * j) & (column < 32 * j + 64) for j in range(4)], 1)
    inside = inside.astype(np.float64)
    same_even = inside[:, [0, 2]] @ inside[:, [0, 2]].T
    same_odd = inside[:, [1, 3]] @ inside[:, [1, 3]].T
    spread = np.repeat(inside, 32, axis=1)
    lane_odd = (np.arange(128) // 32 % 2).astype(np.float64)
    means = np.concatenate([same_even, same_odd, spread], 1)
    totals = np.concatenate([spread * (1 - lane_odd), spread * lane_odd], 0)
    return dict(
        own=rounded(rows[16:144]),
        sides=rounded(np.concatenate([rows[:16], rows[144:]], 0)),
        forward=rounded(forward),
        inverse=rounded(inverse),
        even=rounded(even),
        odd=rounded(odd),
        means=rounded(means),
        totals=rounded(totals),
    )


NAMES = ("own", "sides", "forward", "inverse", "even", "odd", "means", "totals")


def dot(a, b):
    return jnp.dot(a, b, preferred_element_type=F32)


def dot_exact(a, ones):
    high = a.astype(BF16)
    rest = a - high.astype(F32)
    middle = rest.astype(BF16)
    low = (rest - middle.astype(F32)).astype(BF16)
    n = a.shape[0]
    parts = dot(jnp.concatenate([high, middle, low], 0), ones)
    return parts[2 * n :] + parts[n : 2 * n] + parts[:n]


def lanes(shape):
    return lax.broadcasted_iota(jnp.int32, shape, len(shape) - 1)


def edges_kernel(s_ref, a_ref, b_ref):
    odd = lax.axis_index("gx") % 2 == 1
    lane = lanes((128, 128))
    left = jnp.zeros((128, 128), F32)
    right = jnp.zeros((128, 128), F32)
    for s in range(6):
        block = s_ref[s].astype(F32)
        here = (lane // 16) == s
        first = pltpu.roll(block, 16 * s, 1) if s else block
        last = pltpu.roll(block, 16 * s + 16, 1)
        left = jnp.where(here, first, left)
        right = jnp.where(here, last, right)
    left = left.astype(BF16)
    right = right.astype(BF16)
    a_ref[...] = jnp.where(odd, left, right)
    b_ref[...] = jnp.where(odd, right, left)


def rows_kernel(s_ref, xa_ref, xb_ref, e_ref, a_ref, b_ref, z_ref):
    odd_x = lax.axis_index("gx") % 2 == 1
    odd_y = lax.axis_index("gy") % 2 == 1
    xa = xa_ref[...].astype(F32)
    xb = xb_ref[...].astype(F32)
    left = jnp.where(odd_x, xa, xb)
    right = jnp.where(odd_x, xb, xa)
    low = lanes((128, 128)) < 64
    e0 = jnp.where(low, left, pltpu.roll(right, 64, 1)).astype(BF16)
    e1 = jnp.where(low, pltpu.roll(left, 64, 1), right).astype(BF16)
    e_ref[0] = e0
    e_ref[1] = e1
    first = jnp.concatenate([s_ref[s, :16] for s in range(6)] + [e0[:16], e1[:16]], 0)
    last = jnp.concatenate([s_ref[s, 112:] for s in range(6)] + [e0[112:], e1[112:]], 0)
    a_ref[...] = jnp.where(odd_y, first, last)
    b_ref[...] = jnp.where(odd_y, last, first)
    z_ref[0] = s_ref[0]
    z_ref[1] = s_ref[1]
    z_ref[2] = e0


def spectra(count, first, slot_f, own, edge, ya_ref, yb_ref, flag, c, w):
    odd_y = lax.axis_index("gy") % 2 == 1
    top = jnp.where(odd_y, ya_ref[...], yb_ref[...])
    bottom = jnp.where(odd_y, yb_ref[...], ya_ref[...])
    lane = lanes((64, 128))
    zero_slot = lane % 32 == 0
    row_lane = lanes((8, 128))
    sides = c["sides"][...]
    groups = []
    for g in range((count + 3) // 4):
        groups.append(
            jnp.concatenate(
                [top[96 + 16 * g : 112 + 16 * g], edge(g), bottom[96 + 16 * g : 112 + 16 * g]], 0
            )
        )

    def column_stats(block):
        block = block.astype(F32).reshape(5, 32, 128)
        mean = jnp.sum(block, 1, keepdims=True) * (1.0 / 32)
        centred = block - mean
        return mean[:, 0], jnp.sum(centred * centred, 1)

    edge_stats = [column_stats(g) for g in groups]
    w["mu"][...] = jnp.zeros(w["mu"].shape, F32)
    w["sq"][...] = jnp.zeros(w["sq"].shape, F32)
    for s in range(count):
        q, g = s % 4, s // 4
        block = jnp.concatenate([top[16 * s : 16 * s + 16], own(s), bottom[16 * s : 16 * s + 16]], 0)
        gap0 = jnp.zeros((16 * q, 256), BF16)
        gap1 = jnp.zeros((48 - 16 * q, 256), BF16)
        pieces = [c["own"][...], gap0, sides[:16], gap1, gap0, sides[16:], gap1]
        table = jnp.concatenate([p for p in pieces if p.shape[0]], 0)
        w["g"][s] = dot(jnp.concatenate([block, groups[g]], 1), table)
        mean, square = column_stats(block)
        mean_e, square_e = edge_stats[g]
        if q:
            mean_e = pltpu.roll(mean_e, 128 - 16 * q, 1)
            square_e = pltpu.roll(square_e, 128 - 16 * q, 1)
        w["mu"][:, s, :128] = mean
        w["mu"][:, s, 128:] = mean_e
        w["sq"][:, s, :128] = square
        w["sq"][:, s, 128:] = square_e

    mu = w["mu"][...]
    sq = w["sq"][...]
    mu0, mu1 = mu[:4].reshape(32, 256), mu[1:].reshape(32, 256)
    sq01 = (sq[:4] + sq[1:]).reshape(32, 256)
    sums = dot_exact(mu0 + mu1, c["means"][...])
    total = []
    for parity in range(2):
        centre = sums[:, 256 * parity : 256 * parity + 256] * (1.0 / 128)
        d0, d1 = mu0 - centre, mu1 - centre
        total.append(sq01 + 32.0 * (d0 * d0 + d1 * d1))
    variance = dot_exact(jnp.concatenate(total, 1), c["totals"][...]) * (1.0 / 4096)
    scale = lax.rsqrt(variance + 1e-05) * (1.0 / PATCH)
    if flag is not None:
        scale = scale * flag
    w["scale"][...] = scale.reshape(4, 8, 128)
    centre = jnp.where(lanes((32, 128)) % 32 == 0, sums[:, 512:] * 0.5, 0.0)
    w["centre"][...] = centre.reshape(4, 8, 128)

    w["g32"][...] = jnp.zeros(w["g32"].shape, F32)

    def section(s, carry):
        for pair in range(2):
            columns = []
            for i in (2 * pair, 2 * pair + 1):
                re = w["g"][s, 32 * i : 32 * i + 64, :128] - w["centre"][i, pl.ds(s, 1), :]
                im = w["g"][s, 32 * i : 32 * i + 64, 128:]
                slot = 4 * (s + first) + i
                w["g32"][...] = jnp.where(lane % 32 == slot, pltpu.roll(im, slot, 1), w["g32"][...])
                im = jnp.where(zero_slot, 0.0, im)
                columns.append(jnp.concatenate([re, im], 0).astype(BF16))
            f = dot(c["forward"][...], jnp.concatenate(columns, 1))
            for n, i in enumerate((2 * pair, 2 * pair + 1)):
                part = f[:, 128 * n : 128 * n + 128] * w["scale"][i, pl.ds(s, 1), :]
                w["f"][s + slot_f, i] = part.astype(BF16)
        return carry

    lax.fori_loop(0, count, section, 0)

    scale32 = jnp.zeros((8, 128), F32)
    sublane = lax.broadcasted_iota(jnp.int32, (8, 128), 0)
    for i in range(4):
        scale32 = scale32 + jnp.where(row_lane % 32 == 4 * (sublane + first) + i, w["scale"][i], 0.0)
    scale32 = jnp.sum(scale32, 0, keepdims=True)
    f = dot(c["forward"][:, :64], w["g32"][...].astype(BF16))
    return (f * scale32).astype(BF16)


def maps(lo, hi, f32, offset, c, w, o_ref):
    f32 = f32.astype(F32)
    re, im = f32[:64], f32[64:]
    for k in range(2):
        re_p = pltpu.roll(re, 128 - 4 * (k + 1), 1)
        im_p = pltpu.roll(im, 128 - 4 * (k + 1), 1)
        q = jnp.concatenate([re * re_p + im * im_p, im * re_p - re * im_p], 0).astype(BF16)
        w["h32"][k] = dot(c["inverse"][:64], q)
    lane = lanes((64, 128))
    zero_slot = lane % 32 == 0
    low = lanes((32, 128)) < 64

    def copy(p):
        return pltpu.make_async_copy(
            w["o"].at[p - lo], o_ref.at[p // 2, p % 2], w["sem"].at[p - lo]
        )

    def pair(p, carry):
        s, k = p // 2, p % 2
        even, odd = [], []
        for half in range(2):
            columns = []
            for i in (2 * half, 2 * half + 1):
                here = w["f"][s - offset, i].astype(F32)
                there = w["f"][s + k + 1 - offset, i].astype(F32)
                f_re, f_im, p_re, p_im = here[:64], here[64:], there[:64], there[64:]
                q = jnp.concatenate([f_re * p_re + f_im * p_im, f_im * p_re - f_re * p_im], 0)
                columns.append(q.astype(BF16))
            h = dot(c["inverse"][...], jnp.concatenate(columns, 1))
            for n, i in enumerate((2 * half, 2 * half + 1)):
                h_re = h[:64, 128 * n : 128 * n + 128]
                special = pltpu.roll(w["h32"][k], 128 - (4 * s + i), 1)
                h_im = jnp.where(zero_slot, special, h[64:, 128 * n : 128 * n + 128])
                h_cat = jnp.concatenate([h_re, h_im], 1).astype(BF16)
                even.append(h_cat[:32])
                odd.append(h_cat[32:])
        even = dot(jnp.concatenate(even, 0), c["even"][...])
        odd = dot(jnp.concatenate(odd, 0), c["odd"][...])
        for i in range(4):
            for half in range(2):
                e = even[32 * i : 32 * i + 32, 128 * half : 128 * half + 128]
                o = odd[32 * i : 32 * i + 32, 128 * half : 128 * half + 128]
                w["mix"][i, pl.ds(2 * half, 32, stride=4), :] = jnp.where(low, e, o)
                w["mix"][i, pl.ds(2 * half + 1, 32, stride=4), :] = pltpu.roll(
                    jnp.where(low, o, e), 64, 1
                )
            w["o"][p - lo, i] = w["mix"][i].astype(BF16)
        copy(p).start()
        return carry

    lax.fori_loop(lo, hi, pair, 0)
    for p in range(lo, hi):
        copy(p).wait()


SCRATCH = dict(
    g=lambda n: pltpu.VMEM((n, 160, 256), F32),
    mu=lambda n: pltpu.VMEM((5, 8, 256), F32),
    sq=lambda n: pltpu.VMEM((5, 8, 256), F32),
    scale=lambda n: pltpu.VMEM((4, 8, 128), F32),
    centre=lambda n: pltpu.VMEM((4, 8, 128), F32),
    g32=lambda n: pltpu.VMEM((64, 128), F32),
    h32=lambda n: pltpu.VMEM((2, 64, 128), F32),
    mix=lambda n: pltpu.VMEM((4, 128, 128), F32),
)


def own_kernel(s_ref, e_ref, ya_ref, yb_ref, *refs):
    c = dict(zip(NAMES, refs[: len(NAMES)]))
    o_ref, f_ref, f32_ref = refs[len(NAMES) : len(NAMES) + 3]
    w = dict(zip((*SCRATCH, "o", "sem"), refs[len(NAMES) + 3 :]))
    w["f"] = f_ref
    f32 = spectra(6, 0, 0, lambda s: s_ref[s], lambda g: e_ref[g], ya_ref, yb_ref, None, c, w)
    f32_ref[...] = f32
    maps(0, 9, f32, 0, c, w, o_ref)


def rest_kernel(z_ref, ya_ref, yb_ref, f_ref, f32_ref, *refs):
    c = dict(zip(NAMES, refs[: len(NAMES)]))
    o_ref = refs[len(NAMES) + 1]
    w = dict(zip((*SCRATCH, "f", "o", "sem"), refs[len(NAMES) + 2 :]))
    flag = jnp.where(lax.axis_index("gz") == 0, 1.0, 0.0)
    w["f"][0] = f_ref[4]
    w["f"][1] = f_ref[5]
    extra = spectra(2, 6, 2, lambda s: z_ref[s], lambda g: z_ref[2], ya_ref, yb_ref, flag, c, w)
    f32 = jnp.where(lanes((128, 128)) % 32 >= 24, extra.astype(F32), f32_ref[...].astype(F32))
    maps(9, 12, f32, 4, c, w, o_ref)


def exchange(value_a, value_b, axis, count):
    pairs_a = [(n, n ^ 1) for n in range(count)]
    pairs_b = [(n, n + 1 if n % 2 else n - 1) for n in range(1, count - 1)]
    return lax.ppermute(value_a, axis, pairs_a), lax.ppermute(value_b, axis, pairs_b)


def other(value):
    return lax.ppermute(value, "gz", [(0, 1), (1, 0)])


def shaped(*shape):
    return jax.ShapeDtypeStruct(shape, BF16)


def local(sections):
    table = [jnp.asarray(constants()[name]) for name in NAMES]
    params = pltpu.CompilerParams(vmem_limit_bytes=32 * 2**20)
    edge = shaped(128, 128)
    xa, xb = pl.pallas_call(
        edges_kernel, out_shape=(edge, edge), in_specs=[VMEM], out_specs=(VMEM, VMEM)
    )(sections)
    xa, xb = exchange(xa, xb, "gx", lax.axis_size("gx"))
    edges, ya, yb, z = pl.pallas_call(
        rows_kernel,
        out_shape=(shaped(2, 128, 128), edge, edge, shaped(3, 128, 128)),
        in_specs=[VMEM] * 3,
        out_specs=(VMEM,) * 4,
    )(sections, xa, xb)
    ya, yb = exchange(ya, yb, "gy", lax.axis_size("gy"))
    z = other(z)
    za, zb = other(ya), other(yb)
    scratch = [make(6) for make in SCRATCH.values()]
    out, f, f32 = pl.pallas_call(
        own_kernel,
        out_shape=(shaped(6, 2, 4, 128, 128), shaped(6, 4, 128, 128), edge),
        in_specs=[VMEM] * (4 + len(table)),
        out_specs=(ANY, VMEM, VMEM),
        scratch_shapes=scratch + [pltpu.VMEM((9, 4, 128, 128), BF16), pltpu.SemaphoreType.DMA((9,))],
        compiler_params=params,
        cost_estimate=pl.CostEstimate(flops=10**9, bytes_accessed=4 * 10**6, transcendentals=0),
    )(sections, edges, ya, yb, *table)
    scratch = [make(2) for make in SCRATCH.values()]
    out = pl.pallas_call(
        rest_kernel,
        out_shape=shaped(6, 2, 4, 128, 128),
        in_specs=[VMEM] * (5 + len(table)) + [ANY],
        out_specs=ANY,
        scratch_shapes=scratch
        + [
            pltpu.VMEM((4, 4, 128, 128), BF16),
            pltpu.VMEM((3, 4, 128, 128), BF16),
            pltpu.SemaphoreType.DMA((3,)),
        ],
        input_output_aliases={5 + len(table): 0},
        compiler_params=params,
    )(z, za, zb, f, f32, *table, out)
    out = out.reshape(6, 2, 4, 32, 4, 128).transpose(0, 1, 2, 4, 3, 5)
    return out.reshape(6, 2, 4, 4, 4096)


def solution(mesh):
    return jax.shard_map(
        local,
        mesh=mesh,
        in_specs=(P("gz", "gy", "gx"),),
        out_specs=P("gz", None, "gy", "gx", None),
        check_vma=False,
    )
```

time: 83.3 us -> 42.5 us (0.51)
  waiting for transfers between devices: 21.3 us -> 2.54 us
  other arithmetic: 14 us -> 0 us
  Pallas kernels: 0 us -> 13.2 us
  matrix products: 11.4 us -> 0 us
  local copies, waits for them, and re-layouts: 19.6 us -> 9.13 us
  starting transfers between devices: 15.9 us -> 16.8 us
    ppermute x5 -> x7, waiting for transfers between devices: 21.3 us -> 2.54 us  [the longest x2 2.52 us: exchange(): lax.ppermute(value_b, axis, pairs_b)]
    pallas_call x0 -> x4, Pallas kernels: none -> 13.2 us  [the longest x1 6.62 us: local(): pl.pallas_call(own_kernel, out_shape=(shaped(6, 2, 4, 128, 128), shaped(6...]
    dot_general x7 -> x0, matrix products: 11.4 us -> none  [the longest x2 4.38 us: correlate(): jnp.einsum('...uc,cd->...ud', q_cat, inverse, preferred_element_type=jnp....]
    convert_element_type x4 -> x0, local copies, waits for them, and re-layouts: 9.46 us -> none  [correlate(): return maps.reshape(maps.shape[:-2] + (PATCH * PATCH,)).astype(jnp.bfloat16)]
    unnamed x6 -> x26, local copies, waits for them, and re-layouts: 0.01 us -> 9.13 us
    another operation x3 -> x0, other arithmetic: 6.88 us -> none
    reshape x2 -> x0, local copies, waits for them, and re-layouts: 6.12 us -> none  [correlate(): h_split = h_cat.reshape(h_cat.shape[:-1] + (2, PATCH))]
    concatenate x4 -> x0, other arithmetic: 2.52 us -> none  [the longest x1 1.17 us: with_halo(): block = jnp.concatenate([low, block, high], axis=dim)]
  transfers between devices with their start and end apart: 5 -> 7, of which waited for: 4 -> 1; matrix products, arithmetic and copies ran while one was open for 2% -> 0% of each run, Pallas kernels for 0% -> 16%
where the time goes in v1:
time: 42.5 us; the launch traced here: 41.7 us
  starting transfers between devices  16.8 us (40%)
  Pallas kernels  13.2 us (31%)
  local copies, waits for them, and re-layouts  9.13 us (21%)
  waiting for transfers between devices  2.54 us (6%)
    ppermute x2, starting transfers between devices, exchange(): lax.ppermute(value_b, axis, pairs_b)  10.9 us
    unnamed x26, local copies, waits for them, and re-layouts  9.13 us
    pallas_call x1, Pallas kernels, local(): pl.pallas_call(own_kernel, out_shape=(shaped(6, 2, 4, 128, 128), shaped(6...  6.62 us
    ppermute x3, starting transfers between devices, other(): return lax.ppermute(value, 'gz', [(0, 1), (1, 0)])  5.74 us
    pallas_call x1, Pallas kernels, local(): pl.pallas_call(rest_kernel, out_shape=shaped(6, 2, 4, 128, 128), in_specs...  3.14 us
    ppermute x2, waiting for transfers between devices, exchange(): lax.ppermute(value_b, axis, pairs_b)  2.52 us
    pallas_call x1, Pallas kernels, local(): pl.pallas_call(rows_kernel, out_shape=(shaped(2, 128, 128), edge, edge, s...  1.72 us
    pallas_call x1, Pallas kernels, local(): pl.pallas_call(edges_kernel, out_shape=(edge, edge), in_specs=[VMEM], out...  1.71 us
  transfers between devices with their start and end apart: 7, of which 1 were waited for; matrix products, arithmetic and copies ran while one was open for 0% of the time, Pallas kernels for 16%

profile of v1, /device:TPU:98, one launch (start us, length us, event | category | flops | bytes accessed | tf_op | source)
XLA Modules:
  0.0 41.7 jit_solution(17903974482783859155)
XLA Ops:
  0.0 1.7 %shard_map.91 = (bf16[128,128]{1,0:T(8,128)(2,1)}, bf16[128,128]{1,0:T(8,128)(2,1)}) custom-call(bf16[6,128,128]{2,1,0:T(8,128)(2,1)} %s_ref.5), custom_call_target="tpu_custom_call" | custom-call | tf_op jit(solution)/shard_map/pallas_call | solution.py:333
  1.7 0.0 collective-permute-start
  1.7 5.0 %collective-permute-start.1 = (bf16[128,128]{1,0:T(8,128)(2,1)}, bf16[128,128]{1,0:T(8,128)(2,1)S(1)}, u32[]{:S(2)}, u32[]{:S(2)}) collective-permute-start(bf16[128,128]{1,0:T(8,128)(2,1)} %get-tuple-element.15), channel_id=1, source_target_pairs={{16,32},{32,16},{48,64},{64,48},{80,96},{96,80},{112,128},{128,112... | collective-permute-start | bytes 98312 | tf_op jit(solution)/shard_map/ppermute | solution.py:318
  6.7 0.0 collective-permute-done.xa_ref
  6.7 0.0 copy-start.11
  6.7 2.5 %collective-permute-done.1.xb_ref = bf16[128,128]{1,0:T(8,128)(2,1)S(1)} collective-permute-done((bf16[128,128]{1,0:T(8,128)(2,1)}, bf16[128,128]{1,0:T(8,128)(2,1)S(1)}, u32[]{:S(2)}, u32[]{:S(2)}) %collective-permute-start.1) | collective-permute-done | bytes 32800 | tf_op jit(solution)/shard_map/ppermute | solution.py:318
  9.3 0.0 copy-done.11
  9.3 0.0 copy-start.12
  9.3 0.6 %copy-done.12 = bf16[128,128]{1,0:T(8,128)(2,1)} copy-done((bf16[128,128]{1,0:T(8,128)(2,1)}, bf16[128,128]{1,0:T(8,128)(2,1)S(1)}, u32[]{:S(2)}) %copy-start.12) | copy-done | bytes 32792
  9.9 1.7 %shard_map.92 = (bf16[2,128,128]{2,1,0:T(8,128)(2,1)}, bf16[128,128]{1,0:T(8,128)(2,1)}, bf16[128,128]{1,0:T(8,128)(2,1)}, bf16[3,128,128]{2,1,0:T(8,128)(2,1)}) custom-call(bf16[6,128,128]{2,1,0:T(8,128)(2,1)} %s_ref.5, bf16[128,128]{1,0:T(8,128)(2,1)} %copy-done.11, bf16[128,128]{1,0:T(8,128)(2,1)} %copy-done.12), custom_call_target="tpu_custom_call" | custom-call | tf_op jit(solution)/shard_map/pallas_call | solution.py:337
  11.6 0.1 collective-permute-start.3
  11.7 5.9 %collective-permute-start.5 = (bf16[128,128]{1,0:T(8,128)(2,1)}, bf16[128,128]{1,0:T(8,128)(2,1)S(1)}, u32[]{:S(2)}, u32[]{:S(2)}) collective-permute-start(bf16[128,128]{1,0:T(8,128)(2,1)} %get-tuple-element.18), channel_id=1, source_target_pairs={{2,4},{4,2},{6,8},{8,6},{10,12},{12,10},{3,5},{5,3},{7,9},{9,7},{1... | collective-permute-start | bytes 98312 | tf_op jit(solution)/shard_map/ppermute | solution.py:318
  17.6 2.2 %collective-permute-start.2 = (bf16[3,128,128]{2,1,0:T(8,128)(2,1)}, bf16[3,128,128]{2,1,0:T(8,128)(2,1)S(1)}, u32[]{:S(2)}, u32[]{:S(2)}) collective-permute-start(bf16[3,128,128]{2,1,0:T(8,128)(2,1)} %get-tuple-element.16), channel_id=1, source_target_pairs={{0,1},{1,0},{2,3},{3,2},{4,5},{5,4},{6,7},{7,6},{8,9},{9,8},{10,11... | collective-permute-start | bytes 294920 | tf_op jit(solution)/shard_map/ppermute | solution.py:322
  19.8 0.0 collective-permute-done.3.ya_ref
  19.9 1.4 %collective-permute-start.4 = (bf16[128,128]{1,0:T(8,128)(2,1)S(1)}, bf16[128,128]{1,0:T(8,128)(2,1)S(1)}, u32[]{:S(2)}, u32[]{:S(2)}) collective-permute-start(bf16[128,128]{1,0:T(8,128)(2,1)S(1)} %collective-permute-done.3.ya_ref), channel_id=1, source_target_pairs={{0,1},{1,0},{2,3},{3,2},{4,5},{5,4},{6,7},{7,6},{8,9},{9,8},{10,11... | collective-permute-start | bytes 98312 | tf_op jit(solution)/shard_map/ppermute | solution.py:322
  21.3 0.0 collective-permute-done.5.yb_ref
  21.3 2.1 %collective-permute-start.6 = (bf16[128,128]{1,0:T(8,128)(2,1)S(1)}, bf16[128,128]{1,0:T(8,128)(2,1)S(1)}, u32[]{:S(2)}, u32[]{:S(2)}) collective-permute-start(bf16[128,128]{1,0:T(8,128)(2,1)S(1)} %collective-permute-done.5.yb_ref), channel_id=1, source_target_pairs={{0,1},{1,0},{2,3},{3,2},{4,5},{5,4},{6,7},{7,6},{8,9},{9,8},{10,11... | collective-permute-start | bytes 98312 | tf_op jit(solution)/shard_map/ppermute | solution.py:322
  23.4 0.0 copy-start
  23.4 0.9 %copy-done = bf16[6,128,128]{2,1,0:T(8,128)(2,1)S(1)} copy-done((bf16[6,128,128]{2,1,0:T(8,128)(2,1)S(1)}, bf16[6,128,128]{2,1,0:T(8,128)(2,1)}, u32[]{:S(2)}) %copy-start) | copy-done | bytes 196632
  24.3 0.0 copy-start.1
  24.3 1.0 %copy-done.1 = bf16[256,640]{1,0:T(8,128)(2,1)S(1)} copy-done((bf16[256,640]{1,0:T(8,128)(2,1)S(1)}, bf16[256,640]{1,0:T(8,128)(2,1)}, u32[]{:S(2)}) %copy-start.1) | copy-done | bytes 327704
  25.3 0.0 copy-start.3
  25.3 0.9 %copy-done.3 = bf16[512,128]{1,0:T(8,128)(2,1)S(1)} copy-done((bf16[512,128]{1,0:T(8,128)(2,1)S(1)}, bf16[512,128]{1,0:T(8,128)(2,1)}, u32[]{:S(2)}) %copy-start.3) | copy-done | bytes 131096
  26.2 0.0 copy-start.4
  26.2 0.9 %copy-done.4 = bf16[256,256]{1,0:T(8,128)(2,1)S(1)} copy-done((bf16[256,256]{1,0:T(8,128)(2,1)S(1)}, bf16[256,256]{1,0:T(8,128)(2,1)}, u32[]{:S(2)}) %copy-start.4) | copy-done | bytes 131096
  27.1 0.0 copy-start.5
  27.1 0.9 %copy-done.5 = bf16[256,256]{1,0:T(8,128)(2,1)S(1)} copy-done((bf16[256,256]{1,0:T(8,128)(2,1)S(1)}, bf16[256,256]{1,0:T(8,128)(2,1)}, u32[]{:S(2)}) %copy-start.5) | copy-done | bytes 131096
  28.0 0.0 copy-start.6
  28.0 0.8 %copy-done.6 = bf16[128,256]{1,0:T(8,128)(2,1)S(1)} copy-done((bf16[128,256]{1,0:T(8,128)(2,1)S(1)}, bf16[128,256]{1,0:T(8,128)(2,1)}, u32[]{:S(2)}) %copy-start.6) | copy-done | bytes 65560
  28.8 0.0 copy-start.7
  28.8 0.8 %copy-done.7 = bf16[128,128]{1,0:T(8,128)(2,1)S(1)} copy-done((bf16[128,128]{1,0:T(8,128)(2,1)S(1)}, bf16[128,128]{1,0:T(8,128)(2,1)}, u32[]{:S(2)}) %copy-start.7) | copy-done | bytes 32792
  29.6 0.0 copy-start.8
  29.6 0.8 %copy-done.8 = bf16[128,128]{1,0:T(8,128)(2,1)S(1)} copy-done((bf16[128,128]{1,0:T(8,128)(2,1)S(1)}, bf16[128,128]{1,0:T(8,128)(2,1)}, u32[]{:S(2)}) %copy-start.8) | copy-done | bytes 32792
  30.4 0.0 copy-start.9
  30.4 0.7 %copy-done.9 = bf16[32,256]{1,0:T(8,128)(2,1)S(1)} copy-done((bf16[32,256]{1,0:T(8,128)(2,1)S(1)}, bf16[32,256]{1,0:T(8,128)(2,1)}, u32[]{:S(2)}) %copy-start.9) | copy-done | bytes 16408
  31.1 0.0 copy-start.10
  31.1 0.8 %copy-done.10 = bf16[2,128,128]{2,1,0:T(8,128)(2,1)S(1)} copy-done((bf16[2,128,128]{2,1,0:T(8,128)(2,1)S(1)}, bf16[2,128,128]{2,1,0:T(8,128)(2,1)}, u32[]{:S(2)}) %copy-start.10) | copy-done | bytes 65560
  31.9 0.0 copy-start.2
  31.9 6.6 %shard_map.93 = (bf16[6,2,4,128,128]{4,3,2,1,0:T(8,128)(2,1)}, bf16[6,4,128,128]{3,2,1,0:T(8,128)(2,1)S(1)}, bf16[128,128]{1,0:T(8,128)(2,1)S(1)}) custom-call(bf16[6,128,128]{2,1,0:T(8,128)(2,1)S(1)} %copy-done, bf16[2,128,128]{2,1,0:T(8,128)(2,1)S(1)} %copy-done.10, bf16[128,128]{1,0:T(8,128)(2,1)S(1)} %collective-permute-done.3.ya_ref, ...), custom_call_target="tpu_custom_call" | custom-call | flops 1000000000 | bytes 4000000 | tf_op jit(solution)/shard_map/pallas_call | solution.py:347
  38.5 0.0 collective-permute-done.4.ya_ref
  38.6 0.0 collective-permute-done.6.yb_ref
  38.6 0.0 collective-permute-done.2.z_ref
  38.6 0.0 copy-done.2
  38.6 3.1 %shard_map.94 = bf16[6,2,4,128,128]{4,3,2,1,0:T(8,128)(2,1)} custom-call(bf16[3,128,128]{2,1,0:T(8,128)(2,1)S(1)} %collective-permute-done.2.z_ref, bf16[128,128]{1,0:T(8,128)(2,1)S(1)} %collective-permute-done.4.ya_ref, bf16[128,128]{1,0:T(8,128)(2,1)S(1)} %collective-permute-done.6.yb_ref, ...), custom_call_target="tpu_custom_call", output_to_operand_aliasing={{}: (13, {})} | custom-call | tf_op jit(solution)/shard_map/pallas_call | solution.py:357
Async XLA Ops:
  1.7 5.0 %collective-permute-start = (bf16[128,128]{1,0:T(8,128)(2,1)}, bf16[128,128]{1,0:T(8,128)(2,1)S(1)}, u32[]{:S(2)}, u32[]{:S(2)}) collective-permute-start(bf16[128,128]{1,0:T(8,128)(2,1)} %get-tuple-element.14), channel_id=1, source_target_pairs={{0,16},{16,0},{32,48},{48,32},{64,80},{80,64},{96,112},{112,96},{1... | collective-permute-start | bytes 98312 | tf_op jit(solution)/shard_map/ppermute | solution.py:318
  1.7 7.5 %collective-permute-start.1 = (bf16[128,128]{1,0:T(8,128)(2,1)}, bf16[128,128]{1,0:T(8,128)(2,1)S(1)}, u32[]{:S(2)}, u32[]{:S(2)}) collective-permute-start(bf16[128,128]{1,0:T(8,128)(2,1)} %get-tuple-element.15), channel_id=1, source_target_pairs={{16,32},{32,16},{48,64},{64,48},{80,96},{96,80},{112,128},{128,112... | collective-permute-start | bytes 98312 | tf_op jit(solution)/shard_map/ppermute | solution.py:318
  6.7 2.5 %copy-start.11 = (bf16[128,128]{1,0:T(8,128)(2,1)}, bf16[128,128]{1,0:T(8,128)(2,1)S(1)}, u32[]{:S(2)}) copy-start(bf16[128,128]{1,0:T(8,128)(2,1)S(1)} %collective-permute-done.xa_ref) | copy-start | bytes 98308
  9.3 0.6 %copy-start.12 = (bf16[128,128]{1,0:T(8,128)(2,1)}, bf16[128,128]{1,0:T(8,128)(2,1)S(1)}, u32[]{:S(2)}) copy-start(bf16[128,128]{1,0:T(8,128)(2,1)S(1)} %collective-permute-done.1.xb_ref) | copy-start | bytes 98308
  11.6 8.3 %collective-permute-start.3 = (bf16[128,128]{1,0:T(8,128)(2,1)}, bf16[128,128]{1,0:T(8,128)(2,1)S(1)}, u32[]{:S(2)}, u32[]{:S(2)}) collective-permute-start(bf16[128,128]{1,0:T(8,128)(2,1)} %get-tuple-element.17), channel_id=1, source_target_pairs={{0,2},{2,0},{4,6},{6,4},{8,10},{10,8},{12,14},{14,12},{1,3},{3,1},... | collective-permute-start | bytes 98312 | tf_op jit(solution)/shard_map/ppermute | solution.py:318
  11.7 9.6 %collective-permute-start.5 = (bf16[128,128]{1,0:T(8,128)(2,1)}, bf16[128,128]{1,0:T(8,128)(2,1)S(1)}, u32[]{:S(2)}, u32[]{:S(2)}) collective-permute-start(bf16[128,128]{1,0:T(8,128)(2,1)} %get-tuple-element.18), channel_id=1, source_target_pairs={{2,4},{4,2},{6,8},{8,6},{10,12},{12,10},{3,5},{5,3},{7,9},{9,7},{1... | collective-permute-start | bytes 98312 | tf_op jit(solution)/shard_map/ppermute | solution.py:318
  17.6 20.9 %collective-permute-start.2 = (bf16[3,128,128]{2,1,0:T(8,128)(2,1)}, bf16[3,128,128]{2,1,0:T(8,128)(2,1)S(1)}, u32[]{:S(2)}, u32[]{:S(2)}) collective-permute-start(bf16[3,128,128]{2,1,0:T(8,128)(2,1)} %get-tuple-element.16), channel_id=1, source_target_pairs={{0,1},{1,0},{2,3},{3,2},{4,5},{5,4},{6,7},{7,6},{8,9},{9,8},{10,11... | collective-permute-start | bytes 294920 | tf_op jit(solution)/shard_map/ppermute | solution.py:322
  19.9 18.7 %collective-permute-start.4 = (bf16[128,128]{1,0:T(8,128)(2,1)S(1)}, bf16[128,128]{1,0:T(8,128)(2,1)S(1)}, u32[]{:S(2)}, u32[]{:S(2)}) collective-permute-start(bf16[128,128]{1,0:T(8,128)(2,1)S(1)} %collective-permute-done.3.ya_ref), channel_id=1, source_target_pairs={{0,1},{1,0},{2,3},{3,2},{4,5},{5,4},{6,7},{7,6},{8,9},{9,8},{10,11... | collective-permute-start | bytes 98312 | tf_op jit(solution)/shard_map/ppermute | solution.py:322
  21.3 17.3 %collective-permute-start.6 = (bf16[128,128]{1,0:T(8,128)(2,1)S(1)}, bf16[128,128]{1,0:T(8,128)(2,1)S(1)}, u32[]{:S(2)}, u32[]{:S(2)}) collective-permute-start(bf16[128,128]{1,0:T(8,128)(2,1)S(1)} %collective-permute-done.5.yb_ref), channel_id=1, source_target_pairs={{0,1},{1,0},{2,3},{3,2},{4,5},{5,4},{6,7},{7,6},{8,9},{9,8},{10,11... | collective-permute-start | bytes 98312 | tf_op jit(solution)/shard_map/ppermute | solution.py:322
  23.4 0.9 %copy-start = (bf16[6,128,128]{2,1,0:T(8,128)(2,1)S(1)}, bf16[6,128,128]{2,1,0:T(8,128)(2,1)}, u32[]{:S(2)}) copy-start(bf16[6,128,128]{2,1,0:T(8,128)(2,1)} %s_ref.5) | copy-start | bytes 589828
  24.3 1.0 %copy-start.1 = (bf16[256,640]{1,0:T(8,128)(2,1)S(1)}, bf16[256,640]{1,0:T(8,128)(2,1)}, u32[]{:S(2)}) copy-start(bf16[256,640]{1,0:T(8,128)(2,1)} %constant.22.clone.refs_6_) | copy-start | bytes 983044
  25.3 0.9 %copy-start.3 = (bf16[512,128]{1,0:T(8,128)(2,1)S(1)}, bf16[512,128]{1,0:T(8,128)(2,1)}, u32[]{:S(2)}) copy-start(bf16[512,128]{1,0:T(8,128)(2,1)} %constant.23.clone.refs_7_) | copy-start | bytes 393220
  26.2 0.9 %copy-start.4 = (bf16[256,256]{1,0:T(8,128)(2,1)S(1)}, bf16[256,256]{1,0:T(8,128)(2,1)}, u32[]{:S(2)}) copy-start(bf16[256,256]{1,0:T(8,128)(2,1)} %constant.21.clone.refs_5_) | copy-start | bytes 393220
  27.1 0.9 %copy-start.5 = (bf16[256,256]{1,0:T(8,128)(2,1)S(1)}, bf16[256,256]{1,0:T(8,128)(2,1)}, u32[]{:S(2)}) copy-start(bf16[256,256]{1,0:T(8,128)(2,1)} %constant.20.clone.refs_4_) | copy-start | bytes 393220
  28.0 0.8 %copy-start.6 = (bf16[128,256]{1,0:T(8,128)(2,1)S(1)}, bf16[128,256]{1,0:T(8,128)(2,1)}, u32[]{:S(2)}) copy-start(bf16[128,256]{1,0:T(8,128)(2,1)} %constant.16.clone.refs_0_) | copy-start | bytes 196612
  28.8 0.8 %copy-start.7 = (bf16[128,128]{1,0:T(8,128)(2,1)S(1)}, bf16[128,128]{1,0:T(8,128)(2,1)}, u32[]{:S(2)}) copy-start(bf16[128,128]{1,0:T(8,128)(2,1)} %constant.19.clone.refs_3_) | copy-start | bytes 98308
  29.6 0.8 %copy-start.8 = (bf16[128,128]{1,0:T(8,128)(2,1)S(1)}, bf16[128,128]{1,0:T(8,128)(2,1)}, u32[]{:S(2)}) copy-start(bf16[128,128]{1,0:T(8,128)(2,1)} %constant.18.clone.refs_2_) | copy-start | bytes 98308
  30.4 0.7 %copy-start.9 = (bf16[32,256]{1,0:T(8,128)(2,1)S(1)}, bf16[32,256]{1,0:T(8,128)(2,1)}, u32[]{:S(2)}) copy-start(bf16[32,256]{1,0:T(8,128)(2,1)} %constant.17.clone.refs_1_) | copy-start | bytes 49156
  31.1 0.8 %copy-start.10 = (bf16[2,128,128]{2,1,0:T(8,128)(2,1)S(1)}, bf16[2,128,128]{2,1,0:T(8,128)(2,1)}, u32[]{:S(2)}) copy-start(bf16[2,128,128]{2,1,0:T(8,128)(2,1)} %get-tuple-element.19.e_ref) | copy-start | bytes 196612
  31.9 6.7 %copy-start.2 = (bf16[256,640]{1,0:T(8,128)(2,1)S(1)}, bf16[256,640]{1,0:T(8,128)(2,1)}, u32[]{:S(2)}) copy-start(bf16[256,640]{1,0:T(8,128)(2,1)} %constant.22.clone.refs_6_) | copy-start | bytes 983044

commit v2 on v1

--- a/solution.py
+++ b/solution.py
@@ -14,7 +14,7 @@
 F32 = jnp.float32
 BF16 = jnp.bfloat16
 VMEM = pl.BlockSpec(memory_space=pltpu.VMEM)
-ANY = pl.BlockSpec(memory_space=pl.ANY)
+HBM = pl.BlockSpec(memory_space=pltpu.HBM)
 
 
 def rounded(values):
@@ -61,19 +61,33 @@
     lane_odd = (np.arange(128) // 32 % 2).astype(np.float64)
     means = np.concatenate([same_even, same_odd, spread], 1)
     totals = np.concatenate([spread * (1 - lane_odd), spread * lane_odd], 0)
-    return dict(
-        own=rounded(rows[16:144]),
-        sides=rounded(np.concatenate([rows[:16], rows[144:]], 0)),
-        forward=rounded(forward),
-        inverse=rounded(inverse),
-        even=rounded(even),
-        odd=rounded(odd),
-        means=rounded(means),
-        totals=rounded(totals),
+    tables = dict(
+        own=rows[16:144],
+        sides=np.concatenate([rows[:16], rows[144:]], 0),
+        forward=forward,
+        inverse=inverse,
+        even=even,
+        odd=odd,
+        means=means,
+        totals=totals,
     )
-
-
-NAMES = ("own", "sides", "forward", "inverse", "even", "odd", "means", "totals")
+    pieces, places, at = [], {}, 0
+    for name, table in tables.items():
+        height, width = table.shape
+        places[name] = (at, height, width // 128)
+        pieces += np.split(table, width // 128, 1)
+        at += height * width // 128
+    return rounded(np.concatenate(pieces, 0)), places
+
+
+class Tables:
+    def __init__(self, ref):
+        self.ref = ref
+
+    def __getitem__(self, name):
+        at, height, width = constants()[1][name]
+        pieces = [self.ref[at + height * n : at + height * (n + 1)] for n in range(width)]
+        return jnp.concatenate(pieces, 1) if width > 1 else pieces[0]
 
 
 def dot(a, b):
@@ -94,7 +108,12 @@
     return lax.broadcasted_iota(jnp.int32, shape, len(shape) - 1)
 
 
-def edges_kernel(s_ref, a_ref, b_ref):
+def edges_kernel(s_hbm, t_hbm, a_ref, b_ref, s_ref, t_ref, sem):
+    sections = pltpu.make_async_copy(s_hbm, s_ref, sem.at[0])
+    tables = pltpu.make_async_copy(t_hbm, t_ref, sem.at[1])
+    sections.start()
+    tables.start()
+    sections.wait()
     odd = lax.axis_index("gx") % 2 == 1
     lane = lanes((128, 128))
     left = jnp.zeros((128, 128), F32)
@@ -106,10 +125,9 @@
         last = pltpu.roll(block, 16 * s + 16, 1)
         left = jnp.where(here, first, left)
         right = jnp.where(here, last, right)
-    left = left.astype(BF16)
-    right = right.astype(BF16)
-    a_ref[...] = jnp.where(odd, left, right)
-    b_ref[...] = jnp.where(odd, right, left)
+    a_ref[...] = jnp.where(odd, left, right).astype(BF16)
+    b_ref[...] = jnp.where(odd, right, left).astype(BF16)
+    tables.wait()
 
 
 def rows_kernel(s_ref, xa_ref, xb_ref, e_ref, a_ref, b_ref, z_ref):
@@ -133,39 +151,41 @@
     z_ref[2] = e0
 
 
-def spectra(count, first, slot_f, own, edge, ya_ref, yb_ref, flag, c, w):
-    odd_y = lax.axis_index("gy") % 2 == 1
-    top = jnp.where(odd_y, ya_ref[...], yb_ref[...])
-    bottom = jnp.where(odd_y, yb_ref[...], ya_ref[...])
+def halo_kernel(ya_ref, yb_ref, z_ref):
+    top, bottom = halo(ya_ref, yb_ref)
+    for n, at in enumerate((0, 16, 96)):
+        z_ref[16 * n : 16 * n + 16] = top[at : at + 16]
+        z_ref[48 + 16 * n : 64 + 16 * n] = bottom[at : at + 16]
+
+
+def halo(ya_ref, yb_ref):
+    odd = lax.axis_index("gy") % 2 == 1
+    ya, yb = ya_ref[...], yb_ref[...]
+    return jnp.where(odd, ya, yb), jnp.where(odd, yb, ya)
+
+
+def spectra(count, first, slot_f, sections, edges, flag, c, w):
     lane = lanes((64, 128))
     zero_slot = lane % 32 == 0
     row_lane = lanes((8, 128))
-    sides = c["sides"][...]
-    groups = []
-    for g in range((count + 3) // 4):
-        groups.append(
-            jnp.concatenate(
-                [top[96 + 16 * g : 112 + 16 * g], edge(g), bottom[96 + 16 * g : 112 + 16 * g]], 0
-            )
-        )
-
+    sides = c["sides"]
     def column_stats(block):
         block = block.astype(F32).reshape(5, 32, 128)
         mean = jnp.sum(block, 1, keepdims=True) * (1.0 / 32)
         centred = block - mean
         return mean[:, 0], jnp.sum(centred * centred, 1)
 
-    edge_stats = [column_stats(g) for g in groups]
+    edge_stats = [column_stats(g) for g in edges]
     w["mu"][...] = jnp.zeros(w["mu"].shape, F32)
     w["sq"][...] = jnp.zeros(w["sq"].shape, F32)
     for s in range(count):
         q, g = s % 4, s // 4
-        block = jnp.concatenate([top[16 * s : 16 * s + 16], own(s), bottom[16 * s : 16 * s + 16]], 0)
+        block = sections[s]
         gap0 = jnp.zeros((16 * q, 256), BF16)
         gap1 = jnp.zeros((48 - 16 * q, 256), BF16)
-        pieces = [c["own"][...], gap0, sides[:16], gap1, gap0, sides[16:], gap1]
+        pieces = [c["own"], gap0, sides[:16], gap1, gap0, sides[16:], gap1]
         table = jnp.concatenate([p for p in pieces if p.shape[0]], 0)
-        w["g"][s] = dot(jnp.concatenate([block, groups[g]], 1), table)
+        w["g"][s] = dot(jnp.concatenate([block, edges[g]], 1), table)
         mean, square = column_stats(block)
         mean_e, square_e = edge_stats[g]
         if q:
@@ -180,13 +200,13 @@
     sq = w["sq"][...]
     mu0, mu1 = mu[:4].reshape(32, 256), mu[1:].reshape(32, 256)
     sq01 = (sq[:4] + sq[1:]).reshape(32, 256)
-    sums = dot_exact(mu0 + mu1, c["means"][...])
+    sums = dot_exact(mu0 + mu1, c["means"])
     total = []
     for parity in range(2):
         centre = sums[:, 256 * parity : 256 * parity + 256] * (1.0 / 128)
         d0, d1 = mu0 - centre, mu1 - centre
         total.append(sq01 + 32.0 * (d0 * d0 + d1 * d1))
-    variance = dot_exact(jnp.concatenate(total, 1), c["totals"][...]) * (1.0 / 4096)
+    variance = dot_exact(jnp.concatenate(total, 1), c["totals"]) * (1.0 / 4096)
     scale = lax.rsqrt(variance + 1e-05) * (1.0 / PATCH)
     if flag is not None:
         scale = scale * flag
@@ -206,7 +226,7 @@
                 w["g32"][...] = jnp.where(lane % 32 == slot, pltpu.roll(im, slot, 1), w["g32"][...])
                 im = jnp.where(zero_slot, 0.0, im)
                 columns.append(jnp.concatenate([re, im], 0).astype(BF16))
-            f = dot(c["forward"][...], jnp.concatenate(columns, 1))
+            f = dot(c["forward"], jnp.concatenate(columns, 1))
             for n, i in enumerate((2 * pair, 2 * pair + 1)):
                 part = f[:, 128 * n : 128 * n + 128] * w["scale"][i, pl.ds(s, 1), :]
                 w["f"][s + slot_f, i] = part.astype(BF16)
@@ -251,7 +271,7 @@
                 f_re, f_im, p_re, p_im = here[:64], here[64:], there[:64], there[64:]
                 q = jnp.concatenate([f_re * p_re + f_im * p_im, f_im * p_re - f_re * p_im], 0)
                 columns.append(q.astype(BF16))
-            h = dot(c["inverse"][...], jnp.concatenate(columns, 1))
+            h = dot(c["inverse"], jnp.concatenate(columns, 1))
             for n, i in enumerate((2 * half, 2 * half + 1)):
                 h_re = h[:64, 128 * n : 128 * n + 128]
                 special = pltpu.roll(w["h32"][k], 128 - (4 * s + i), 1)
@@ -259,8 +279,8 @@
                 h_cat = jnp.concatenate([h_re, h_im], 1).astype(BF16)
                 even.append(h_cat[:32])
                 odd.append(h_cat[32:])
-        even = dot(jnp.concatenate(even, 0), c["even"][...])
-        odd = dot(jnp.concatenate(odd, 0), c["odd"][...])
+        even = dot(jnp.concatenate(even, 0), c["even"])
+        odd = dot(jnp.concatenate(odd, 0), c["odd"])
         for i in range(4):
             for half in range(2):
                 e = even[32 * i : 32 * i + 32, 128 * half : 128 * half + 128]
@@ -290,24 +310,33 @@
 )
 
 
-def own_kernel(s_ref, e_ref, ya_ref, yb_ref, *refs):
-    c = dict(zip(NAMES, refs[: len(NAMES)]))
-    o_ref, f_ref, f32_ref = refs[len(NAMES) : len(NAMES) + 3]
-    w = dict(zip((*SCRATCH, "o", "sem"), refs[len(NAMES) + 3 :]))
+def own_kernel(s_ref, e_ref, ya_ref, yb_ref, t_ref, o_ref, f_ref, f32_ref, *scratch):
+    c = Tables(t_ref)
+    w = dict(zip((*SCRATCH, "o", "sem"), scratch))
     w["f"] = f_ref
-    f32 = spectra(6, 0, 0, lambda s: s_ref[s], lambda g: e_ref[g], ya_ref, yb_ref, None, c, w)
+    top, bottom = halo(ya_ref, yb_ref)
+
+    def tall(middle, n):
+        return jnp.concatenate([top[16 * n : 16 * n + 16], middle, bottom[16 * n : 16 * n + 16]], 0)
+
+    sections = [tall(s_ref[s], s) for s in range(6)]
+    edges = [tall(e_ref[g], 6 + g) for g in range(2)]
+    f32 = spectra(6, 0, 0, sections, edges, None, c, w)
     f32_ref[...] = f32
     maps(0, 9, f32, 0, c, w, o_ref)
 
 
-def rest_kernel(z_ref, ya_ref, yb_ref, f_ref, f32_ref, *refs):
-    c = dict(zip(NAMES, refs[: len(NAMES)]))
-    o_ref = refs[len(NAMES) + 1]
-    w = dict(zip((*SCRATCH, "f", "o", "sem"), refs[len(NAMES) + 2 :]))
+def rest_kernel(z_ref, h_ref, f_ref, f32_ref, t_ref, _, o_ref, *scratch):
+    c = Tables(t_ref)
+    w = dict(zip((*SCRATCH, "f", "o", "sem"), scratch))
     flag = jnp.where(lax.axis_index("gz") == 0, 1.0, 0.0)
     w["f"][0] = f_ref[4]
     w["f"][1] = f_ref[5]
-    extra = spectra(2, 6, 2, lambda s: z_ref[s], lambda g: z_ref[2], ya_ref, yb_ref, flag, c, w)
+    tall = [
+        jnp.concatenate([h_ref[16 * n : 16 * n + 16], z_ref[n], h_ref[48 + 16 * n : 64 + 16 * n]], 0)
+        for n in range(3)
+    ]
+    extra = spectra(2, 6, 2, tall[:2], tall[2:], flag, c, w)
     f32 = jnp.where(lanes((128, 128)) % 32 >= 24, extra.astype(F32), f32_ref[...].astype(F32))
     maps(9, 12, f32, 4, c, w, o_ref)
 
@@ -326,48 +355,64 @@
     return jax.ShapeDtypeStruct(shape, BF16)
 
 
+def params(mib):
+    return pltpu.CompilerParams(vmem_limit_bytes=mib * 2**20)
+
+
 def local(sections):
-    table = [jnp.asarray(constants()[name]) for name in NAMES]
-    params = pltpu.CompilerParams(vmem_limit_bytes=32 * 2**20)
     edge = shaped(128, 128)
-    xa, xb = pl.pallas_call(
-        edges_kernel, out_shape=(edge, edge), in_specs=[VMEM], out_specs=(VMEM, VMEM)
-    )(sections)
+    fixed = [pltpu.with_memory_space_constraint(value, pltpu.HBM) for value in (sections, constants()[0])]
+    xa, xb, sections, table = pl.pallas_call(
+        edges_kernel,
+        out_shape=(edge, edge, *(shaped(*value.shape) for value in fixed)),
+        in_specs=[HBM] * 2,
+        out_specs=(VMEM,) * 4,
+        scratch_shapes=[pltpu.SemaphoreType.DMA((2,))],
+        compiler_params=params(8),
+    )(*fixed)
     xa, xb = exchange(xa, xb, "gx", lax.axis_size("gx"))
     edges, ya, yb, z = pl.pallas_call(
         rows_kernel,
         out_shape=(shaped(2, 128, 128), edge, edge, shaped(3, 128, 128)),
         in_specs=[VMEM] * 3,
         out_specs=(VMEM,) * 4,
+        compiler_params=params(8),
     )(sections, xa, xb)
     ya, yb = exchange(ya, yb, "gy", lax.axis_size("gy"))
     z = other(z)
-    za, zb = other(ya), other(yb)
+    rows = pl.pallas_call(
+        halo_kernel,
+        out_shape=shaped(96, 128),
+        in_specs=[VMEM] * 2,
+        out_specs=VMEM,
+        compiler_params=params(8),
+    )(ya, yb)
+    rows = other(rows)
     scratch = [make(6) for make in SCRATCH.values()]
     out, f, f32 = pl.pallas_call(
         own_kernel,
         out_shape=(shaped(6, 2, 4, 128, 128), shaped(6, 4, 128, 128), edge),
-        in_specs=[VMEM] * (4 + len(table)),
-        out_specs=(ANY, VMEM, VMEM),
+        in_specs=[VMEM] * 5,
+        out_specs=(HBM, VMEM, VMEM),
         scratch_shapes=scratch + [pltpu.VMEM((9, 4, 128, 128), BF16), pltpu.SemaphoreType.DMA((9,))],
-        compiler_params=params,
+        compiler_params=params(16),
         cost_estimate=pl.CostEstimate(flops=10**9, bytes_accessed=4 * 10**6, transcendentals=0),
-    )(sections, edges, ya, yb, *table)
+    )(sections, edges, ya, yb, table)
     scratch = [make(2) for make in SCRATCH.values()]
     out = pl.pallas_call(
         rest_kernel,
         out_shape=shaped(6, 2, 4, 128, 128),
-        in_specs=[VMEM] * (5 + len(table)) + [ANY],
-        out_specs=ANY,
+        in_specs=[VMEM] * 5 + [HBM],
+        out_specs=HBM,
         scratch_shapes=scratch
         + [
             pltpu.VMEM((4, 4, 128, 128), BF16),
             pltpu.VMEM((3, 4, 128, 128), BF16),
             pltpu.SemaphoreType.DMA((3,)),
         ],
-        input_output_aliases={5 + len(table): 0},
-        compiler_params=params,
-    )(z, za, zb, f, f32, *table, out)
+        input_output_aliases={5: 0},
+        compiler_params=params(16),
+    )(z, rows, f, f32, table, out)
     out = out.reshape(6, 2, 4, 32, 4, 128).transpose(0, 1, 2, 4, 3, 5)
     return out.reshape(6, 2, 4, 4, 4096)
 

time: 42.5 us -> 29.1 us (0.68); the launches traced: 41.7 us -> 28.9 us
  local copies, waits for them, and re-layouts: 9.13 us -> 0 us
  Pallas kernels: 13.2 us -> 11.2 us
  starting transfers between devices: 16.8 us -> 15.3 us
    unnamed x26 -> x0, local copies, waits for them, and re-layouts: 9.13 us -> none
    ppermute x3 -> x2, starting transfers between devices: 5.74 us -> 4.07 us  [other(): return lax.ppermute(value, 'gz', [(0, 1), (1, 0)])]
    pallas_call x1, Pallas kernels: 1.72 us -> 0.09 us  [local(): pl.pallas_call(rows_kernel, out_shape=(shaped(2, 128, 128), edge, edge, s...]
    pallas_call x1 -> x2, Pallas kernels: 1.71 us -> 1.3 us  [the longest x1 1.29 us: local(): pl.pallas_call(edges_kernel, out_shape=(edge, edge, *(shaped(*value.shape...]
  transfers between devices with their start and end apart: 7 -> 6, of which waited for: 1 -> 1; matrix products, arithmetic and copies ran while one was open for 0% -> 0% of each run, Pallas kernels for 16% -> 23%
where the time goes in v2:
time: 29.1 us; the launch traced here: 28.9 us
  starting transfers between devices  15.3 us (53%)
  Pallas kernels  11.2 us (38%)
  waiting for transfers between devices  2.35 us (8%)
    ppermute x2, starting transfers between devices, exchange(): lax.ppermute(value_b, axis, pairs_b)  10.9 us
    pallas_call x1, Pallas kernels, local(): pl.pallas_call(own_kernel, out_shape=(shaped(6, 2, 4, 128, 128), shaped(6...  6.63 us
    ppermute x2, starting transfers between devices, other(): return lax.ppermute(value, 'gz', [(0, 1), (1, 0)])  4.07 us
    pallas_call x1, Pallas kernels, local(): pl.pallas_call(rest_kernel, out_shape=shaped(6, 2, 4, 128, 128), in_specs...  3.13 us
    ppermute x2, waiting for transfers between devices, exchange(): lax.ppermute(value_b, axis, pairs_b)  2.34 us
    pallas_call x1, Pallas kernels, local(): pl.pallas_call(edges_kernel, out_shape=(edge, edge, *(shaped(*value.shape...  1.29 us
  transfers between devices with their start and end apart: 6, of which 1 were waited for; matrix products, arithmetic and copies ran while one was open for 0% of the time, Pallas kernels for 23%

profile of v2, /device:TPU:98, one launch (start us, length us, event | category | flops | bytes accessed | tf_op | source)
XLA Modules:
  0.0 28.9 jit_solution(17331580242765596203)
XLA Ops:
  0.0 1.3 %shard_map.28 = (bf16[128,128]{1,0:T(8,128)(2,1)S(1)}, bf16[128,128]{1,0:T(8,128)(2,1)S(1)}, bf16[6,128,128]{2,1,0:T(8,128)(2,1)S(1)}, bf16[3392,128]{1,0:T(8,128)(2,1)S(1)}) custom-call(bf16[6,128,128]{2,1,0:T(8,128)(2,1)} %s_hbm.1, bf16[3392,128]{1,0:T(8,128)(2,1)} %constant.2.clone.t_hbm), custom_call_target="tpu_custom_call" | custom-call | tf_op jit(solution)/shard_map/pallas_call | solution.py:365
  1.3 0.1 collective-permute-start
  1.4 5.0 %collective-permute-start.1 = (bf16[128,128]{1,0:T(8,128)(2,1)S(1)}, bf16[128,128]{1,0:T(8,128)(2,1)S(1)}, u32[]{:S(2)}, u32[]{:S(2)}) collective-permute-start(bf16[128,128]{1,0:T(8,128)(2,1)S(1)} %get-tuple-element.18), channel_id=1, source_target_pairs={{16,32},{32,16},{48,64},{64,48},{80,96},{96,80},{112,128},{128,112... | collective-permute-start | bytes 98312 | tf_op jit(solution)/shard_map/ppermute | solution.py:347
  6.4 0.0 collective-permute-done.xa_ref
  6.4 2.3 %collective-permute-done.1.xb_ref = bf16[128,128]{1,0:T(8,128)(2,1)S(1)} collective-permute-done((bf16[128,128]{1,0:T(8,128)(2,1)S(1)}, bf16[128,128]{1,0:T(8,128)(2,1)S(1)}, u32[]{:S(2)}, u32[]{:S(2)}) %collective-permute-start.1) | collective-permute-done | bytes 32800 | tf_op jit(solution)/shard_map/ppermute | solution.py:347
  8.7 0.1 shard_map.29
  8.8 0.2 collective-permute-start.3
  9.0 5.9 %collective-permute-start.4 = (bf16[128,128]{1,0:T(8,128)(2,1)S(1)}, bf16[128,128]{1,0:T(8,128)(2,1)S(1)}, u32[]{:S(2)}, u32[]{:S(2)}) collective-permute-start(bf16[128,128]{1,0:T(8,128)(2,1)S(1)} %get-tuple-element.21), channel_id=1, source_target_pairs={{2,4},{4,2},{6,8},{8,6},{10,12},{12,10},{3,5},{5,3},{7,9},{9,7},{1... | collective-permute-start | bytes 98312 | tf_op jit(solution)/shard_map/ppermute | solution.py:347
  15.0 2.2 %collective-permute-start.2 = (bf16[3,128,128]{2,1,0:T(8,128)(2,1)S(1)}, bf16[3,128,128]{2,1,0:T(8,128)(2,1)S(1)}, u32[]{:S(2)}, u32[]{:S(2)}) collective-permute-start(bf16[3,128,128]{2,1,0:T(8,128)(2,1)S(1)} %get-tuple-element.19), channel_id=1, source_target_pairs={{0,1},{1,0},{2,3},{3,2},{4,5},{5,4},{6,7},{7,6},{8,9},{9,8},{10,11... | collective-permute-start | bytes 294920 | tf_op jit(solution)/shard_map/ppermute | solution.py:351
  17.2 0.0 collective-permute-done.3.ya_ref
  17.2 0.0 collective-permute-done.4.yb_ref
  17.2 1.9 %collective-permute-start.5 = (bf16[96,128]{1,0:T(8,128)(2,1)S(1)}, bf16[96,128]{1,0:T(8,128)(2,1)S(1)}, u32[]{:S(2)}, u32[]{:S(2)}) collective-permute-start(bf16[96,128]{1,0:T(8,128)(2,1)S(1)} %shard_map.30), channel_id=1, source_target_pairs={{0,1},{1,0},{2,3},{3,2},{4,5},{5,4},{6,7},{7,6},{8,9},{9,8},{10,11... | collective-permute-start | bytes 73736 | tf_op jit(solution)/shard_map/ppermute | solution.py:351
  19.1 6.6 %shard_map.31 = (bf16[6,2,4,128,128]{4,3,2,1,0:T(8,128)(2,1)}, bf16[6,4,128,128]{3,2,1,0:T(8,128)(2,1)S(1)}, bf16[128,128]{1,0:T(8,128)(2,1)S(1)}) custom-call(bf16[6,128,128]{2,1,0:T(8,128)(2,1)S(1)} %get-tuple-element.16.s_ref, bf16[2,128,128]{2,1,0:T(8,128)(2,1)S(1)} %get-tuple-element.22.e_ref, bf16[128,128]{1,0:T(8,128)(2,1)S(1)} %collective-permute-done.3.ya_ref, ...), custom_call_target="tpu_custom_call" | custom-call | flops 1000000000 | bytes 4000000 | tf_op jit(solution)/shard_map/pallas_call | solution.py:392
  25.7 0.0 collective-permute-done.5.h_ref
  25.7 0.0 collective-permute-done.2.z_ref
  25.7 3.1 %shard_map.32 = bf16[6,2,4,128,128]{4,3,2,1,0:T(8,128)(2,1)} custom-call(bf16[3,128,128]{2,1,0:T(8,128)(2,1)S(1)} %collective-permute-done.2.z_ref, bf16[96,128]{1,0:T(8,128)(2,1)S(1)} %collective-permute-done.5.h_ref, bf16[6,4,128,128]{3,2,1,0:T(8,128)(2,1)S(1)} %get-tuple-element.24.f_ref, ...), custom_call_target="tpu_custom_call", output_to_operand_aliasing={{}: (5, {})} | custom-call | tf_op jit(solution)/shard_map/pallas_call | solution.py:402
  (1 shorter events, 0.0 us)
Async XLA Ops:
  1.3 5.1 %collective-permute-start = (bf16[128,128]{1,0:T(8,128)(2,1)S(1)}, bf16[128,128]{1,0:T(8,128)(2,1)S(1)}, u32[]{:S(2)}, u32[]{:S(2)}) collective-permute-start(bf16[128,128]{1,0:T(8,128)(2,1)S(1)} %get-tuple-element.17), channel_id=1, source_target_pairs={{0,16},{16,0},{32,48},{48,32},{64,80},{80,64},{96,112},{112,96},{1... | collective-permute-start | bytes 98312 | tf_op jit(solution)/shard_map/ppermute | solution.py:347
  1.4 7.3 %collective-permute-start.1 = (bf16[128,128]{1,0:T(8,128)(2,1)S(1)}, bf16[128,128]{1,0:T(8,128)(2,1)S(1)}, u32[]{:S(2)}, u32[]{:S(2)}) collective-permute-start(bf16[128,128]{1,0:T(8,128)(2,1)S(1)} %get-tuple-element.18), channel_id=1, source_target_pairs={{16,32},{32,16},{48,64},{64,48},{80,96},{96,80},{112,128},{128,112... | collective-permute-start | bytes 98312 | tf_op jit(solution)/shard_map/ppermute | solution.py:347
  8.8 8.4 %collective-permute-start.3 = (bf16[128,128]{1,0:T(8,128)(2,1)S(1)}, bf16[128,128]{1,0:T(8,128)(2,1)S(1)}, u32[]{:S(2)}, u32[]{:S(2)}) collective-permute-start(bf16[128,128]{1,0:T(8,128)(2,1)S(1)} %get-tuple-element.20), channel_id=1, source_target_pairs={{0,2},{2,0},{4,6},{6,4},{8,10},{10,8},{12,14},{14,12},{1,3},{3,1},... | collective-permute-start | bytes 98312 | tf_op jit(solution)/shard_map/ppermute | solution.py:347
  9.0 8.2 %collective-permute-start.4 = (bf16[128,128]{1,0:T(8,128)(2,1)S(1)}, bf16[128,128]{1,0:T(8,128)(2,1)S(1)}, u32[]{:S(2)}, u32[]{:S(2)}) collective-permute-start(bf16[128,128]{1,0:T(8,128)(2,1)S(1)} %get-tuple-element.21), channel_id=1, source_target_pairs={{2,4},{4,2},{6,8},{8,6},{10,12},{12,10},{3,5},{5,3},{7,9},{9,7},{1... | collective-permute-start | bytes 98312 | tf_op jit(solution)/shard_map/ppermute | solution.py:347
  15.0 10.7 %collective-permute-start.2 = (bf16[3,128,128]{2,1,0:T(8,128)(2,1)S(1)}, bf16[3,128,128]{2,1,0:T(8,128)(2,1)S(1)}, u32[]{:S(2)}, u32[]{:S(2)}) collective-permute-start(bf16[3,128,128]{2,1,0:T(8,128)(2,1)S(1)} %get-tuple-element.19), channel_id=1, source_target_pairs={{0,1},{1,0},{2,3},{3,2},{4,5},{5,4},{6,7},{7,6},{8,9},{9,8},{10,11... | collective-permute-start | bytes 294920 | tf_op jit(solution)/shard_map/ppermute | solution.py:351
  17.2 8.5 %collective-permute-start.5 = (bf16[96,128]{1,0:T(8,128)(2,1)S(1)}, bf16[96,128]{1,0:T(8,128)(2,1)S(1)}, u32[]{:S(2)}, u32[]{:S(2)}) collective-permute-start(bf16[96,128]{1,0:T(8,128)(2,1)S(1)} %shard_map.30), channel_id=1, source_target_pairs={{0,1},{1,0},{2,3},{3,2},{4,5},{5,4},{6,7},{7,6},{8,9},{9,8},{10,11... | collective-permute-start | bytes 73736 | tf_op jit(solution)/shard_map/ppermute | solution.py:351

commit v3 on v2

--- a/solution.py
+++ b/solution.py
@@ -11,6 +11,7 @@
 from jax.sharding import PartitionSpec as P
 
 PATCH = 64
+AXES = ("gx", "gy", "gz")
 F32 = jnp.float32
 BF16 = jnp.bfloat16
 VMEM = pl.BlockSpec(memory_space=pltpu.VMEM)
@@ -131,12 +132,9 @@
 
 
 def rows_kernel(s_ref, xa_ref, xb_ref, e_ref, a_ref, b_ref, z_ref):
-    odd_x = lax.axis_index("gx") % 2 == 1
     odd_y = lax.axis_index("gy") % 2 == 1
-    xa = xa_ref[...].astype(F32)
-    xb = xb_ref[...].astype(F32)
-    left = jnp.where(odd_x, xa, xb)
-    right = jnp.where(odd_x, xb, xa)
+    left, right = low_high(xa_ref[...], xb_ref[...], "gx")
+    left, right = left.astype(F32), right.astype(F32)
     low = lanes((128, 128)) < 64
     e0 = jnp.where(low, left, pltpu.roll(right, 64, 1)).astype(BF16)
     e1 = jnp.where(low, pltpu.roll(left, 64, 1), right).astype(BF16)
@@ -152,16 +150,19 @@
 
 
 def halo_kernel(ya_ref, yb_ref, z_ref):
-    top, bottom = halo(ya_ref, yb_ref)
+    top, bottom = low_high(ya_ref[...], yb_ref[...], "gy")
     for n, at in enumerate((0, 16, 96)):
         z_ref[16 * n : 16 * n + 16] = top[at : at + 16]
         z_ref[48 + 16 * n : 64 + 16 * n] = bottom[at : at + 16]
 
 
-def halo(ya_ref, yb_ref):
-    odd = lax.axis_index("gy") % 2 == 1
-    ya, yb = ya_ref[...], yb_ref[...]
-    return jnp.where(odd, ya, yb), jnp.where(odd, yb, ya)
+def low_high(a, b, axis):
+    at = lax.axis_index(axis)
+    odd = at % 2 == 1
+    zero = jnp.zeros_like(a)
+    low = jnp.where(odd, a, jnp.where(at == 0, zero, b))
+    high = jnp.where(odd, jnp.where(at == lax.axis_size(axis) - 1, zero, b), a)
+    return low, high
 
 
 def spectra(count, first, slot_f, sections, edges, flag, c, w):
@@ -216,23 +217,23 @@
 
     w["g32"][...] = jnp.zeros(w["g32"].shape, F32)
 
-    def section(s, carry):
+    def section(s):
         for pair in range(2):
             columns = []
             for i in (2 * pair, 2 * pair + 1):
-                re = w["g"][s, 32 * i : 32 * i + 64, :128] - w["centre"][i, pl.ds(s, 1), :]
+                re = w["g"][s, 32 * i : 32 * i + 64, :128] - w["centre"][i, s : s + 1, :]
                 im = w["g"][s, 32 * i : 32 * i + 64, 128:]
                 slot = 4 * (s + first) + i
-                w["g32"][...] = jnp.where(lane % 32 == slot, pltpu.roll(im, slot, 1), w["g32"][...])
+                w["g32"][...] = jnp.where(lane % 32 == slot, (pltpu.roll(im, slot, 1) if slot else im), w["g32"][...])
                 im = jnp.where(zero_slot, 0.0, im)
                 columns.append(jnp.concatenate([re, im], 0).astype(BF16))
             f = dot(c["forward"], jnp.concatenate(columns, 1))
             for n, i in enumerate((2 * pair, 2 * pair + 1)):
-                part = f[:, 128 * n : 128 * n + 128] * w["scale"][i, pl.ds(s, 1), :]
+                part = f[:, 128 * n : 128 * n + 128] * w["scale"][i, s : s + 1, :]
                 w["f"][s + slot_f, i] = part.astype(BF16)
-        return carry
-
-    lax.fori_loop(0, count, section, 0)
+
+    for s in range(count):
+        section(s)
 
     scale32 = jnp.zeros((8, 128), F32)
     sublane = lax.broadcasted_iota(jnp.int32, (8, 128), 0)
@@ -260,7 +261,7 @@
             w["o"].at[p - lo], o_ref.at[p // 2, p % 2], w["sem"].at[p - lo]
         )
 
-    def pair(p, carry):
+    def pair(p):
         s, k = p // 2, p % 2
         even, odd = [], []
         for half in range(2):
@@ -274,7 +275,7 @@
             h = dot(c["inverse"], jnp.concatenate(columns, 1))
             for n, i in enumerate((2 * half, 2 * half + 1)):
                 h_re = h[:64, 128 * n : 128 * n + 128]
-                special = pltpu.roll(w["h32"][k], 128 - (4 * s + i), 1)
+                special = pltpu.roll(w["h32"][k], (128 - 4 * s - i) % 128, 1)
                 h_im = jnp.where(zero_slot, special, h[64:, 128 * n : 128 * n + 128])
                 h_cat = jnp.concatenate([h_re, h_im], 1).astype(BF16)
                 even.append(h_cat[:32])
@@ -291,9 +292,9 @@
                 )
             w["o"][p - lo, i] = w["mix"][i].astype(BF16)
         copy(p).start()
-        return carry
-
-    lax.fori_loop(lo, hi, pair, 0)
+
+    for p in range(lo, hi):
+        pair(p)
     for p in range(lo, hi):
         copy(p).wait()
 
@@ -314,7 +315,7 @@
     c = Tables(t_ref)
     w = dict(zip((*SCRATCH, "o", "sem"), scratch))
     w["f"] = f_ref
-    top, bottom = halo(ya_ref, yb_ref)
+    top, bottom = low_high(ya_ref[...], yb_ref[...], "gy")
 
     def tall(middle, n):
         return jnp.concatenate([top[16 * n : 16 * n + 16], middle, bottom[16 * n : 16 * n + 16]], 0)
@@ -341,10 +342,27 @@
     maps(9, 12, f32, 4, c, w, o_ref)
 
 
-def exchange(value_a, value_b, axis, count):
-    pairs_a = [(n, n ^ 1) for n in range(count)]
-    pairs_b = [(n, n + 1 if n % 2 else n - 1) for n in range(1, count - 1)]
-    return lax.ppermute(value_a, axis, pairs_a), lax.ppermute(value_b, axis, pairs_b)
+def exchange(value_a, value_b, axis):
+    sizes = [lax.axis_size(name) for name in AXES]
+    along, across = AXES.index(axis), 1 - AXES.index(axis)
+
+    def partner(place, first):
+        place = list(place)
+        up = place[along] % 2 == first
+        moved = place[along] + (1 if up else -1)
+        if 0 <= moved < sizes[along]:
+            place[along] = moved
+        else:
+            place[across] ^= 1
+        return place
+
+    def pairs(first):
+        return [
+            (int(np.ravel_multi_index(at, sizes)), int(np.ravel_multi_index(partner(at, first), sizes)))
+            for at in np.ndindex(*sizes)
+        ]
+
+    return lax.ppermute(value_a, AXES, pairs(0)), lax.ppermute(value_b, AXES, pairs(1))
 
 
 def other(value):
@@ -370,7 +388,7 @@
         scratch_shapes=[pltpu.SemaphoreType.DMA((2,))],
         compiler_params=params(8),
     )(*fixed)
-    xa, xb = exchange(xa, xb, "gx", lax.axis_size("gx"))
+    xa, xb = exchange(xa, xb, "gx")
     edges, ya, yb, z = pl.pallas_call(
         rows_kernel,
         out_shape=(shaped(2, 128, 128), edge, edge, shaped(3, 128, 128)),
@@ -378,7 +396,7 @@
         out_specs=(VMEM,) * 4,
         compiler_params=params(8),
     )(sections, xa, xb)
-    ya, yb = exchange(ya, yb, "gy", lax.axis_size("gy"))
+    ya, yb = exchange(ya, yb, "gy")
     z = other(z)
     rows = pl.pallas_call(
         halo_kernel,

time: 29.1 us -> 21.5 us (0.74)
  Pallas kernels: 11.2 us -> 7.33 us
  starting transfers between devices: 15.3 us -> 11.5 us
    ppermute x4, starting transfers between devices: 11.2 us -> 7.41 us  [the longest x2 7.13 us: exchange(): lax.ppermute(value_b, AXES, pairs(1))]
    pallas_call x1, Pallas kernels: 6.63 us -> 3.74 us  [local(): pl.pallas_call(own_kernel, out_shape=(shaped(6, 2, 4, 128, 128), shaped(6...]
    pallas_call x1, Pallas kernels: 3.13 us -> 2.19 us  [local(): pl.pallas_call(rest_kernel, out_shape=shaped(6, 2, 4, 128, 128), in_specs...]
  transfers between devices with their start and end apart: 6 -> 6, of which waited for: 1 -> 1; matrix products, arithmetic and copies ran while one was open for 0% -> 0% of each run, Pallas kernels for 23% -> 18%
where the time goes in v3:
time: 21.5 us; the launch traced here: 21.3 us
  starting transfers between devices  11.5 us (53%)
  Pallas kernels  7.33 us (34%)
  waiting for transfers between devices  2.46 us (11%)
    ppermute x2, starting transfers between devices, exchange(): lax.ppermute(value_b, AXES, pairs(1))  7.13 us
    ppermute x2, starting transfers between devices, other(): return lax.ppermute(value, 'gz', [(0, 1), (1, 0)])  4.09 us
    pallas_call x1, Pallas kernels, local(): pl.pallas_call(own_kernel, out_shape=(shaped(6, 2, 4, 128, 128), shaped(6...  3.74 us
    ppermute x2, waiting for transfers between devices, exchange(): lax.ppermute(value_b, AXES, pairs(1))  2.45 us
    pallas_call x1, Pallas kernels, local(): pl.pallas_call(rest_kernel, out_shape=shaped(6, 2, 4, 128, 128), in_specs...  2.19 us
    pallas_call x1, Pallas kernels, local(): pl.pallas_call(edges_kernel, out_shape=(edge, edge, *(shaped(*value.shape...  1.29 us
  transfers between devices with their start and end apart: 6, of which 1 were waited for; matrix products, arithmetic and copies ran while one was open for 0% of the time, Pallas kernels for 18%

profile of v3, /device:TPU:98, one launch (start us, length us, event | category | flops | bytes accessed | tf_op | source)
XLA Modules:
  0.0 21.3 jit_solution(9523449930793964236)
XLA Ops:
  0.0 1.3 %shard_map.28 = (bf16[128,128]{1,0:T(8,128)(2,1)S(1)}, bf16[128,128]{1,0:T(8,128)(2,1)S(1)}, bf16[6,128,128]{2,1,0:T(8,128)(2,1)S(1)}, bf16[3392,128]{1,0:T(8,128)(2,1)S(1)}) custom-call(bf16[6,128,128]{2,1,0:T(8,128)(2,1)} %s_hbm.1, bf16[3392,128]{1,0:T(8,128)(2,1)} %constant.2.clone.t_hbm), custom_call_target="tpu_custom_call" | custom-call | tf_op jit(solution)/shard_map/pallas_call | solution.py:383
  1.3 0.1 collective-permute-start
  1.4 3.1 %collective-permute-start.1 = (bf16[128,128]{1,0:T(8,128)(2,1)S(1)}, bf16[128,128]{1,0:T(8,128)(2,1)S(1)}, u32[]{:S(2)}, u32[]{:S(2)}) collective-permute-start(bf16[128,128]{1,0:T(8,128)(2,1)S(1)} %get-tuple-element.18), channel_id=1, source_target_pairs={{0,2},{1,3},{2,0},{3,1},{4,6},{5,7},{6,4},{7,5},{8,10},{9,11},{10,... | collective-permute-start | bytes 98312 | tf_op jit(solution)/shard_map/ppermute | solution.py:365
  4.5 0.0 collective-permute-done.xa_ref
  4.5 2.4 %collective-permute-done.1.xb_ref = bf16[128,128]{1,0:T(8,128)(2,1)S(1)} collective-permute-done((bf16[128,128]{1,0:T(8,128)(2,1)S(1)}, bf16[128,128]{1,0:T(8,128)(2,1)S(1)}, u32[]{:S(2)}, u32[]{:S(2)}) %collective-permute-start.1) | collective-permute-done | bytes 32800 | tf_op jit(solution)/shard_map/ppermute | solution.py:365
  6.9 0.1 shard_map.29
  7.0 0.2 collective-permute-start.3
  7.2 4.0 %collective-permute-start.4 = (bf16[128,128]{1,0:T(8,128)(2,1)S(1)}, bf16[128,128]{1,0:T(8,128)(2,1)S(1)}, u32[]{:S(2)}, u32[]{:S(2)}) collective-permute-start(bf16[128,128]{1,0:T(8,128)(2,1)S(1)} %get-tuple-element.21), channel_id=1, source_target_pairs={{0,16},{1,17},{2,4},{3,5},{4,2},{5,3},{6,8},{7,9},{8,6},{9,7},{10,... | collective-permute-start | bytes 98312 | tf_op jit(solution)/shard_map/ppermute | solution.py:365
  11.3 2.1 %collective-permute-start.2 = (bf16[3,128,128]{2,1,0:T(8,128)(2,1)S(1)}, bf16[3,128,128]{2,1,0:T(8,128)(2,1)S(1)}, u32[]{:S(2)}, u32[]{:S(2)}) collective-permute-start(bf16[3,128,128]{2,1,0:T(8,128)(2,1)S(1)} %get-tuple-element.19), channel_id=1, source_target_pairs={{0,1},{1,0},{2,3},{3,2},{4,5},{5,4},{6,7},{7,6},{8,9},{9,8},{10,11... | collective-permute-start | bytes 294920 | tf_op jit(solution)/shard_map/ppermute | solution.py:369
  13.4 0.0 collective-permute-done.3.ya_ref
  13.4 0.0 collective-permute-done.4.yb_ref
  13.4 2.0 %collective-permute-start.5 = (bf16[96,128]{1,0:T(8,128)(2,1)S(1)}, bf16[96,128]{1,0:T(8,128)(2,1)S(1)}, u32[]{:S(2)}, u32[]{:S(2)}) collective-permute-start(bf16[96,128]{1,0:T(8,128)(2,1)S(1)} %shard_map.30), channel_id=1, source_target_pairs={{0,1},{1,0},{2,3},{3,2},{4,5},{5,4},{6,7},{7,6},{8,9},{9,8},{10,11... | collective-permute-start | bytes 73736 | tf_op jit(solution)/shard_map/ppermute | solution.py:369
  15.4 3.7 %shard_map.31 = (bf16[6,2,4,128,128]{4,3,2,1,0:T(8,128)(2,1)}, bf16[6,4,128,128]{3,2,1,0:T(8,128)(2,1)S(1)}, bf16[128,128]{1,0:T(8,128)(2,1)S(1)}) custom-call(bf16[6,128,128]{2,1,0:T(8,128)(2,1)S(1)} %get-tuple-element.16.s_ref, bf16[2,128,128]{2,1,0:T(8,128)(2,1)S(1)} %get-tuple-element.22.e_ref, bf16[128,128]{1,0:T(8,128)(2,1)S(1)} %collective-permute-done.3.ya_ref, ...), custom_call_target="tpu_custom_call" | custom-call | flops 1000000000 | bytes 4000000 | tf_op jit(solution)/shard_map/pallas_call | solution.py:410
  19.1 0.0 collective-permute-done.5.h_ref
  19.1 0.0 collective-permute-done.2.z_ref
  19.2 2.2 %shard_map.32 = bf16[6,2,4,128,128]{4,3,2,1,0:T(8,128)(2,1)} custom-call(bf16[3,128,128]{2,1,0:T(8,128)(2,1)S(1)} %collective-permute-done.2.z_ref, bf16[96,128]{1,0:T(8,128)(2,1)S(1)} %collective-permute-done.5.h_ref, bf16[6,4,128,128]{3,2,1,0:T(8,128)(2,1)S(1)} %get-tuple-element.24.f_ref, ...), custom_call_target="tpu_custom_call", output_to_operand_aliasing={{}: (5, {})} | custom-call | tf_op jit(solution)/shard_map/pallas_call | solution.py:420
  (1 shorter events, 0.0 us)
Async XLA Ops:
  1.3 3.2 %collective-permute-start = (bf16[128,128]{1,0:T(8,128)(2,1)S(1)}, bf16[128,128]{1,0:T(8,128)(2,1)S(1)}, u32[]{:S(2)}, u32[]{:S(2)}) collective-permute-start(bf16[128,128]{1,0:T(8,128)(2,1)S(1)} %get-tuple-element.17), channel_id=1, source_target_pairs={{0,16},{1,17},{2,18},{3,19},{4,20},{5,21},{6,22},{7,23},{8,24},{9,... | collective-permute-start | bytes 98312 | tf_op jit(solution)/shard_map/ppermute | solution.py:365
  1.4 5.5 %collective-permute-start.1 = (bf16[128,128]{1,0:T(8,128)(2,1)S(1)}, bf16[128,128]{1,0:T(8,128)(2,1)S(1)}, u32[]{:S(2)}, u32[]{:S(2)}) collective-permute-start(bf16[128,128]{1,0:T(8,128)(2,1)S(1)} %get-tuple-element.18), channel_id=1, source_target_pairs={{0,2},{1,3},{2,0},{3,1},{4,6},{5,7},{6,4},{7,5},{8,10},{9,11},{10,... | collective-permute-start | bytes 98312 | tf_op jit(solution)/shard_map/ppermute | solution.py:365
  7.0 6.4 %collective-permute-start.3 = (bf16[128,128]{1,0:T(8,128)(2,1)S(1)}, bf16[128,128]{1,0:T(8,128)(2,1)S(1)}, u32[]{:S(2)}, u32[]{:S(2)}) collective-permute-start(bf16[128,128]{1,0:T(8,128)(2,1)S(1)} %get-tuple-element.20), channel_id=1, source_target_pairs={{0,2},{1,3},{2,0},{3,1},{4,6},{5,7},{6,4},{7,5},{8,10},{9,11},{10,... | collective-permute-start | bytes 98312 | tf_op jit(solution)/shard_map/ppermute | solution.py:365
  7.2 6.2 %collective-permute-start.4 = (bf16[128,128]{1,0:T(8,128)(2,1)S(1)}, bf16[128,128]{1,0:T(8,128)(2,1)S(1)}, u32[]{:S(2)}, u32[]{:S(2)}) collective-permute-start(bf16[128,128]{1,0:T(8,128)(2,1)S(1)} %get-tuple-element.21), channel_id=1, source_target_pairs={{0,16},{1,17},{2,4},{3,5},{4,2},{5,3},{6,8},{7,9},{8,6},{9,7},{10,... | collective-permute-start | bytes 98312 | tf_op jit(solution)/shard_map/ppermute | solution.py:365
  11.3 7.9 %collective-permute-start.2 = (bf16[3,128,128]{2,1,0:T(8,128)(2,1)S(1)}, bf16[3,128,128]{2,1,0:T(8,128)(2,1)S(1)}, u32[]{:S(2)}, u32[]{:S(2)}) collective-permute-start(bf16[3,128,128]{2,1,0:T(8,128)(2,1)S(1)} %get-tuple-element.19), channel_id=1, source_target_pairs={{0,1},{1,0},{2,3},{3,2},{4,5},{5,4},{6,7},{7,6},{8,9},{9,8},{10,11... | collective-permute-start | bytes 294920 | tf_op jit(solution)/shard_map/ppermute | solution.py:369
  13.4 5.7 %collective-permute-start.5 = (bf16[96,128]{1,0:T(8,128)(2,1)S(1)}, bf16[96,128]{1,0:T(8,128)(2,1)S(1)}, u32[]{:S(2)}, u32[]{:S(2)}) collective-permute-start(bf16[96,128]{1,0:T(8,128)(2,1)S(1)} %shard_map.30), channel_id=1, source_target_pairs={{0,1},{1,0},{2,3},{3,2},{4,5},{5,4},{6,7},{7,6},{8,9},{9,8},{10,11... | collective-permute-start | bytes 73736 | tf_op jit(solution)/shard_map/ppermute | solution.py:369

commit v4 on v3

--- a/solution.py
+++ b/solution.py
@@ -58,9 +58,9 @@
     inside = inside.astype(np.float64)
     same_even = inside[:, [0, 2]] @ inside[:, [0, 2]].T
     same_odd = inside[:, [1, 3]] @ inside[:, [1, 3]].T
-    spread = np.repeat(inside, 32, axis=1)
-    lane_odd = (np.arange(128) // 32 % 2).astype(np.float64)
-    means = np.concatenate([same_even, same_odd, spread], 1)
+    spread = np.repeat(inside, 64, axis=1)
+    lane_odd = (np.arange(256) // 64 % 2).astype(np.float64)
+    means = np.concatenate([same_even, same_odd], 1)
     totals = np.concatenate([spread * (1 - lane_odd), spread * lane_odd], 0)
     tables = dict(
         own=rows[16:144],
@@ -165,38 +165,28 @@
     return low, high
 
 
-def spectra(count, first, slot_f, sections, edges, flag, c, w):
-    lane = lanes((64, 128))
-    zero_slot = lane % 32 == 0
-    row_lane = lanes((8, 128))
-    sides = c["sides"]
-    def column_stats(block):
-        block = block.astype(F32).reshape(5, 32, 128)
-        mean = jnp.sum(block, 1, keepdims=True) * (1.0 / 32)
-        centred = block - mean
-        return mean[:, 0], jnp.sum(centred * centred, 1)
-
+def column_stats(block):
+    block = block.astype(F32).reshape(5, 32, 128)
+    mean = jnp.sum(block, 1, keepdims=True) * (1.0 / 32)
+    centred = block - mean
+    return mean[:, 0], jnp.sum(centred * centred, 1)
+
+
+def scales(first, sections, edges, c, w):
     edge_stats = [column_stats(g) for g in edges]
     w["mu"][...] = jnp.zeros(w["mu"].shape, F32)
     w["sq"][...] = jnp.zeros(w["sq"].shape, F32)
-    for s in range(count):
+    for s, block in enumerate(sections):
         q, g = s % 4, s // 4
-        block = sections[s]
-        gap0 = jnp.zeros((16 * q, 256), BF16)
-        gap1 = jnp.zeros((48 - 16 * q, 256), BF16)
-        pieces = [c["own"], gap0, sides[:16], gap1, gap0, sides[16:], gap1]
-        table = jnp.concatenate([p for p in pieces if p.shape[0]], 0)
-        w["g"][s] = dot(jnp.concatenate([block, edges[g]], 1), table)
         mean, square = column_stats(block)
         mean_e, square_e = edge_stats[g]
         if q:
             mean_e = pltpu.roll(mean_e, 128 - 16 * q, 1)
             square_e = pltpu.roll(square_e, 128 - 16 * q, 1)
-        w["mu"][:, s, :128] = mean
-        w["mu"][:, s, 128:] = mean_e
-        w["sq"][:, s, :128] = square
-        w["sq"][:, s, 128:] = square_e
-
+        w["mu"][:, first + s, :128] = mean
+        w["mu"][:, first + s, 128:] = mean_e
+        w["sq"][:, first + s, :128] = square
+        w["sq"][:, first + s, 128:] = square_e
     mu = w["mu"][...]
     sq = w["sq"][...]
     mu0, mu1 = mu[:4].reshape(32, 256), mu[1:].reshape(32, 256)
@@ -208,62 +198,67 @@
         d0, d1 = mu0 - centre, mu1 - centre
         total.append(sq01 + 32.0 * (d0 * d0 + d1 * d1))
     variance = dot_exact(jnp.concatenate(total, 1), c["totals"]) * (1.0 / 4096)
-    scale = lax.rsqrt(variance + 1e-05) * (1.0 / PATCH)
-    if flag is not None:
-        scale = scale * flag
-    w["scale"][...] = scale.reshape(4, 8, 128)
-    centre = jnp.where(lanes((32, 128)) % 32 == 0, sums[:, 512:] * 0.5, 0.0)
-    w["centre"][...] = centre.reshape(4, 8, 128)
-
-    w["g32"][...] = jnp.zeros(w["g32"].shape, F32)
-
-    def section(s):
+    return lax.rsqrt(variance + 1e-05) * (1.0 / PATCH)
+
+
+def store_scales(scale, w):
+    for half in range(2):
+        part = scale[:, 128 * half : 128 * half + 128]
+        w["scale"][0, half] = part.reshape(4, 8, 128)
+        w["scale"][1, half] = pltpu.roll(part, 64, 1).reshape(4, 8, 128)
+
+
+def spectra(first, slot_f, sections, edges, c, w):
+    lane = lanes((64, 128))
+    zero_slot = lane % 32 == 0
+    sides = c["sides"]
+    for s, block in enumerate(sections):
+        q = s % 4
+        gap0 = jnp.zeros((16 * q, 256), BF16)
+        gap1 = jnp.zeros((48 - 16 * q, 256), BF16)
+        pieces = [c["own"], gap0, sides[:16], gap1, gap0, sides[16:], gap1]
+        table = jnp.concatenate([p for p in pieces if p.shape[0]], 0)
+        w["g"][s] = dot(jnp.concatenate([block, edges[s // 4]], 1), table)
+    special = jnp.zeros((64, 128), F32)
+    for s in range(len(sections)):
         for pair in range(2):
             columns = []
             for i in (2 * pair, 2 * pair + 1):
-                re = w["g"][s, 32 * i : 32 * i + 64, :128] - w["centre"][i, s : s + 1, :]
+                re = w["g"][s, 32 * i : 32 * i + 64, :128]
                 im = w["g"][s, 32 * i : 32 * i + 64, 128:]
+                centre = jnp.sum(re, 0, keepdims=True) * (1.0 / 64)
+                re = jnp.where(zero_slot, re - centre, re)
                 slot = 4 * (s + first) + i
-                w["g32"][...] = jnp.where(lane % 32 == slot, (pltpu.roll(im, slot, 1) if slot else im), w["g32"][...])
+                special = jnp.where(lane % 32 == slot, pltpu.roll(im, slot, 1) if slot else im, special)
                 im = jnp.where(zero_slot, 0.0, im)
                 columns.append(jnp.concatenate([re, im], 0).astype(BF16))
-            f = dot(c["forward"], jnp.concatenate(columns, 1))
+            f = dot(c["forward"], jnp.concatenate(columns, 1)).astype(BF16)
             for n, i in enumerate((2 * pair, 2 * pair + 1)):
-                part = f[:, 128 * n : 128 * n + 128] * w["scale"][i, s : s + 1, :]
-                w["f"][s + slot_f, i] = part.astype(BF16)
-
-    for s in range(count):
-        section(s)
-
-    scale32 = jnp.zeros((8, 128), F32)
-    sublane = lax.broadcasted_iota(jnp.int32, (8, 128), 0)
-    for i in range(4):
-        scale32 = scale32 + jnp.where(row_lane % 32 == 4 * (sublane + first) + i, w["scale"][i], 0.0)
-    scale32 = jnp.sum(scale32, 0, keepdims=True)
-    f = dot(c["forward"][:, :64], w["g32"][...].astype(BF16))
-    return (f * scale32).astype(BF16)
+                w["f"][s + slot_f, i] = f[:, 128 * n : 128 * n + 128]
+    return dot(c["forward"][:, :64], special.astype(BF16)).astype(BF16)
 
 
 def maps(lo, hi, f32, offset, c, w, o_ref):
+    lane = lanes((64, 128))
+    zero_slot = lane % 32 == 0
+    low = lanes((32, 128)) < 64
     f32 = f32.astype(F32)
     re, im = f32[:64], f32[64:]
+    h32 = []
     for k in range(2):
         re_p = pltpu.roll(re, 128 - 4 * (k + 1), 1)
         im_p = pltpu.roll(im, 128 - 4 * (k + 1), 1)
         q = jnp.concatenate([re * re_p + im * im_p, im * re_p - re * im_p], 0).astype(BF16)
-        w["h32"][k] = dot(c["inverse"][:64], q)
-    lane = lanes((64, 128))
-    zero_slot = lane % 32 == 0
-    low = lanes((32, 128)) < 64
+        h32.append(dot(c["inverse"][:64], q))
 
     def copy(p):
         return pltpu.make_async_copy(
             w["o"].at[p - lo], o_ref.at[p // 2, p % 2], w["sem"].at[p - lo]
         )
 
-    def pair(p):
+    def correlate(p):
         s, k = p // 2, p % 2
-        even, odd = [], []
+        spectra = []
         for half in range(2):
             columns = []
             for i in (2 * half, 2 * half + 1):
@@ -272,29 +267,44 @@
                 f_re, f_im, p_re, p_im = here[:64], here[64:], there[:64], there[64:]
                 q = jnp.concatenate([f_re * p_re + f_im * p_im, f_im * p_re - f_re * p_im], 0)
                 columns.append(q.astype(BF16))
-            h = dot(c["inverse"], jnp.concatenate(columns, 1))
-            for n, i in enumerate((2 * half, 2 * half + 1)):
-                h_re = h[:64, 128 * n : 128 * n + 128]
-                special = pltpu.roll(w["h32"][k], (128 - 4 * s - i) % 128, 1)
-                h_im = jnp.where(zero_slot, special, h[64:, 128 * n : 128 * n + 128])
-                h_cat = jnp.concatenate([h_re, h_im], 1).astype(BF16)
-                even.append(h_cat[:32])
-                odd.append(h_cat[32:])
+            spectra.append(dot(c["inverse"], jnp.concatenate(columns, 1)))
+        return spectra
+
+    def last(p, spectra):
+        s, k = p // 2, p % 2
+        even, odd = [], []
+        for i in range(4):
+            h = spectra[i // 2][:, 128 * (i % 2) : 128 * (i % 2) + 128]
+            special = pltpu.roll(h32[k], (128 - 4 * s - i) % 128, 1)
+            h_im = jnp.where(zero_slot, special, h[64:])
+            h_cat = jnp.concatenate([h[:64], h_im], 1).astype(BF16)
+            even.append(h_cat[:32])
+            odd.append(h_cat[32:])
         even = dot(jnp.concatenate(even, 0), c["even"])
         odd = dot(jnp.concatenate(odd, 0), c["odd"])
+        return even, odd
+
+    def store(p, even, odd):
+        s, k = p // 2, p % 2
+        mix = w["mix"].at[p % 2]
         for i in range(4):
             for half in range(2):
-                e = even[32 * i : 32 * i + 32, 128 * half : 128 * half + 128]
-                o = odd[32 * i : 32 * i + 32, 128 * half : 128 * half + 128]
-                w["mix"][i, pl.ds(2 * half, 32, stride=4), :] = jnp.where(low, e, o)
-                w["mix"][i, pl.ds(2 * half + 1, 32, stride=4), :] = pltpu.roll(
-                    jnp.where(low, o, e), 64, 1
-                )
-            w["o"][p - lo, i] = w["mix"][i].astype(BF16)
+                e_scale, o_scale = [
+                    w["scale"][n, half, i, s : s + 1] * w["scale"][n, half, i, s + k + 1 : s + k + 2]
+                    for n in range(2)
+                ]
+                e = even[32 * i : 32 * i + 32, 128 * half : 128 * half + 128] * e_scale
+                o = odd[32 * i : 32 * i + 32, 128 * half : 128 * half + 128] * o_scale
+                mix[i, pl.ds(2 * half, 32, stride=4), :] = jnp.where(low, e, o)
+                mix[i, pl.ds(2 * half + 1, 32, stride=4), :] = pltpu.roll(jnp.where(low, o, e), 64, 1)
+            w["o"][p - lo, i] = mix[i].astype(BF16)
         copy(p).start()
 
+    ready = correlate(lo)
     for p in range(lo, hi):
-        pair(p)
+        following = correlate(p + 1) if p + 1 < hi else None
+        store(p, *last(p, ready))
+        ready = following
     for p in range(lo, hi):
         copy(p).wait()
 
@@ -303,15 +313,12 @@
     g=lambda n: pltpu.VMEM((n, 160, 256), F32),
     mu=lambda n: pltpu.VMEM((5, 8, 256), F32),
     sq=lambda n: pltpu.VMEM((5, 8, 256), F32),
-    scale=lambda n: pltpu.VMEM((4, 8, 128), F32),
-    centre=lambda n: pltpu.VMEM((4, 8, 128), F32),
-    g32=lambda n: pltpu.VMEM((64, 128), F32),
-    h32=lambda n: pltpu.VMEM((2, 64, 128), F32),
-    mix=lambda n: pltpu.VMEM((4, 128, 128), F32),
+    scale=lambda n: pltpu.VMEM((2, 2, 4, 8, 128), F32),
+    mix=lambda n: pltpu.VMEM((2, 4, 128, 128), F32),
 )
 
 
-def own_kernel(s_ref, e_ref, ya_ref, yb_ref, t_ref, o_ref, f_ref, f32_ref, *scratch):
+def own_kernel(s_ref, e_ref, ya_ref, yb_ref, t_ref, o_ref, f_ref, f32_ref, scale_ref, *scratch):
     c = Tables(t_ref)
     w = dict(zip((*SCRATCH, "o", "sem"), scratch))
     w["f"] = f_ref
@@ -322,12 +329,15 @@
 
     sections = [tall(s_ref[s], s) for s in range(6)]
     edges = [tall(e_ref[g], 6 + g) for g in range(2)]
-    f32 = spectra(6, 0, 0, sections, edges, None, c, w)
+    f32 = spectra(0, 0, sections, edges, c, w)
+    scale = scales(0, sections, edges, c, w)
+    store_scales(scale, w)
     f32_ref[...] = f32
+    scale_ref[...] = scale
     maps(0, 9, f32, 0, c, w, o_ref)
 
 
-def rest_kernel(z_ref, h_ref, f_ref, f32_ref, t_ref, _, o_ref, *scratch):
+def rest_kernel(z_ref, h_ref, f_ref, f32_ref, scale_ref, t_ref, _, o_ref, *scratch):
     c = Tables(t_ref)
     w = dict(zip((*SCRATCH, "f", "o", "sem"), scratch))
     flag = jnp.where(lax.axis_index("gz") == 0, 1.0, 0.0)
@@ -337,7 +347,10 @@
         jnp.concatenate([h_ref[16 * n : 16 * n + 16], z_ref[n], h_ref[48 + 16 * n : 64 + 16 * n]], 0)
         for n in range(3)
     ]
-    extra = spectra(2, 6, 2, tall[:2], tall[2:], flag, c, w)
+    extra = spectra(6, 2, tall[:2], tall[2:], c, w)
+    scale = scales(6, tall[:2], tall[2:], c, w) * flag
+    scale = jnp.where(lax.broadcasted_iota(jnp.int32, (32, 256), 0) % 8 >= 6, scale, scale_ref[...])
+    store_scales(scale, w)
     f32 = jnp.where(lanes((128, 128)) % 32 >= 24, extra.astype(F32), f32_ref[...].astype(F32))
     maps(9, 12, f32, 4, c, w, o_ref)
 
@@ -375,6 +388,39 @@
 
 def params(mib):
     return pltpu.CompilerParams(vmem_limit_bytes=mib * 2**20)
+
+
+def compute(sections, edges, ya, yb, z, rows, table):
+    scratch = [make(6) for make in SCRATCH.values()]
+    out, f, f32, scale = pl.pallas_call(
+        own_kernel,
+        out_shape=(
+            shaped(6, 2, 4, 128, 128),
+            shaped(6, 4, 128, 128),
+            shaped(128, 128),
+            jax.ShapeDtypeStruct((32, 256), F32),
+        ),
+        in_specs=[VMEM] * 5,
+        out_specs=(HBM, VMEM, VMEM, VMEM),
+        scratch_shapes=scratch + [pltpu.VMEM((9, 4, 128, 128), BF16), pltpu.SemaphoreType.DMA((9,))],
+        compiler_params=params(16),
+        cost_estimate=pl.CostEstimate(flops=10**9, bytes_accessed=4 * 10**6, transcendentals=0),
+    )(sections, edges, ya, yb, table)
+    scratch = [make(2) for make in SCRATCH.values()]
+    return pl.pallas_call(
+        rest_kernel,
+        out_shape=shaped(6, 2, 4, 128, 128),
+        in_specs=[VMEM] * 6 + [HBM],
+        out_specs=HBM,
+        scratch_shapes=scratch
+        + [
+            pltpu.VMEM((4, 4, 128, 128), BF16),
+            pltpu.VMEM((3, 4, 128, 128), BF16),
+            pltpu.SemaphoreType.DMA((3,)),
+        ],
+        input_output_aliases={6: 0},
+        compiler_params=params(16),
+    )(z, rows, f, f32, scale, table, out)
 
 
 def local(sections):
@@ -406,31 +452,7 @@
         compiler_params=params(8),
     )(ya, yb)
     rows = other(rows)
-    scratch = [make(6) for make in SCRATCH.values()]
-    out, f, f32 = pl.pallas_call(
-        own_kernel,
-        out_shape=(shaped(6, 2, 4, 128, 128), shaped(6, 4, 128, 128), edge),
-        in_specs=[VMEM] * 5,
-        out_specs=(HBM, VMEM, VMEM),
-        scratch_shapes=scratch + [pltpu.VMEM((9, 4, 128, 128), BF16), pltpu.SemaphoreType.DMA((9,))],
-        compiler_params=params(16),
-        cost_estimate=pl.CostEstimate(flops=10**9, bytes_accessed=4 * 10**6, transcendentals=0),
-    )(sections, edges, ya, yb, table)
-    scratch = [make(2) for make in SCRATCH.values()]
-    out = pl.pallas_call(
-        rest_kernel,
-        out_shape=shaped(6, 2, 4, 128, 128),
-        in_specs=[VMEM] * 5 + [HBM],
-        out_specs=HBM,
-        scratch_shapes=scratch
-        + [
-            pltpu.VMEM((4, 4, 128, 128), BF16),
-            pltpu.VMEM((3, 4, 128, 128), BF16),
-            pltpu.SemaphoreType.DMA((3,)),
-        ],
-        input_output_aliases={5: 0},
-        compiler_params=params(16),
-    )(z, rows, f, f32, table, out)
+    out = compute(sections, edges, ya, yb, z, rows, table)
     out = out.reshape(6, 2, 4, 32, 4, 128).transpose(0, 1, 2, 4, 3, 5)
     return out.reshape(6, 2, 4, 4, 4096)
 

time: 21.5 us -> 20.9 us (0.972)
  Pallas kernels: 7.33 us -> 6.19 us
  waiting for transfers between devices: 2.46 us -> 3.02 us
    pallas_call x2, Pallas kernels: 5.92 us -> 4.77 us  [the longest x1 2.88 us: compute(): pl.pallas_call(own_kernel, out_shape=(shaped(6, 2, 4, 128, 128), shaped(6...]
    ppermute x2, waiting for transfers between devices: 0.01 us -> 0.57 us  [other(): return lax.ppermute(value, 'gz', [(0, 1), (1, 0)])]
  transfers between devices with their start and end apart: 6 -> 6, of which waited for: 1 -> 2; matrix products, arithmetic and copies ran while one was open for 0% -> 0% of each run, Pallas kernels for 18% -> 14%
where the time goes in v4:
time: 20.9 us; the launch traced here: 20.8 us
  starting transfers between devices  11.5 us (55%)
  Pallas kernels  6.19 us (30%)
  waiting for transfers between devices  3.02 us (14%)
    ppermute x2, starting transfers between devices, exchange(): lax.ppermute(value_b, AXES, pairs(1))  7.13 us
    ppermute x2, starting transfers between devices, other(): return lax.ppermute(value, 'gz', [(0, 1), (1, 0)])  4.09 us
    pallas_call x1, Pallas kernels, compute(): pl.pallas_call(own_kernel, out_shape=(shaped(6, 2, 4, 128, 128), shaped(6...  2.88 us
    ppermute x2, waiting for transfers between devices, exchange(): lax.ppermute(value_b, AXES, pairs(1))  2.45 us
    pallas_call x1, Pallas kernels, compute(): pl.pallas_call(rest_kernel, out_shape=shaped(6, 2, 4, 128, 128), in_specs...  1.89 us
    pallas_call x1, Pallas kernels, local(): pl.pallas_call(edges_kernel, out_shape=(edge, edge, *(shaped(*value.shape...  1.31 us
    ppermute x2, waiting for transfers between devices, other(): return lax.ppermute(value, 'gz', [(0, 1), (1, 0)])  0.57 us
  transfers between devices with their start and end apart: 6, of which 2 were waited for; matrix products, arithmetic and copies ran while one was open for 0% of the time, Pallas kernels for 14%

profile of v4, /device:TPU:98, one launch (start us, length us, event | category | flops | bytes accessed | tf_op | source)
XLA Modules:
  0.0 20.8 jit_solution(16624280206145748553)
XLA Ops:
  0.0 1.3 %shard_map.28 = (bf16[128,128]{1,0:T(8,128)(2,1)S(1)}, bf16[128,128]{1,0:T(8,128)(2,1)S(1)}, bf16[6,128,128]{2,1,0:T(8,128)(2,1)S(1)}, bf16[3648,128]{1,0:T(8,128)(2,1)S(1)}) custom-call(bf16[6,128,128]{2,1,0:T(8,128)(2,1)} %s_hbm.1, bf16[3648,128]{1,0:T(8,128)(2,1)} %constant.2.clone.t_hbm), custom_call_target="tpu_custom_call" | custom-call | tf_op jit(solution)/shard_map/pallas_call | solution.py:429
  1.3 0.1 collective-permute-start
  1.4 3.1 %collective-permute-start.1 = (bf16[128,128]{1,0:T(8,128)(2,1)S(1)}, bf16[128,128]{1,0:T(8,128)(2,1)S(1)}, u32[]{:S(2)}, u32[]{:S(2)}) collective-permute-start(bf16[128,128]{1,0:T(8,128)(2,1)S(1)} %get-tuple-element.19), channel_id=1, source_target_pairs={{0,2},{1,3},{2,0},{3,1},{4,6},{5,7},{6,4},{7,5},{8,10},{9,11},{10,... | collective-permute-start | bytes 98312 | tf_op jit(solution)/shard_map/ppermute | solution.py:378
  4.5 0.0 collective-permute-done.xa_ref
  4.5 2.4 %collective-permute-done.1.xb_ref = bf16[128,128]{1,0:T(8,128)(2,1)S(1)} collective-permute-done((bf16[128,128]{1,0:T(8,128)(2,1)S(1)}, bf16[128,128]{1,0:T(8,128)(2,1)S(1)}, u32[]{:S(2)}, u32[]{:S(2)}) %collective-permute-start.1) | collective-permute-done | bytes 32800 | tf_op jit(solution)/shard_map/ppermute | solution.py:378
  7.0 0.1 shard_map.29
  7.1 0.2 collective-permute-start.3
  7.3 4.0 %collective-permute-start.4 = (bf16[128,128]{1,0:T(8,128)(2,1)S(1)}, bf16[128,128]{1,0:T(8,128)(2,1)S(1)}, u32[]{:S(2)}, u32[]{:S(2)}) collective-permute-start(bf16[128,128]{1,0:T(8,128)(2,1)S(1)} %get-tuple-element.22), channel_id=1, source_target_pairs={{0,16},{1,17},{2,4},{3,5},{4,2},{5,3},{6,8},{7,9},{8,6},{9,7},{10,... | collective-permute-start | bytes 98312 | tf_op jit(solution)/shard_map/ppermute | solution.py:378
  11.3 2.1 %collective-permute-start.2 = (bf16[3,128,128]{2,1,0:T(8,128)(2,1)S(1)}, bf16[3,128,128]{2,1,0:T(8,128)(2,1)S(1)}, u32[]{:S(2)}, u32[]{:S(2)}) collective-permute-start(bf16[3,128,128]{2,1,0:T(8,128)(2,1)S(1)} %get-tuple-element.20), channel_id=1, source_target_pairs={{0,1},{1,0},{2,3},{3,2},{4,5},{5,4},{6,7},{7,6},{8,9},{9,8},{10,11... | collective-permute-start | bytes 294920 | tf_op jit(solution)/shard_map/ppermute | solution.py:382
  13.4 0.0 collective-permute-done.3.ya_ref
  13.4 0.0 collective-permute-done.4.yb_ref
  13.5 2.0 %collective-permute-start.5 = (bf16[96,128]{1,0:T(8,128)(2,1)S(1)}, bf16[96,128]{1,0:T(8,128)(2,1)S(1)}, u32[]{:S(2)}, u32[]{:S(2)}) collective-permute-start(bf16[96,128]{1,0:T(8,128)(2,1)S(1)} %shard_map.30), channel_id=1, source_target_pairs={{0,1},{1,0},{2,3},{3,2},{4,5},{5,4},{6,7},{7,6},{8,9},{9,8},{10,11... | collective-permute-start | bytes 73736 | tf_op jit(solution)/shard_map/ppermute | solution.py:382
  15.4 2.9 %shard_map.31 = (bf16[6,2,4,128,128]{4,3,2,1,0:T(8,128)(2,1)}, bf16[6,4,128,128]{3,2,1,0:T(8,128)(2,1)S(1)}, bf16[128,128]{1,0:T(8,128)(2,1)S(1)}, f32[32,256]{1,0:T(8,128)S(1)}) custom-call(bf16[6,128,128]{2,1,0:T(8,128)(2,1)S(1)} %get-tuple-element.17.s_ref, bf16[2,128,128]{2,1,0:T(8,128)(2,1)S(1)} %get-tuple-element.23.e_ref, ...), custom_call_target="tpu_custom_call" | custom-call | flops 1000000000 | bytes 4000000 | tf_op jit(solution)/shard_map/pallas_call | solution.py:395
  18.3 0.6 %collective-permute-done.5.h_ref = bf16[96,128]{1,0:T(8,128)(2,1)S(1)} collective-permute-done((bf16[96,128]{1,0:T(8,128)(2,1)S(1)}, bf16[96,128]{1,0:T(8,128)(2,1)S(1)}, u32[]{:S(2)}, u32[]{:S(2)}) %collective-permute-start.5) | collective-permute-done | bytes 24608 | tf_op jit(solution)/shard_map/ppermute | solution.py:382
  18.9 0.0 collective-permute-done.2.z_ref
  18.9 1.9 %shard_map.32 = bf16[6,2,4,128,128]{4,3,2,1,0:T(8,128)(2,1)} custom-call(bf16[3,128,128]{2,1,0:T(8,128)(2,1)S(1)} %collective-permute-done.2.z_ref, bf16[96,128]{1,0:T(8,128)(2,1)S(1)} %collective-permute-done.5.h_ref, bf16[6,4,128,128]{3,2,1,0:T(8,128)(2,1)S(1)} %get-tuple-element.25.f_ref, ...), custom_call_target="tpu_custom_call", output_to_operand_aliasing={{}: (6, {})} | custom-call | tf_op jit(solution)/shard_map/pallas_call | solution.py:410
  (1 shorter events, 0.0 us)
Async XLA Ops:
  1.3 3.2 %collective-permute-start = (bf16[128,128]{1,0:T(8,128)(2,1)S(1)}, bf16[128,128]{1,0:T(8,128)(2,1)S(1)}, u32[]{:S(2)}, u32[]{:S(2)}) collective-permute-start(bf16[128,128]{1,0:T(8,128)(2,1)S(1)} %get-tuple-element.18), channel_id=1, source_target_pairs={{0,16},{1,17},{2,18},{3,19},{4,20},{5,21},{6,22},{7,23},{8,24},{9,... | collective-permute-start | bytes 98312 | tf_op jit(solution)/shard_map/ppermute | solution.py:378
  1.4 5.5 %collective-permute-start.1 = (bf16[128,128]{1,0:T(8,128)(2,1)S(1)}, bf16[128,128]{1,0:T(8,128)(2,1)S(1)}, u32[]{:S(2)}, u32[]{:S(2)}) collective-permute-start(bf16[128,128]{1,0:T(8,128)(2,1)S(1)} %get-tuple-element.19), channel_id=1, source_target_pairs={{0,2},{1,3},{2,0},{3,1},{4,6},{5,7},{6,4},{7,5},{8,10},{9,11},{10,... | collective-permute-start | bytes 98312 | tf_op jit(solution)/shard_map/ppermute | solution.py:378
  7.1 6.4 %collective-permute-start.3 = (bf16[128,128]{1,0:T(8,128)(2,1)S(1)}, bf16[128,128]{1,0:T(8,128)(2,1)S(1)}, u32[]{:S(2)}, u32[]{:S(2)}) collective-permute-start(bf16[128,128]{1,0:T(8,128)(2,1)S(1)} %get-tuple-element.21), channel_id=1, source_target_pairs={{0,2},{1,3},{2,0},{3,1},{4,6},{5,7},{6,4},{7,5},{8,10},{9,11},{10,... | collective-permute-start | bytes 98312 | tf_op jit(solution)/shard_map/ppermute | solution.py:378
  7.3 6.2 %collective-permute-start.4 = (bf16[128,128]{1,0:T(8,128)(2,1)S(1)}, bf16[128,128]{1,0:T(8,128)(2,1)S(1)}, u32[]{:S(2)}, u32[]{:S(2)}) collective-permute-start(bf16[128,128]{1,0:T(8,128)(2,1)S(1)} %get-tuple-element.22), channel_id=1, source_target_pairs={{0,16},{1,17},{2,4},{3,5},{4,2},{5,3},{6,8},{7,9},{8,6},{9,7},{10,... | collective-permute-start | bytes 98312 | tf_op jit(solution)/shard_map/ppermute | solution.py:378
  11.3 7.6 %collective-permute-start.2 = (bf16[3,128,128]{2,1,0:T(8,128)(2,1)S(1)}, bf16[3,128,128]{2,1,0:T(8,128)(2,1)S(1)}, u32[]{:S(2)}, u32[]{:S(2)}) collective-permute-start(bf16[3,128,128]{2,1,0:T(8,128)(2,1)S(1)} %get-tuple-element.20), channel_id=1, source_target_pairs={{0,1},{1,0},{2,3},{3,2},{4,5},{5,4},{6,7},{7,6},{8,9},{9,8},{10,11... | collective-permute-start | bytes 294920 | tf_op jit(solution)/shard_map/ppermute | solution.py:382
  13.5 5.4 %collective-permute-start.5 = (bf16[96,128]{1,0:T(8,128)(2,1)S(1)}, bf16[96,128]{1,0:T(8,128)(2,1)S(1)}, u32[]{:S(2)}, u32[]{:S(2)}) collective-permute-start(bf16[96,128]{1,0:T(8,128)(2,1)S(1)} %shard_map.30), channel_id=1, source_target_pairs={{0,1},{1,0},{2,3},{3,2},{4,5},{5,4},{6,7},{7,6},{8,9},{9,8},{10,11... | collective-permute-start | bytes 73736 | tf_op jit(solution)/shard_map/ppermute | solution.py:382

commit v5 on v4

--- a/solution.py
+++ b/solution.py
@@ -109,51 +109,63 @@
     return lax.broadcasted_iota(jnp.int32, shape, len(shape) - 1)
 
 
-def edges_kernel(s_hbm, t_hbm, a_ref, b_ref, s_ref, t_ref, sem):
+def first_kernel(s_hbm, a_ref, b_ref, sem):
+    odd = lax.axis_index("gy") % 2 == 1
+    copies = []
+    for n, (out, at) in enumerate(((a_ref, jnp.where(odd, 0, 112)), (b_ref, jnp.where(odd, 112, 0)))):
+        rows = s_hbm.at[:, pl.ds(pl.multiple_of(at, 16), 16), :]
+        copies.append(pltpu.make_async_copy(rows, out, sem.at[n]))
+    for copy in copies:
+        copy.start()
+    for copy in copies:
+        copy.wait()
+
+
+def pack_sides(blocks):
+    lane = lanes(blocks[0].shape)
+    left = jnp.zeros(lane.shape, F32)
+    right = jnp.zeros(lane.shape, F32)
+    for s, block in enumerate(blocks):
+        block = block.astype(F32)
+        here = (lane // 16) == s
+        left = jnp.where(here, pltpu.roll(block, 16 * s, 1) if s else block, left)
+        right = jnp.where(here, pltpu.roll(block, 16 * s + 16, 1), right)
+    return left.astype(BF16), right.astype(BF16)
+
+
+def stage_kernel(s_hbm, t_hbm, s_ref, t_ref, l_ref, r_ref, sem):
     sections = pltpu.make_async_copy(s_hbm, s_ref, sem.at[0])
     tables = pltpu.make_async_copy(t_hbm, t_ref, sem.at[1])
     sections.start()
     tables.start()
     sections.wait()
+    l_ref[...], r_ref[...] = pack_sides([s_ref[s] for s in range(6)])
+    tables.wait()
+
+
+def sides_kernel(ya_ref, yb_ref, s_ref, l_ref, r_ref, _, a_ref, b_ref, z_ref):
     odd = lax.axis_index("gx") % 2 == 1
-    lane = lanes((128, 128))
-    left = jnp.zeros((128, 128), F32)
-    right = jnp.zeros((128, 128), F32)
-    for s in range(6):
-        block = s_ref[s].astype(F32)
-        here = (lane // 16) == s
-        first = pltpu.roll(block, 16 * s, 1) if s else block
-        last = pltpu.roll(block, 16 * s + 16, 1)
-        left = jnp.where(here, first, left)
-        right = jnp.where(here, last, right)
-    a_ref[...] = jnp.where(odd, left, right).astype(BF16)
-    b_ref[...] = jnp.where(odd, right, left).astype(BF16)
-    tables.wait()
-
-
-def rows_kernel(s_ref, xa_ref, xb_ref, e_ref, a_ref, b_ref, z_ref):
-    odd_y = lax.axis_index("gy") % 2 == 1
+    top, bottom = low_high(ya_ref[...], yb_ref[...], "gy")
+    left, right = pack_sides([jnp.concatenate([top[s], bottom[s]], 0) for s in range(6)])
+    left = jnp.concatenate([left[:16], l_ref[...], left[16:]], 0)
+    right = jnp.concatenate([right[:16], r_ref[...], right[16:]], 0)
+    a_ref[...] = jnp.where(odd, left, right)
+    b_ref[...] = jnp.where(odd, right, left)
+    for s in range(2):
+        z_ref[s] = jnp.concatenate([top[s], s_ref[s], bottom[s]], 0)
+
+
+def side_tiles(xa_ref, xb_ref):
     left, right = low_high(xa_ref[...], xb_ref[...], "gx")
     left, right = left.astype(F32), right.astype(F32)
-    low = lanes((128, 128)) < 64
-    e0 = jnp.where(low, left, pltpu.roll(right, 64, 1)).astype(BF16)
-    e1 = jnp.where(low, pltpu.roll(left, 64, 1), right).astype(BF16)
-    e_ref[0] = e0
-    e_ref[1] = e1
-    first = jnp.concatenate([s_ref[s, :16] for s in range(6)] + [e0[:16], e1[:16]], 0)
-    last = jnp.concatenate([s_ref[s, 112:] for s in range(6)] + [e0[112:], e1[112:]], 0)
-    a_ref[...] = jnp.where(odd_y, first, last)
-    b_ref[...] = jnp.where(odd_y, last, first)
-    z_ref[0] = s_ref[0]
-    z_ref[1] = s_ref[1]
-    z_ref[2] = e0
-
-
-def halo_kernel(ya_ref, yb_ref, z_ref):
-    top, bottom = low_high(ya_ref[...], yb_ref[...], "gy")
-    for n, at in enumerate((0, 16, 96)):
-        z_ref[16 * n : 16 * n + 16] = top[at : at + 16]
-        z_ref[48 + 16 * n : 64 + 16 * n] = bottom[at : at + 16]
+    low = lanes((160, 128)) < 64
+    return jnp.where(low, left, pltpu.roll(right, 64, 1)), jnp.where(low, pltpu.roll(left, 64, 1), right)
+
+
+def halo_kernel(xb_ref, xa_ref, h_ref):
+    tile, _ = side_tiles(xa_ref, xb_ref)
+    own = lanes((80, 128)) % 64 < 32
+    h_ref[...] = jnp.where(own, tile[:80], pltpu.roll(tile[80:], 32, 1)).astype(BF16)
 
 
 def low_high(a, b, axis):
@@ -318,17 +330,13 @@
 )
 
 
-def own_kernel(s_ref, e_ref, ya_ref, yb_ref, t_ref, o_ref, f_ref, f32_ref, scale_ref, *scratch):
+def own_kernel(xb_ref, xa_ref, ya_ref, yb_ref, s_ref, t_ref, o_ref, f_ref, f32_ref, scale_ref, *scratch):
     c = Tables(t_ref)
     w = dict(zip((*SCRATCH, "o", "sem"), scratch))
     w["f"] = f_ref
     top, bottom = low_high(ya_ref[...], yb_ref[...], "gy")
-
-    def tall(middle, n):
-        return jnp.concatenate([top[16 * n : 16 * n + 16], middle, bottom[16 * n : 16 * n + 16]], 0)
-
-    sections = [tall(s_ref[s], s) for s in range(6)]
-    edges = [tall(e_ref[g], 6 + g) for g in range(2)]
+    sections = [jnp.concatenate([top[s], s_ref[s], bottom[s]], 0) for s in range(6)]
+    edges = [tile.astype(BF16) for tile in side_tiles(xa_ref, xb_ref)]
     f32 = spectra(0, 0, sections, edges, c, w)
     scale = scales(0, sections, edges, c, w)
     store_scales(scale, w)
@@ -343,12 +351,12 @@
     flag = jnp.where(lax.axis_index("gz") == 0, 1.0, 0.0)
     w["f"][0] = f_ref[4]
     w["f"][1] = f_ref[5]
-    tall = [
-        jnp.concatenate([h_ref[16 * n : 16 * n + 16], z_ref[n], h_ref[48 + 16 * n : 64 + 16 * n]], 0)
-        for n in range(3)
-    ]
-    extra = spectra(6, 2, tall[:2], tall[2:], c, w)
-    scale = scales(6, tall[:2], tall[2:], c, w) * flag
+    sections = [z_ref[0], z_ref[1]]
+    sides = h_ref[...]
+    lower = pltpu.roll(sides.astype(F32), 96, 1).astype(BF16)
+    edges = [jnp.concatenate([sides, lower], 0)]
+    extra = spectra(6, 2, sections, edges, c, w)
+    scale = scales(6, sections, edges, c, w) * flag
     scale = jnp.where(lax.broadcasted_iota(jnp.int32, (32, 256), 0) % 8 >= 6, scale, scale_ref[...])
     store_scales(scale, w)
     f32 = jnp.where(lanes((128, 128)) % 32 >= 24, extra.astype(F32), f32_ref[...].astype(F32))
@@ -375,7 +383,8 @@
             for at in np.ndindex(*sizes)
         ]
 
-    return lax.ppermute(value_a, AXES, pairs(0)), lax.ppermute(value_b, AXES, pairs(1))
+    value_b = lax.ppermute(value_b, AXES, pairs(1))
+    return lax.ppermute(value_a, AXES, pairs(0)), value_b
 
 
 def other(value):
@@ -390,7 +399,7 @@
     return pltpu.CompilerParams(vmem_limit_bytes=mib * 2**20)
 
 
-def compute(sections, edges, ya, yb, z, rows, table):
+def compute(sections, xa, xb, ya, yb, z, sides, table):
     scratch = [make(6) for make in SCRATCH.values()]
     out, f, f32, scale = pl.pallas_call(
         own_kernel,
@@ -400,12 +409,12 @@
             shaped(128, 128),
             jax.ShapeDtypeStruct((32, 256), F32),
         ),
-        in_specs=[VMEM] * 5,
+        in_specs=[VMEM] * 6,
         out_specs=(HBM, VMEM, VMEM, VMEM),
         scratch_shapes=scratch + [pltpu.VMEM((9, 4, 128, 128), BF16), pltpu.SemaphoreType.DMA((9,))],
         compiler_params=params(16),
         cost_estimate=pl.CostEstimate(flops=10**9, bytes_accessed=4 * 10**6, transcendentals=0),
-    )(sections, edges, ya, yb, table)
+    )(xb, xa, ya, yb, sections, table)
     scratch = [make(2) for make in SCRATCH.values()]
     return pl.pallas_call(
         rest_kernel,
@@ -420,39 +429,49 @@
         ],
         input_output_aliases={6: 0},
         compiler_params=params(16),
-    )(z, rows, f, f32, scale, table, out)
+    )(z, sides, f, f32, scale, table, out)
 
 
 def local(sections):
-    edge = shaped(128, 128)
-    fixed = [pltpu.with_memory_space_constraint(value, pltpu.HBM) for value in (sections, constants()[0])]
-    xa, xb, sections, table = pl.pallas_call(
-        edges_kernel,
-        out_shape=(edge, edge, *(shaped(*value.shape) for value in fixed)),
-        in_specs=[HBM] * 2,
+    pixels = pltpu.with_memory_space_constraint(sections, pltpu.HBM)
+    table = constants()[0]
+    rows, side, middle = shaped(6, 16, 128), shaped(160, 128), shaped(128, 128)
+    ya, yb = pl.pallas_call(
+        first_kernel,
+        out_shape=(rows, rows),
+        in_specs=[HBM],
+        out_specs=(VMEM, VMEM),
+        scratch_shapes=[pltpu.SemaphoreType.DMA((2,))],
+        compiler_params=params(8),
+    )(pixels)
+    ya, yb = exchange(ya, yb, "gy")
+    sections, table, left, right = pl.pallas_call(
+        stage_kernel,
+        out_shape=(shaped(*sections.shape), shaped(*table.shape), middle, middle),
+        in_specs=[HBM, HBM],
         out_specs=(VMEM,) * 4,
         scratch_shapes=[pltpu.SemaphoreType.DMA((2,))],
         compiler_params=params(8),
-    )(*fixed)
+        cost_estimate=pl.CostEstimate(flops=0, bytes_accessed=2 * 10**6, transcendentals=0),
+    )(pixels, pltpu.with_memory_space_constraint(table, pltpu.HBM))
+    xa, xb, z = pl.pallas_call(
+        sides_kernel,
+        out_shape=(side, side, shaped(2, 160, 128)),
+        in_specs=[VMEM] * 6,
+        out_specs=(VMEM,) * 3,
+        compiler_params=params(8),
+    )(ya, yb, sections, left, right, table)
     xa, xb = exchange(xa, xb, "gx")
-    edges, ya, yb, z = pl.pallas_call(
-        rows_kernel,
-        out_shape=(shaped(2, 128, 128), edge, edge, shaped(3, 128, 128)),
-        in_specs=[VMEM] * 3,
-        out_specs=(VMEM,) * 4,
-        compiler_params=params(8),
-    )(sections, xa, xb)
-    ya, yb = exchange(ya, yb, "gy")
     z = other(z)
-    rows = pl.pallas_call(
+    sides = pl.pallas_call(
         halo_kernel,
-        out_shape=shaped(96, 128),
+        out_shape=shaped(80, 128),
         in_specs=[VMEM] * 2,
         out_specs=VMEM,
         compiler_params=params(8),
-    )(ya, yb)
-    rows = other(rows)
-    out = compute(sections, edges, ya, yb, z, rows, table)
+    )(xb, xa)
+    sides = other(sides)
+    out = compute(sections, xa, xb, ya, yb, z, sides, table)
     out = out.reshape(6, 2, 4, 32, 4, 128).transpose(0, 1, 2, 4, 3, 5)
     return out.reshape(6, 2, 4, 4, 4096)
 

time: 20.9 us -> 20.2 us (0.967)
  starting transfers between devices: 11.5 us -> 10.3 us
  Pallas kernels: 6.19 us -> 7.19 us
  waiting for transfers between devices: 3.02 us -> 2.43 us
    ppermute x4, starting transfers between devices: 7.41 us -> 6.01 us  [the longest x2 5.53 us: exchange(): value_b = lax.ppermute(value_b, AXES, pairs(1))]
    pallas_call x3 -> x4, Pallas kernels: 1.43 us -> 2.36 us  [the longest x1 1.31 us: local(): pl.pallas_call(stage_kernel, out_shape=(shaped(*sections.shape), shaped(*...]
    ppermute x2, waiting for transfers between devices: 0.57 us -> 0.25 us  [other(): return lax.ppermute(value, 'gz', [(0, 1), (1, 0)])]
    ppermute x4, waiting for transfers between devices: 2.45 us -> 2.19 us  [the longest x2 2.18 us: exchange(): value_b = lax.ppermute(value_b, AXES, pairs(1))]
  transfers between devices with their start and end apart: 6 -> 6, of which waited for: 2 -> 3; matrix products, arithmetic and copies ran while one was open for 0% -> 0% of each run, Pallas kernels for 14% -> 22%
where the time goes in v5:
time: 20.2 us; the launch traced here: 20 us
  starting transfers between devices  10.3 us (51%)
  Pallas kernels  7.19 us (36%)
  waiting for transfers between devices  2.43 us (12%)
    ppermute x2, starting transfers between devices, exchange(): value_b = lax.ppermute(value_b, AXES, pairs(1))  5.53 us
    ppermute x2, starting transfers between devices, other(): return lax.ppermute(value, 'gz', [(0, 1), (1, 0)])  4.29 us
    pallas_call x1, Pallas kernels, compute(): pl.pallas_call(own_kernel, out_shape=(shaped(6, 2, 4, 128, 128), shaped(6...  2.91 us
    ppermute x2, waiting for transfers between devices, exchange(): value_b = lax.ppermute(value_b, AXES, pairs(1))  2.18 us
    pallas_call x1, Pallas kernels, compute(): pl.pallas_call(rest_kernel, out_shape=shaped(6, 2, 4, 128, 128), in_specs...  1.91 us
    pallas_call x1, Pallas kernels, local(): pl.pallas_call(stage_kernel, out_shape=(shaped(*sections.shape), shaped(*...  1.31 us
    pallas_call x1, Pallas kernels, local(): pl.pallas_call(first_kernel, out_shape=(rows, rows), in_specs=[HBM], out_...  0.77 us
    ppermute x2, starting transfers between devices, exchange(): return (lax.ppermute(value_a, AXES, pairs(0)), value_b)  0.48 us
  transfers between devices with their start and end apart: 6, of which 3 were waited for; matrix products, arithmetic and copies ran while one was open for 0% of the time, Pallas kernels for 22%

profile of v5, /device:TPU:98, one launch (start us, length us, event | category | flops | bytes accessed | tf_op | source)
XLA Modules:
  0.0 20.0 jit_solution(12801842226555968031)
XLA Ops:
  0.0 0.8 %shard_map.28 = (bf16[6,16,128]{2,1,0:T(8,128)(2,1)S(1)}, bf16[6,16,128]{2,1,0:T(8,128)(2,1)S(1)}) custom-call(bf16[6,128,128]{2,1,0:T(8,128)(2,1)} %s_hbm.3), custom_call_target="tpu_custom_call" | custom-call | tf_op jit(solution)/shard_map/pallas_call | solution.py:439
  0.8 0.2 collective-permute-start
  1.0 4.0 %collective-permute-start.1 = (bf16[6,16,128]{2,1,0:T(8,128)(2,1)S(1)}, bf16[6,16,128]{2,1,0:T(8,128)(2,1)S(1)}, u32[]{:S(2)}, u32[]{:S(2)}) collective-permute-start(bf16[6,16,128]{2,1,0:T(8,128)(2,1)S(1)} %get-tuple-element.19), channel_id=1, source_target_pairs={{0,16},{1,17},{2,4},{3,5},{4,2},{5,3},{6,8},{7,9},{8,6},{9,7},{10,... | collective-permute-start | bytes 73736 | tf_op jit(solution)/shard_map/ppermute | solution.py:386
  5.0 1.3 %shard_map.29 = (bf16[6,128,128]{2,1,0:T(8,128)(2,1)S(1)}, bf16[3648,128]{1,0:T(8,128)(2,1)S(1)}, bf16[128,128]{1,0:T(8,128)(2,1)S(1)}, bf16[128,128]{1,0:T(8,128)(2,1)S(1)}) custom-call(bf16[6,128,128]{2,1,0:T(8,128)(2,1)} %s_hbm.3, bf16[3648,128]{1,0:T(8,128)(2,1)} %constant.2.clone.t_hbm), custom_call_target="tpu_custom_call" | custom-call | bytes 2000000 | tf_op jit(solution)/shard_map/pallas_call | solution.py:448
  6.3 0.0 collective-permute-done.ya_ref
  6.3 0.5 %collective-permute-done.1.yb_ref = bf16[6,16,128]{2,1,0:T(8,128)(2,1)S(1)} collective-permute-done((bf16[6,16,128]{2,1,0:T(8,128)(2,1)S(1)}, bf16[6,16,128]{2,1,0:T(8,128)(2,1)S(1)}, u32[]{:S(2)}, u32[]{:S(2)}) %collective-permute-start.1) | collective-permute-done | bytes 24608 | tf_op jit(solution)/shard_map/ppermute | solution.py:386
  6.8 0.1 shard_map.30
  6.9 1.5 %collective-permute-start.3 = (bf16[160,128]{1,0:T(8,128)(2,1)S(1)}, bf16[160,128]{1,0:T(8,128)(2,1)S(1)}, u32[]{:S(2)}, u32[]{:S(2)}) collective-permute-start(bf16[160,128]{1,0:T(8,128)(2,1)S(1)} %get-tuple-element.25), channel_id=1, source_target_pairs={{0,2},{1,3},{2,0},{3,1},{4,6},{5,7},{6,4},{7,5},{8,10},{9,11},{10,... | collective-permute-start | bytes 122888 | tf_op jit(solution)/shard_map/ppermute | solution.py:386
  8.4 0.3 %collective-permute-start.4 = (bf16[160,128]{1,0:T(8,128)(2,1)S(1)}, bf16[160,128]{1,0:T(8,128)(2,1)S(1)}, u32[]{:S(2)}, u32[]{:S(2)}) collective-permute-start(bf16[160,128]{1,0:T(8,128)(2,1)S(1)} %get-tuple-element.26), channel_id=1, source_target_pairs={{0,16},{1,17},{2,18},{3,19},{4,20},{5,21},{6,22},{7,23},{8,24},{9,... | collective-permute-start | bytes 122888 | tf_op jit(solution)/shard_map/ppermute | solution.py:387
  8.7 2.1 %collective-permute-start.2 = (bf16[2,160,128]{2,1,0:T(8,128)(2,1)S(1)}, bf16[2,160,128]{2,1,0:T(8,128)(2,1)S(1)}, u32[]{:S(2)}, u32[]{:S(2)}) collective-permute-start(bf16[2,160,128]{2,1,0:T(8,128)(2,1)S(1)} %get-tuple-element.24), channel_id=1, source_target_pairs={{0,1},{1,0},{2,3},{3,2},{4,5},{5,4},{6,7},{7,6},{8,9},{9,8},{10,11... | collective-permute-start | bytes 245768 | tf_op jit(solution)/shard_map/ppermute | solution.py:391
  10.9 1.7 %collective-permute-done.3.xb_ref = bf16[160,128]{1,0:T(8,128)(2,1)S(1)} collective-permute-done((bf16[160,128]{1,0:T(8,128)(2,1)S(1)}, bf16[160,128]{1,0:T(8,128)(2,1)S(1)}, u32[]{:S(2)}, u32[]{:S(2)}) %collective-permute-start.3) | collective-permute-done | bytes 40992 | tf_op jit(solution)/shard_map/ppermute | solution.py:386
  12.6 0.0 collective-permute-done.4.xa_ref
  12.6 0.2 shard_map.31
  12.7 2.2 %collective-permute-start.5 = (bf16[80,128]{1,0:T(8,128)(2,1)S(1)}, bf16[80,128]{1,0:T(8,128)(2,1)S(1)}, u32[]{:S(2)}, u32[]{:S(2)}) collective-permute-start(bf16[80,128]{1,0:T(8,128)(2,1)S(1)} %shard_map.31), channel_id=1, source_target_pairs={{0,1},{1,0},{2,3},{3,2},{4,5},{5,4},{6,7},{7,6},{8,9},{9,8},{10,11... | collective-permute-start | bytes 61448 | tf_op jit(solution)/shard_map/ppermute | solution.py:391
  14.9 2.9 %shard_map.32 = (bf16[6,2,4,128,128]{4,3,2,1,0:T(8,128)(2,1)}, bf16[6,4,128,128]{3,2,1,0:T(8,128)(2,1)S(1)}, bf16[128,128]{1,0:T(8,128)(2,1)S(1)}, f32[32,256]{1,0:T(8,128)S(1)}) custom-call(bf16[160,128]{1,0:T(8,128)(2,1)S(1)} %collective-permute-done.3.xb_ref, bf16[160,128]{1,0:T(8,128)(2,1)S(1)} %collective-permute-done.4.xa_ref, ...), custom_call_target="tpu_custom_call" | custom-call | flops 1000000000 | bytes 4000000 | tf_op jit(solution)/shard_map/pallas_call | solution.py:404
  17.8 0.2 %collective-permute-done.5.h_ref = bf16[80,128]{1,0:T(8,128)(2,1)S(1)} collective-permute-done((bf16[80,128]{1,0:T(8,128)(2,1)S(1)}, bf16[80,128]{1,0:T(8,128)(2,1)S(1)}, u32[]{:S(2)}, u32[]{:S(2)}) %collective-permute-start.5) | collective-permute-done | bytes 20512 | tf_op jit(solution)/shard_map/ppermute | solution.py:391
  18.0 0.0 collective-permute-done.2.z_ref
  18.1 1.9 %shard_map.33 = bf16[6,2,4,128,128]{4,3,2,1,0:T(8,128)(2,1)} custom-call(bf16[2,160,128]{2,1,0:T(8,128)(2,1)S(1)} %collective-permute-done.2.z_ref, bf16[80,128]{1,0:T(8,128)(2,1)S(1)} %collective-permute-done.5.h_ref, bf16[6,4,128,128]{3,2,1,0:T(8,128)(2,1)S(1)} %get-tuple-element.27.f_ref, ...), custom_call_target="tpu_custom_call", output_to_operand_aliasing={{}: (6, {})} | custom-call | tf_op jit(solution)/shard_map/pallas_call | solution.py:419
Async XLA Ops:
  0.8 5.6 %collective-permute-start = (bf16[6,16,128]{2,1,0:T(8,128)(2,1)S(1)}, bf16[6,16,128]{2,1,0:T(8,128)(2,1)S(1)}, u32[]{:S(2)}, u32[]{:S(2)}) collective-permute-start(bf16[6,16,128]{2,1,0:T(8,128)(2,1)S(1)} %get-tuple-element.18), channel_id=1, source_target_pairs={{0,2},{1,3},{2,0},{3,1},{4,6},{5,7},{6,4},{7,5},{8,10},{9,11},{10,... | collective-permute-start | bytes 73736 | tf_op jit(solution)/shard_map/ppermute | solution.py:387
  1.0 5.8 %collective-permute-start.1 = (bf16[6,16,128]{2,1,0:T(8,128)(2,1)S(1)}, bf16[6,16,128]{2,1,0:T(8,128)(2,1)S(1)}, u32[]{:S(2)}, u32[]{:S(2)}) collective-permute-start(bf16[6,16,128]{2,1,0:T(8,128)(2,1)S(1)} %get-tuple-element.19), channel_id=1, source_target_pairs={{0,16},{1,17},{2,4},{3,5},{4,2},{5,3},{6,8},{7,9},{8,6},{9,7},{10,... | collective-permute-start | bytes 73736 | tf_op jit(solution)/shard_map/ppermute | solution.py:386
  6.9 5.6 %collective-permute-start.3 = (bf16[160,128]{1,0:T(8,128)(2,1)S(1)}, bf16[160,128]{1,0:T(8,128)(2,1)S(1)}, u32[]{:S(2)}, u32[]{:S(2)}) collective-permute-start(bf16[160,128]{1,0:T(8,128)(2,1)S(1)} %get-tuple-element.25), channel_id=1, source_target_pairs={{0,2},{1,3},{2,0},{3,1},{4,6},{5,7},{6,4},{7,5},{8,10},{9,11},{10,... | collective-permute-start | bytes 122888 | tf_op jit(solution)/shard_map/ppermute | solution.py:386
  8.4 4.1 %collective-permute-start.4 = (bf16[160,128]{1,0:T(8,128)(2,1)S(1)}, bf16[160,128]{1,0:T(8,128)(2,1)S(1)}, u32[]{:S(2)}, u32[]{:S(2)}) collective-permute-start(bf16[160,128]{1,0:T(8,128)(2,1)S(1)} %get-tuple-element.26), channel_id=1, source_target_pairs={{0,16},{1,17},{2,18},{3,19},{4,20},{5,21},{6,22},{7,23},{8,24},{9,... | collective-permute-start | bytes 122888 | tf_op jit(solution)/shard_map/ppermute | solution.py:387
  8.7 9.3 %collective-permute-start.2 = (bf16[2,160,128]{2,1,0:T(8,128)(2,1)S(1)}, bf16[2,160,128]{2,1,0:T(8,128)(2,1)S(1)}, u32[]{:S(2)}, u32[]{:S(2)}) collective-permute-start(bf16[2,160,128]{2,1,0:T(8,128)(2,1)S(1)} %get-tuple-element.24), channel_id=1, source_target_pairs={{0,1},{1,0},{2,3},{3,2},{4,5},{5,4},{6,7},{7,6},{8,9},{9,8},{10,11... | collective-permute-start | bytes 245768 | tf_op jit(solution)/shard_map/ppermute | solution.py:391
  12.7 5.3 %collective-permute-start.5 = (bf16[80,128]{1,0:T(8,128)(2,1)S(1)}, bf16[80,128]{1,0:T(8,128)(2,1)S(1)}, u32[]{:S(2)}, u32[]{:S(2)}) collective-permute-start(bf16[80,128]{1,0:T(8,128)(2,1)S(1)} %shard_map.31), channel_id=1, source_target_pairs={{0,1},{1,0},{2,3},{3,2},{4,5},{5,4},{6,7},{7,6},{8,9},{9,8},{10,11... | collective-permute-start | bytes 61448 | tf_op jit(solution)/shard_map/ppermute | solution.py:391

commit v6 on v5

--- a/solution.py
+++ b/solution.py
@@ -127,9 +127,8 @@
     right = jnp.zeros(lane.shape, F32)
     for s, block in enumerate(blocks):
         block = block.astype(F32)
-        here = (lane // 16) == s
-        left = jnp.where(here, pltpu.roll(block, 16 * s, 1) if s else block, left)
-        right = jnp.where(here, pltpu.roll(block, 16 * s + 16, 1), right)
+        left = jnp.where(lane // 16 == (s + 4) % 8, pltpu.roll(block, (16 * s + 64) % 128, 1) if s != 4 else block, left)
+        right = jnp.where(lane // 16 == s, pltpu.roll(block, 16 * s + 16, 1), right)
     return left.astype(BF16), right.astype(BF16)
 
 
@@ -157,13 +156,12 @@
 
 def side_tiles(xa_ref, xb_ref):
     left, right = low_high(xa_ref[...], xb_ref[...], "gx")
-    left, right = left.astype(F32), right.astype(F32)
     low = lanes((160, 128)) < 64
-    return jnp.where(low, left, pltpu.roll(right, 64, 1)), jnp.where(low, pltpu.roll(left, 64, 1), right)
+    return jnp.where(low, left, right), jnp.where(low, right, left)
 
 
 def halo_kernel(xb_ref, xa_ref, h_ref):
-    tile, _ = side_tiles(xa_ref, xb_ref)
+    tile = side_tiles(xa_ref, xb_ref)[0].astype(F32)
     own = lanes((80, 128)) % 64 < 32
     h_ref[...] = jnp.where(own, tile[:80], pltpu.roll(tile[80:], 32, 1)).astype(BF16)
 
@@ -192,9 +190,9 @@
         q, g = s % 4, s // 4
         mean, square = column_stats(block)
         mean_e, square_e = edge_stats[g]
-        if q:
-            mean_e = pltpu.roll(mean_e, 128 - 16 * q, 1)
-            square_e = pltpu.roll(square_e, 128 - 16 * q, 1)
+        if s:
+            mean_e = pltpu.roll(mean_e, 128 - 16 * q - 64 * g, 1)
+            square_e = pltpu.roll(square_e, 128 - 16 * q - 64 * g, 1)
         w["mu"][:, first + s, :128] = mean
         w["mu"][:, first + s, 128:] = mean_e
         w["sq"][:, first + s, :128] = square
@@ -228,7 +226,8 @@
         q = s % 4
         gap0 = jnp.zeros((16 * q, 256), BF16)
         gap1 = jnp.zeros((48 - 16 * q, 256), BF16)
-        pieces = [c["own"], gap0, sides[:16], gap1, gap0, sides[16:], gap1]
+        one, two = (sides[:16], sides[16:]) if s < 4 else (sides[16:], sides[:16])
+        pieces = [c["own"], gap0, one, gap1, gap0, two, gap1]
         table = jnp.concatenate([p for p in pieces if p.shape[0]], 0)
         w["g"][s] = dot(jnp.concatenate([block, edges[s // 4]], 1), table)
     special = jnp.zeros((64, 128), F32)
@@ -312,11 +311,12 @@
             w["o"][p - lo, i] = mix[i].astype(BF16)
         copy(p).start()
 
-    ready = correlate(lo)
-    for p in range(lo, hi):
-        following = correlate(p + 1) if p + 1 < hi else None
-        store(p, *last(p, ready))
-        ready = following
+    ready = {}
+    for p in range(lo, hi + 2):
+        if p < hi:
+            ready[p] = correlate(p)
+        if p >= lo + 2:
+            store(p - 2, *last(p - 2, ready.pop(p - 2)))
     for p in range(lo, hi):
         copy(p).wait()
 
@@ -336,7 +336,7 @@
     w["f"] = f_ref
     top, bottom = low_high(ya_ref[...], yb_ref[...], "gy")
     sections = [jnp.concatenate([top[s], s_ref[s], bottom[s]], 0) for s in range(6)]
-    edges = [tile.astype(BF16) for tile in side_tiles(xa_ref, xb_ref)]
+    edges = side_tiles(xa_ref, xb_ref)
     f32 = spectra(0, 0, sections, edges, c, w)
     scale = scales(0, sections, edges, c, w)
     store_scales(scale, w)

time: 20.2 us -> 20.1 us (level)
  Pallas kernels: 7.19 us -> 6.89 us
  transfers between devices with their start and end apart: 6 -> 6, of which waited for: 3 -> 3; matrix products, arithmetic and copies ran while one was open for 0% -> 0% of each run, Pallas kernels for 22% -> 21%
where the time goes in v6:
time: 20.1 us; the launch traced here: 19.8 us
  starting transfers between devices  10.3 us (51%)
  Pallas kernels  6.89 us (34%)
  waiting for transfers between devices  2.58 us (13%)
    ppermute x2, starting transfers between devices, exchange(): value_b = lax.ppermute(value_b, AXES, pairs(1))  5.53 us
    ppermute x2, starting transfers between devices, other(): return lax.ppermute(value, 'gz', [(0, 1), (1, 0)])  4.31 us
    pallas_call x1, Pallas kernels, compute(): pl.pallas_call(own_kernel, out_shape=(shaped(6, 2, 4, 128, 128), shaped(6...  2.76 us
    ppermute x2, waiting for transfers between devices, exchange(): value_b = lax.ppermute(value_b, AXES, pairs(1))  2.18 us
    pallas_call x1, Pallas kernels, compute(): pl.pallas_call(rest_kernel, out_shape=shaped(6, 2, 4, 128, 128), in_specs...  1.83 us
    pallas_call x1, Pallas kernels, local(): pl.pallas_call(stage_kernel, out_shape=(shaped(*sections.shape), shaped(*...  1.31 us
    pallas_call x1, Pallas kernels, local(): pl.pallas_call(first_kernel, out_shape=(rows, rows), in_specs=[HBM], out_...  0.77 us
    ppermute x2, starting transfers between devices, exchange(): return (lax.ppermute(value_a, AXES, pairs(0)), value_b)  0.48 us
  transfers between devices with their start and end apart: 6, of which 3 were waited for; matrix products, arithmetic and copies ran while one was open for 0% of the time, Pallas kernels for 21%

profile of v6, /device:TPU:98, one launch (start us, length us, event | category | flops | bytes accessed | tf_op | source)
XLA Modules:
  0.0 19.8 jit_solution(10589636424275545627)
XLA Ops:
  0.0 0.8 %shard_map.28 = (bf16[6,16,128]{2,1,0:T(8,128)(2,1)S(1)}, bf16[6,16,128]{2,1,0:T(8,128)(2,1)S(1)}) custom-call(bf16[6,128,128]{2,1,0:T(8,128)(2,1)} %s_hbm.3), custom_call_target="tpu_custom_call" | custom-call | tf_op jit(solution)/shard_map/pallas_call | solution.py:439
  0.8 0.2 collective-permute-start
  1.0 4.0 %collective-permute-start.1 = (bf16[6,16,128]{2,1,0:T(8,128)(2,1)S(1)}, bf16[6,16,128]{2,1,0:T(8,128)(2,1)S(1)}, u32[]{:S(2)}, u32[]{:S(2)}) collective-permute-start(bf16[6,16,128]{2,1,0:T(8,128)(2,1)S(1)} %get-tuple-element.19), channel_id=1, source_target_pairs={{0,16},{1,17},{2,4},{3,5},{4,2},{5,3},{6,8},{7,9},{8,6},{9,7},{10,... | collective-permute-start | bytes 73736 | tf_op jit(solution)/shard_map/ppermute | solution.py:386
  5.0 1.3 %shard_map.29 = (bf16[6,128,128]{2,1,0:T(8,128)(2,1)S(1)}, bf16[3648,128]{1,0:T(8,128)(2,1)S(1)}, bf16[128,128]{1,0:T(8,128)(2,1)S(1)}, bf16[128,128]{1,0:T(8,128)(2,1)S(1)}) custom-call(bf16[6,128,128]{2,1,0:T(8,128)(2,1)} %s_hbm.3, bf16[3648,128]{1,0:T(8,128)(2,1)} %constant.2.clone.t_hbm), custom_call_target="tpu_custom_call" | custom-call | bytes 2000000 | tf_op jit(solution)/shard_map/pallas_call | solution.py:448
  6.3 0.0 collective-permute-done.ya_ref
  6.3 0.5 %collective-permute-done.1.yb_ref = bf16[6,16,128]{2,1,0:T(8,128)(2,1)S(1)} collective-permute-done((bf16[6,16,128]{2,1,0:T(8,128)(2,1)S(1)}, bf16[6,16,128]{2,1,0:T(8,128)(2,1)S(1)}, u32[]{:S(2)}, u32[]{:S(2)}) %collective-permute-start.1) | collective-permute-done | bytes 24608 | tf_op jit(solution)/shard_map/ppermute | solution.py:386
  6.8 0.1 shard_map.30
  6.9 1.5 %collective-permute-start.3 = (bf16[160,128]{1,0:T(8,128)(2,1)S(1)}, bf16[160,128]{1,0:T(8,128)(2,1)S(1)}, u32[]{:S(2)}, u32[]{:S(2)}) collective-permute-start(bf16[160,128]{1,0:T(8,128)(2,1)S(1)} %get-tuple-element.25), channel_id=1, source_target_pairs={{0,2},{1,3},{2,0},{3,1},{4,6},{5,7},{6,4},{7,5},{8,10},{9,11},{10,... | collective-permute-start | bytes 122888 | tf_op jit(solution)/shard_map/ppermute | solution.py:386
  8.4 0.3 %collective-permute-start.4 = (bf16[160,128]{1,0:T(8,128)(2,1)S(1)}, bf16[160,128]{1,0:T(8,128)(2,1)S(1)}, u32[]{:S(2)}, u32[]{:S(2)}) collective-permute-start(bf16[160,128]{1,0:T(8,128)(2,1)S(1)} %get-tuple-element.26), channel_id=1, source_target_pairs={{0,16},{1,17},{2,18},{3,19},{4,20},{5,21},{6,22},{7,23},{8,24},{9,... | collective-permute-start | bytes 122888 | tf_op jit(solution)/shard_map/ppermute | solution.py:387
  8.7 2.1 %collective-permute-start.2 = (bf16[2,160,128]{2,1,0:T(8,128)(2,1)S(1)}, bf16[2,160,128]{2,1,0:T(8,128)(2,1)S(1)}, u32[]{:S(2)}, u32[]{:S(2)}) collective-permute-start(bf16[2,160,128]{2,1,0:T(8,128)(2,1)S(1)} %get-tuple-element.24), channel_id=1, source_target_pairs={{0,1},{1,0},{2,3},{3,2},{4,5},{5,4},{6,7},{7,6},{8,9},{9,8},{10,11... | collective-permute-start | bytes 245768 | tf_op jit(solution)/shard_map/ppermute | solution.py:391
  10.9 1.7 %collective-permute-done.3.xb_ref = bf16[160,128]{1,0:T(8,128)(2,1)S(1)} collective-permute-done((bf16[160,128]{1,0:T(8,128)(2,1)S(1)}, bf16[160,128]{1,0:T(8,128)(2,1)S(1)}, u32[]{:S(2)}, u32[]{:S(2)}) %collective-permute-start.3) | collective-permute-done | bytes 40992 | tf_op jit(solution)/shard_map/ppermute | solution.py:386
  12.6 0.0 collective-permute-done.4.xa_ref
  12.6 0.1 shard_map.31
  12.7 2.2 %collective-permute-start.5 = (bf16[80,128]{1,0:T(8,128)(2,1)S(1)}, bf16[80,128]{1,0:T(8,128)(2,1)S(1)}, u32[]{:S(2)}, u32[]{:S(2)}) collective-permute-start(bf16[80,128]{1,0:T(8,128)(2,1)S(1)} %shard_map.31), channel_id=1, source_target_pairs={{0,1},{1,0},{2,3},{3,2},{4,5},{5,4},{6,7},{7,6},{8,9},{9,8},{10,11... | collective-permute-start | bytes 61448 | tf_op jit(solution)/shard_map/ppermute | solution.py:391
  14.8 2.8 %shard_map.32 = (bf16[6,2,4,128,128]{4,3,2,1,0:T(8,128)(2,1)}, bf16[6,4,128,128]{3,2,1,0:T(8,128)(2,1)S(1)}, bf16[128,128]{1,0:T(8,128)(2,1)S(1)}, f32[32,256]{1,0:T(8,128)S(1)}) custom-call(bf16[160,128]{1,0:T(8,128)(2,1)S(1)} %collective-permute-done.3.xb_ref, bf16[160,128]{1,0:T(8,128)(2,1)S(1)} %collective-permute-done.4.xa_ref, ...), custom_call_target="tpu_custom_call" | custom-call | flops 1000000000 | bytes 4000000 | tf_op jit(solution)/shard_map/pallas_call | solution.py:404
  17.6 0.4 %collective-permute-done.5.h_ref = bf16[80,128]{1,0:T(8,128)(2,1)S(1)} collective-permute-done((bf16[80,128]{1,0:T(8,128)(2,1)S(1)}, bf16[80,128]{1,0:T(8,128)(2,1)S(1)}, u32[]{:S(2)}, u32[]{:S(2)}) %collective-permute-start.5) | collective-permute-done | bytes 20512 | tf_op jit(solution)/shard_map/ppermute | solution.py:391
  18.0 0.0 collective-permute-done.2.z_ref
  18.0 1.8 %shard_map.33 = bf16[6,2,4,128,128]{4,3,2,1,0:T(8,128)(2,1)} custom-call(bf16[2,160,128]{2,1,0:T(8,128)(2,1)S(1)} %collective-permute-done.2.z_ref, bf16[80,128]{1,0:T(8,128)(2,1)S(1)} %collective-permute-done.5.h_ref, bf16[6,4,128,128]{3,2,1,0:T(8,128)(2,1)S(1)} %get-tuple-element.27.f_ref, ...), custom_call_target="tpu_custom_call", output_to_operand_aliasing={{}: (6, {})} | custom-call | tf_op jit(solution)/shard_map/pallas_call | solution.py:419
Async XLA Ops:
  0.8 5.6 %collective-permute-start = (bf16[6,16,128]{2,1,0:T(8,128)(2,1)S(1)}, bf16[6,16,128]{2,1,0:T(8,128)(2,1)S(1)}, u32[]{:S(2)}, u32[]{:S(2)}) collective-permute-start(bf16[6,16,128]{2,1,0:T(8,128)(2,1)S(1)} %get-tuple-element.18), channel_id=1, source_target_pairs={{0,2},{1,3},{2,0},{3,1},{4,6},{5,7},{6,4},{7,5},{8,10},{9,11},{10,... | collective-permute-start | bytes 73736 | tf_op jit(solution)/shard_map/ppermute | solution.py:387
  1.0 5.8 %collective-permute-start.1 = (bf16[6,16,128]{2,1,0:T(8,128)(2,1)S(1)}, bf16[6,16,128]{2,1,0:T(8,128)(2,1)S(1)}, u32[]{:S(2)}, u32[]{:S(2)}) collective-permute-start(bf16[6,16,128]{2,1,0:T(8,128)(2,1)S(1)} %get-tuple-element.19), channel_id=1, source_target_pairs={{0,16},{1,17},{2,4},{3,5},{4,2},{5,3},{6,8},{7,9},{8,6},{9,7},{10,... | collective-permute-start | bytes 73736 | tf_op jit(solution)/shard_map/ppermute | solution.py:386
  6.9 5.6 %collective-permute-start.3 = (bf16[160,128]{1,0:T(8,128)(2,1)S(1)}, bf16[160,128]{1,0:T(8,128)(2,1)S(1)}, u32[]{:S(2)}, u32[]{:S(2)}) collective-permute-start(bf16[160,128]{1,0:T(8,128)(2,1)S(1)} %get-tuple-element.25), channel_id=1, source_target_pairs={{0,2},{1,3},{2,0},{3,1},{4,6},{5,7},{6,4},{7,5},{8,10},{9,11},{10,... | collective-permute-start | bytes 122888 | tf_op jit(solution)/shard_map/ppermute | solution.py:386
  8.4 4.1 %collective-permute-start.4 = (bf16[160,128]{1,0:T(8,128)(2,1)S(1)}, bf16[160,128]{1,0:T(8,128)(2,1)S(1)}, u32[]{:S(2)}, u32[]{:S(2)}) collective-permute-start(bf16[160,128]{1,0:T(8,128)(2,1)S(1)} %get-tuple-element.26), channel_id=1, source_target_pairs={{0,16},{1,17},{2,18},{3,19},{4,20},{5,21},{6,22},{7,23},{8,24},{9,... | collective-permute-start | bytes 122888 | tf_op jit(solution)/shard_map/ppermute | solution.py:387
  8.7 9.3 %collective-permute-start.2 = (bf16[2,160,128]{2,1,0:T(8,128)(2,1)S(1)}, bf16[2,160,128]{2,1,0:T(8,128)(2,1)S(1)}, u32[]{:S(2)}, u32[]{:S(2)}) collective-permute-start(bf16[2,160,128]{2,1,0:T(8,128)(2,1)S(1)} %get-tuple-element.24), channel_id=1, source_target_pairs={{0,1},{1,0},{2,3},{3,2},{4,5},{5,4},{6,7},{7,6},{8,9},{9,8},{10,11... | collective-permute-start | bytes 245768 | tf_op jit(solution)/shard_map/ppermute | solution.py:391
  12.7 5.3 %collective-permute-start.5 = (bf16[80,128]{1,0:T(8,128)(2,1)S(1)}, bf16[80,128]{1,0:T(8,128)(2,1)S(1)}, u32[]{:S(2)}, u32[]{:S(2)}) collective-permute-start(bf16[80,128]{1,0:T(8,128)(2,1)S(1)} %shard_map.31), channel_id=1, source_target_pairs={{0,1},{1,0},{2,3},{3,2},{4,5},{5,4},{6,7},{7,6},{8,9},{9,8},{10,11... | collective-permute-start | bytes 61448 | tf_op jit(solution)/shard_map/ppermute | solution.py:391

commit v7 on v6

--- a/solution.py
+++ b/solution.py
@@ -308,7 +308,7 @@
                 o = odd[32 * i : 32 * i + 32, 128 * half : 128 * half + 128] * o_scale
                 mix[i, pl.ds(2 * half, 32, stride=4), :] = jnp.where(low, e, o)
                 mix[i, pl.ds(2 * half + 1, 32, stride=4), :] = pltpu.roll(jnp.where(low, o, e), 64, 1)
-            w["o"][p - lo, i] = mix[i].astype(BF16)
+            w["o"][p - lo, i] = mix[i, :128].astype(BF16)
         copy(p).start()
 
     ready = {}
@@ -326,7 +326,7 @@
     mu=lambda n: pltpu.VMEM((5, 8, 256), F32),
     sq=lambda n: pltpu.VMEM((5, 8, 256), F32),
     scale=lambda n: pltpu.VMEM((2, 2, 4, 8, 128), F32),
-    mix=lambda n: pltpu.VMEM((2, 4, 128, 128), F32),
+    mix=lambda n: pltpu.VMEM((2, 4, 136, 128), F32),
 )
 
 

time: 20.1 us -> 20.1 us (level)
  no operation moved by 1% of the time
where the time goes in v7:
time: 20.1 us; the launch traced here: 19.8 us
  starting transfers between devices  10.3 us (51%)
  Pallas kernels  6.88 us (34%)
  waiting for transfers between devices  2.59 us (13%)
    ppermute x2, starting transfers between devices, exchange(): value_b = lax.ppermute(value_b, AXES, pairs(1))  5.53 us
    ppermute x2, starting transfers between devices, other(): return lax.ppermute(value, 'gz', [(0, 1), (1, 0)])  4.31 us
    pallas_call x1, Pallas kernels, compute(): pl.pallas_call(own_kernel, out_shape=(shaped(6, 2, 4, 128, 128), shaped(6...  2.75 us
    ppermute x2, waiting for transfers between devices, exchange(): value_b = lax.ppermute(value_b, AXES, pairs(1))  2.18 us
    pallas_call x1, Pallas kernels, compute(): pl.pallas_call(rest_kernel, out_shape=shaped(6, 2, 4, 128, 128), in_specs...  1.83 us
    pallas_call x1, Pallas kernels, local(): pl.pallas_call(stage_kernel, out_shape=(shaped(*sections.shape), shaped(*...  1.31 us
    pallas_call x1, Pallas kernels, local(): pl.pallas_call(first_kernel, out_shape=(rows, rows), in_specs=[HBM], out_...  0.77 us
    ppermute x2, starting transfers between devices, exchange(): return (lax.ppermute(value_a, AXES, pairs(0)), value_b)  0.48 us
  transfers between devices with their start and end apart: 6, of which 3 were waited for; matrix products, arithmetic and copies ran while one was open for 0% of the time, Pallas kernels for 21%

profile of v7, /device:TPU:98, one launch (start us, length us, event | category | flops | bytes accessed | tf_op | source)
XLA Modules:
  0.0 19.8 jit_solution(14609476515703754472)
XLA Ops:
  0.0 0.8 %shard_map.28 = (bf16[6,16,128]{2,1,0:T(8,128)(2,1)S(1)}, bf16[6,16,128]{2,1,0:T(8,128)(2,1)S(1)}) custom-call(bf16[6,128,128]{2,1,0:T(8,128)(2,1)} %s_hbm.3), custom_call_target="tpu_custom_call" | custom-call | tf_op jit(solution)/shard_map/pallas_call | solution.py:439
  0.8 0.2 collective-permute-start
  1.0 4.0 %collective-permute-start.1 = (bf16[6,16,128]{2,1,0:T(8,128)(2,1)S(1)}, bf16[6,16,128]{2,1,0:T(8,128)(2,1)S(1)}, u32[]{:S(2)}, u32[]{:S(2)}) collective-permute-start(bf16[6,16,128]{2,1,0:T(8,128)(2,1)S(1)} %get-tuple-element.19), channel_id=1, source_target_pairs={{0,16},{1,17},{2,4},{3,5},{4,2},{5,3},{6,8},{7,9},{8,6},{9,7},{10,... | collective-permute-start | bytes 73736 | tf_op jit(solution)/shard_map/ppermute | solution.py:386
  5.0 1.3 %shard_map.29 = (bf16[6,128,128]{2,1,0:T(8,128)(2,1)S(1)}, bf16[3648,128]{1,0:T(8,128)(2,1)S(1)}, bf16[128,128]{1,0:T(8,128)(2,1)S(1)}, bf16[128,128]{1,0:T(8,128)(2,1)S(1)}) custom-call(bf16[6,128,128]{2,1,0:T(8,128)(2,1)} %s_hbm.3, bf16[3648,128]{1,0:T(8,128)(2,1)} %constant.2.clone.t_hbm), custom_call_target="tpu_custom_call" | custom-call | bytes 2000000 | tf_op jit(solution)/shard_map/pallas_call | solution.py:448
  6.3 0.0 collective-permute-done.ya_ref
  6.3 0.5 %collective-permute-done.1.yb_ref = bf16[6,16,128]{2,1,0:T(8,128)(2,1)S(1)} collective-permute-done((bf16[6,16,128]{2,1,0:T(8,128)(2,1)S(1)}, bf16[6,16,128]{2,1,0:T(8,128)(2,1)S(1)}, u32[]{:S(2)}, u32[]{:S(2)}) %collective-permute-start.1) | collective-permute-done | bytes 24608 | tf_op jit(solution)/shard_map/ppermute | solution.py:386
  6.8 0.1 shard_map.30
  6.9 1.5 %collective-permute-start.3 = (bf16[160,128]{1,0:T(8,128)(2,1)S(1)}, bf16[160,128]{1,0:T(8,128)(2,1)S(1)}, u32[]{:S(2)}, u32[]{:S(2)}) collective-permute-start(bf16[160,128]{1,0:T(8,128)(2,1)S(1)} %get-tuple-element.25), channel_id=1, source_target_pairs={{0,2},{1,3},{2,0},{3,1},{4,6},{5,7},{6,4},{7,5},{8,10},{9,11},{10,... | collective-permute-start | bytes 122888 | tf_op jit(solution)/shard_map/ppermute | solution.py:386
  8.4 0.3 %collective-permute-start.4 = (bf16[160,128]{1,0:T(8,128)(2,1)S(1)}, bf16[160,128]{1,0:T(8,128)(2,1)S(1)}, u32[]{:S(2)}, u32[]{:S(2)}) collective-permute-start(bf16[160,128]{1,0:T(8,128)(2,1)S(1)} %get-tuple-element.26), channel_id=1, source_target_pairs={{0,16},{1,17},{2,18},{3,19},{4,20},{5,21},{6,22},{7,23},{8,24},{9,... | collective-permute-start | bytes 122888 | tf_op jit(solution)/shard_map/ppermute | solution.py:387
  8.7 2.1 %collective-permute-start.2 = (bf16[2,160,128]{2,1,0:T(8,128)(2,1)S(1)}, bf16[2,160,128]{2,1,0:T(8,128)(2,1)S(1)}, u32[]{:S(2)}, u32[]{:S(2)}) collective-permute-start(bf16[2,160,128]{2,1,0:T(8,128)(2,1)S(1)} %get-tuple-element.24), channel_id=1, source_target_pairs={{0,1},{1,0},{2,3},{3,2},{4,5},{5,4},{6,7},{7,6},{8,9},{9,8},{10,11... | collective-permute-start | bytes 245768 | tf_op jit(solution)/shard_map/ppermute | solution.py:391
  10.9 1.7 %collective-permute-done.3.xb_ref = bf16[160,128]{1,0:T(8,128)(2,1)S(1)} collective-permute-done((bf16[160,128]{1,0:T(8,128)(2,1)S(1)}, bf16[160,128]{1,0:T(8,128)(2,1)S(1)}, u32[]{:S(2)}, u32[]{:S(2)}) %collective-permute-start.3) | collective-permute-done | bytes 40992 | tf_op jit(solution)/shard_map/ppermute | solution.py:386
  12.6 0.0 collective-permute-done.4.xa_ref
  12.6 0.1 shard_map.31
  12.7 2.2 %collective-permute-start.5 = (bf16[80,128]{1,0:T(8,128)(2,1)S(1)}, bf16[80,128]{1,0:T(8,128)(2,1)S(1)}, u32[]{:S(2)}, u32[]{:S(2)}) collective-permute-start(bf16[80,128]{1,0:T(8,128)(2,1)S(1)} %shard_map.31), channel_id=1, source_target_pairs={{0,1},{1,0},{2,3},{3,2},{4,5},{5,4},{6,7},{7,6},{8,9},{9,8},{10,11... | collective-permute-start | bytes 61448 | tf_op jit(solution)/shard_map/ppermute | solution.py:391
  14.8 2.8 %shard_map.32 = (bf16[6,2,4,128,128]{4,3,2,1,0:T(8,128)(2,1)}, bf16[6,4,128,128]{3,2,1,0:T(8,128)(2,1)S(1)}, bf16[128,128]{1,0:T(8,128)(2,1)S(1)}, f32[32,256]{1,0:T(8,128)S(1)}) custom-call(bf16[160,128]{1,0:T(8,128)(2,1)S(1)} %collective-permute-done.3.xb_ref, bf16[160,128]{1,0:T(8,128)(2,1)S(1)} %collective-permute-done.4.xa_ref, ...), custom_call_target="tpu_custom_call" | custom-call | flops 1000000000 | bytes 4000000 | tf_op jit(solution)/shard_map/pallas_call | solution.py:404
  17.6 0.4 %collective-permute-done.5.h_ref = bf16[80,128]{1,0:T(8,128)(2,1)S(1)} collective-permute-done((bf16[80,128]{1,0:T(8,128)(2,1)S(1)}, bf16[80,128]{1,0:T(8,128)(2,1)S(1)}, u32[]{:S(2)}, u32[]{:S(2)}) %collective-permute-start.5) | collective-permute-done | bytes 20512 | tf_op jit(solution)/shard_map/ppermute | solution.py:391
  18.0 0.0 collective-permute-done.2.z_ref
  18.0 1.8 %shard_map.33 = bf16[6,2,4,128,128]{4,3,2,1,0:T(8,128)(2,1)} custom-call(bf16[2,160,128]{2,1,0:T(8,128)(2,1)S(1)} %collective-permute-done.2.z_ref, bf16[80,128]{1,0:T(8,128)(2,1)S(1)} %collective-permute-done.5.h_ref, bf16[6,4,128,128]{3,2,1,0:T(8,128)(2,1)S(1)} %get-tuple-element.27.f_ref, ...), custom_call_target="tpu_custom_call", output_to_operand_aliasing={{}: (6, {})} | custom-call | tf_op jit(solution)/shard_map/pallas_call | solution.py:419
Async XLA Ops:
  0.8 5.6 %collective-permute-start = (bf16[6,16,128]{2,1,0:T(8,128)(2,1)S(1)}, bf16[6,16,128]{2,1,0:T(8,128)(2,1)S(1)}, u32[]{:S(2)}, u32[]{:S(2)}) collective-permute-start(bf16[6,16,128]{2,1,0:T(8,128)(2,1)S(1)} %get-tuple-element.18), channel_id=1, source_target_pairs={{0,2},{1,3},{2,0},{3,1},{4,6},{5,7},{6,4},{7,5},{8,10},{9,11},{10,... | collective-permute-start | bytes 73736 | tf_op jit(solution)/shard_map/ppermute | solution.py:387
  1.0 5.8 %collective-permute-start.1 = (bf16[6,16,128]{2,1,0:T(8,128)(2,1)S(1)}, bf16[6,16,128]{2,1,0:T(8,128)(2,1)S(1)}, u32[]{:S(2)}, u32[]{:S(2)}) collective-permute-start(bf16[6,16,128]{2,1,0:T(8,128)(2,1)S(1)} %get-tuple-element.19), channel_id=1, source_target_pairs={{0,16},{1,17},{2,4},{3,5},{4,2},{5,3},{6,8},{7,9},{8,6},{9,7},{10,... | collective-permute-start | bytes 73736 | tf_op jit(solution)/shard_map/ppermute | solution.py:386
  6.9 5.6 %collective-permute-start.3 = (bf16[160,128]{1,0:T(8,128)(2,1)S(1)}, bf16[160,128]{1,0:T(8,128)(2,1)S(1)}, u32[]{:S(2)}, u32[]{:S(2)}) collective-permute-start(bf16[160,128]{1,0:T(8,128)(2,1)S(1)} %get-tuple-element.25), channel_id=1, source_target_pairs={{0,2},{1,3},{2,0},{3,1},{4,6},{5,7},{6,4},{7,5},{8,10},{9,11},{10,... | collective-permute-start | bytes 122888 | tf_op jit(solution)/shard_map/ppermute | solution.py:386
  8.4 4.1 %collective-permute-start.4 = (bf16[160,128]{1,0:T(8,128)(2,1)S(1)}, bf16[160,128]{1,0:T(8,128)(2,1)S(1)}, u32[]{:S(2)}, u32[]{:S(2)}) collective-permute-start(bf16[160,128]{1,0:T(8,128)(2,1)S(1)} %get-tuple-element.26), channel_id=1, source_target_pairs={{0,16},{1,17},{2,18},{3,19},{4,20},{5,21},{6,22},{7,23},{8,24},{9,... | collective-permute-start | bytes 122888 | tf_op jit(solution)/shard_map/ppermute | solution.py:387
  8.7 9.3 %collective-permute-start.2 = (bf16[2,160,128]{2,1,0:T(8,128)(2,1)S(1)}, bf16[2,160,128]{2,1,0:T(8,128)(2,1)S(1)}, u32[]{:S(2)}, u32[]{:S(2)}) collective-permute-start(bf16[2,160,128]{2,1,0:T(8,128)(2,1)S(1)} %get-tuple-element.24), channel_id=1, source_target_pairs={{0,1},{1,0},{2,3},{3,2},{4,5},{5,4},{6,7},{7,6},{8,9},{9,8},{10,11... | collective-permute-start | bytes 245768 | tf_op jit(solution)/shard_map/ppermute | solution.py:391
  12.7 5.3 %collective-permute-start.5 = (bf16[80,128]{1,0:T(8,128)(2,1)S(1)}, bf16[80,128]{1,0:T(8,128)(2,1)S(1)}, u32[]{:S(2)}, u32[]{:S(2)}) collective-permute-start(bf16[80,128]{1,0:T(8,128)(2,1)S(1)} %shard_map.31), channel_id=1, source_target_pairs={{0,1},{1,0},{2,3},{3,2},{4,5},{5,4},{6,7},{7,6},{8,9},{9,8},{10,11... | collective-permute-start | bytes 61448 | tf_op jit(solution)/shard_map/ppermute | solution.py:391

commit v8 on v7

--- a/solution.py
+++ b/solution.py
@@ -218,10 +218,11 @@
         w["scale"][1, half] = pltpu.roll(part, 64, 1).reshape(4, 8, 128)
 
 
-def spectra(first, slot_f, sections, edges, c, w):
+def spectra(first, sections, edges, c, w):
     lane = lanes((64, 128))
     zero_slot = lane % 32 == 0
     sides = c["sides"]
+    rows = []
     for s, block in enumerate(sections):
         q = s % 4
         gap0 = jnp.zeros((16 * q, 256), BF16)
@@ -229,14 +230,14 @@
         one, two = (sides[:16], sides[16:]) if s < 4 else (sides[16:], sides[:16])
         pieces = [c["own"], gap0, one, gap1, gap0, two, gap1]
         table = jnp.concatenate([p for p in pieces if p.shape[0]], 0)
-        w["g"][s] = dot(jnp.concatenate([block, edges[s // 4]], 1), table)
+        rows.append(dot(jnp.concatenate([block, edges[s // 4]], 1), table))
     special = jnp.zeros((64, 128), F32)
     for s in range(len(sections)):
         for pair in range(2):
             columns = []
             for i in (2 * pair, 2 * pair + 1):
-                re = w["g"][s, 32 * i : 32 * i + 64, :128]
-                im = w["g"][s, 32 * i : 32 * i + 64, 128:]
+                re = rows[s][32 * i : 32 * i + 64, :128]
+                im = rows[s][32 * i : 32 * i + 64, 128:]
                 centre = jnp.sum(re, 0, keepdims=True) * (1.0 / 64)
                 re = jnp.where(zero_slot, re - centre, re)
                 slot = 4 * (s + first) + i
@@ -245,20 +246,20 @@
                 columns.append(jnp.concatenate([re, im], 0).astype(BF16))
             f = dot(c["forward"], jnp.concatenate(columns, 1)).astype(BF16)
             for n, i in enumerate((2 * pair, 2 * pair + 1)):
-                w["f"][s + slot_f, i] = f[:, 128 * n : 128 * n + 128]
+                w["f"][s, i] = f[:, 128 * n : 128 * n + 128]
     return dot(c["forward"][:, :64], special.astype(BF16)).astype(BF16)
 
 
-def maps(lo, hi, f32, offset, c, w, o_ref):
+def maps(lo, hi, here32, there32, spectrum, c, w, o_ref):
     lane = lanes((64, 128))
     zero_slot = lane % 32 == 0
     low = lanes((32, 128)) < 64
-    f32 = f32.astype(F32)
-    re, im = f32[:64], f32[64:]
+    here32, there32 = here32.astype(F32), there32.astype(F32)
+    re_p, im_p = there32[:64], there32[64:]
     h32 = []
     for k in range(2):
-        re_p = pltpu.roll(re, 128 - 4 * (k + 1), 1)
-        im_p = pltpu.roll(im, 128 - 4 * (k + 1), 1)
+        here = pltpu.roll(here32, 4 * (k + 1), 1)
+        re, im = here[:64], here[64:]
         q = jnp.concatenate([re * re_p + im * im_p, im * re_p - re * im_p], 0).astype(BF16)
         h32.append(dot(c["inverse"][:64], q))
 
@@ -273,8 +274,8 @@
         for half in range(2):
             columns = []
             for i in (2 * half, 2 * half + 1):
-                here = w["f"][s - offset, i].astype(F32)
-                there = w["f"][s + k + 1 - offset, i].astype(F32)
+                here = spectrum(s, i).astype(F32)
+                there = spectrum(s + k + 1, i).astype(F32)
                 f_re, f_im, p_re, p_im = here[:64], here[64:], there[:64], there[64:]
                 q = jnp.concatenate([f_re * p_re + f_im * p_im, f_im * p_re - f_re * p_im], 0)
                 columns.append(q.astype(BF16))
@@ -286,7 +287,7 @@
         even, odd = [], []
         for i in range(4):
             h = spectra[i // 2][:, 128 * (i % 2) : 128 * (i % 2) + 128]
-            special = pltpu.roll(h32[k], (128 - 4 * s - i) % 128, 1)
+            special = pltpu.roll(h32[k], 128 - 4 * (s + k + 1) - i, 1)
             h_im = jnp.where(zero_slot, special, h[64:])
             h_cat = jnp.concatenate([h[:64], h_im], 1).astype(BF16)
             even.append(h_cat[:32])
@@ -322,7 +323,6 @@
 
 
 SCRATCH = dict(
-    g=lambda n: pltpu.VMEM((n, 160, 256), F32),
     mu=lambda n: pltpu.VMEM((5, 8, 256), F32),
     sq=lambda n: pltpu.VMEM((5, 8, 256), F32),
     scale=lambda n: pltpu.VMEM((2, 2, 4, 8, 128), F32),
@@ -337,30 +337,30 @@
     top, bottom = low_high(ya_ref[...], yb_ref[...], "gy")
     sections = [jnp.concatenate([top[s], s_ref[s], bottom[s]], 0) for s in range(6)]
     edges = side_tiles(xa_ref, xb_ref)
-    f32 = spectra(0, 0, sections, edges, c, w)
+    f32 = spectra(0, sections, edges, c, w)
     scale = scales(0, sections, edges, c, w)
     store_scales(scale, w)
     f32_ref[...] = f32
     scale_ref[...] = scale
-    maps(0, 9, f32, 0, c, w, o_ref)
+    maps(0, 9, f32, f32, lambda s, i: f_ref[s, i], c, w, o_ref)
 
 
 def rest_kernel(z_ref, h_ref, f_ref, f32_ref, scale_ref, t_ref, _, o_ref, *scratch):
     c = Tables(t_ref)
     w = dict(zip((*SCRATCH, "f", "o", "sem"), scratch))
     flag = jnp.where(lax.axis_index("gz") == 0, 1.0, 0.0)
-    w["f"][0] = f_ref[4]
-    w["f"][1] = f_ref[5]
     sections = [z_ref[0], z_ref[1]]
     sides = h_ref[...]
     lower = pltpu.roll(sides.astype(F32), 96, 1).astype(BF16)
     edges = [jnp.concatenate([sides, lower], 0)]
-    extra = spectra(6, 2, sections, edges, c, w)
+    extra = spectra(6, sections, edges, c, w)
     scale = scales(6, sections, edges, c, w) * flag
     scale = jnp.where(lax.broadcasted_iota(jnp.int32, (32, 256), 0) % 8 >= 6, scale, scale_ref[...])
     store_scales(scale, w)
-    f32 = jnp.where(lanes((128, 128)) % 32 >= 24, extra.astype(F32), f32_ref[...].astype(F32))
-    maps(9, 12, f32, 4, c, w, o_ref)
+    def spectrum(s, i):
+        return f_ref[s, i] if s < 6 else w["f"][s - 6, i]
+
+    maps(9, 12, f32_ref[...], extra, spectrum, c, w, o_ref)
 
 
 def exchange(value_a, value_b, axis):
@@ -423,7 +423,7 @@
         out_specs=HBM,
         scratch_shapes=scratch
         + [
-            pltpu.VMEM((4, 4, 128, 128), BF16),
+            pltpu.VMEM((2, 4, 128, 128), BF16),
             pltpu.VMEM((3, 4, 128, 128), BF16),
             pltpu.SemaphoreType.DMA((3,)),
         ],

time: 20.1 us -> 20.1 us (level)
  no operation moved by 1% of the time
where the time goes in v8:
time: 20.1 us; the launch traced here: 19.8 us
  starting transfers between devices  10.3 us (51%)
  Pallas kernels  6.86 us (34%)
  waiting for transfers between devices  2.56 us (13%)
    ppermute x2, starting transfers between devices, exchange(): value_b = lax.ppermute(value_b, AXES, pairs(1))  5.53 us
    ppermute x2, starting transfers between devices, other(): return lax.ppermute(value, 'gz', [(0, 1), (1, 0)])  4.31 us
    pallas_call x1, Pallas kernels, compute(): pl.pallas_call(own_kernel, out_shape=(shaped(6, 2, 4, 128, 128), shaped(6...  2.78 us
    ppermute x2, waiting for transfers between devices, exchange(): value_b = lax.ppermute(value_b, AXES, pairs(1))  2.18 us
    pallas_call x1, Pallas kernels, compute(): pl.pallas_call(rest_kernel, out_shape=shaped(6, 2, 4, 128, 128), in_specs...  1.79 us
    pallas_call x1, Pallas kernels, local(): pl.pallas_call(stage_kernel, out_shape=(shaped(*sections.shape), shaped(*...  1.31 us
    pallas_call x1, Pallas kernels, local(): pl.pallas_call(first_kernel, out_shape=(rows, rows), in_specs=[HBM], out_...  0.77 us
    ppermute x2, starting transfers between devices, exchange(): return (lax.ppermute(value_a, AXES, pairs(0)), value_b)  0.48 us
  transfers between devices with their start and end apart: 6, of which 3 were waited for; matrix products, arithmetic and copies ran while one was open for 0% of the time, Pallas kernels for 21%

profile of v8, /device:TPU:98, one launch (start us, length us, event | category | flops | bytes accessed | tf_op | source)
XLA Modules:
  0.0 19.8 jit_solution(4448119209652822087)
XLA Ops:
  0.0 0.8 %shard_map.28 = (bf16[6,16,128]{2,1,0:T(8,128)(2,1)S(1)}, bf16[6,16,128]{2,1,0:T(8,128)(2,1)S(1)}) custom-call(bf16[6,128,128]{2,1,0:T(8,128)(2,1)} %s_hbm.3), custom_call_target="tpu_custom_call" | custom-call | tf_op jit(solution)/shard_map/pallas_call | solution.py:439
  0.8 0.2 collective-permute-start
  1.0 4.0 %collective-permute-start.1 = (bf16[6,16,128]{2,1,0:T(8,128)(2,1)S(1)}, bf16[6,16,128]{2,1,0:T(8,128)(2,1)S(1)}, u32[]{:S(2)}, u32[]{:S(2)}) collective-permute-start(bf16[6,16,128]{2,1,0:T(8,128)(2,1)S(1)} %get-tuple-element.19), channel_id=1, source_target_pairs={{0,16},{1,17},{2,4},{3,5},{4,2},{5,3},{6,8},{7,9},{8,6},{9,7},{10,... | collective-permute-start | bytes 73736 | tf_op jit(solution)/shard_map/ppermute | solution.py:386
  5.0 1.3 %shard_map.29 = (bf16[6,128,128]{2,1,0:T(8,128)(2,1)S(1)}, bf16[3648,128]{1,0:T(8,128)(2,1)S(1)}, bf16[128,128]{1,0:T(8,128)(2,1)S(1)}, bf16[128,128]{1,0:T(8,128)(2,1)S(1)}) custom-call(bf16[6,128,128]{2,1,0:T(8,128)(2,1)} %s_hbm.3, bf16[3648,128]{1,0:T(8,128)(2,1)} %constant.2.clone.t_hbm), custom_call_target="tpu_custom_call" | custom-call | bytes 2000000 | tf_op jit(solution)/shard_map/pallas_call | solution.py:448
  6.3 0.0 collective-permute-done.ya_ref
  6.3 0.5 %collective-permute-done.1.yb_ref = bf16[6,16,128]{2,1,0:T(8,128)(2,1)S(1)} collective-permute-done((bf16[6,16,128]{2,1,0:T(8,128)(2,1)S(1)}, bf16[6,16,128]{2,1,0:T(8,128)(2,1)S(1)}, u32[]{:S(2)}, u32[]{:S(2)}) %collective-permute-start.1) | collective-permute-done | bytes 24608 | tf_op jit(solution)/shard_map/ppermute | solution.py:386
  6.8 0.1 shard_map.30
  6.9 1.5 %collective-permute-start.3 = (bf16[160,128]{1,0:T(8,128)(2,1)S(1)}, bf16[160,128]{1,0:T(8,128)(2,1)S(1)}, u32[]{:S(2)}, u32[]{:S(2)}) collective-permute-start(bf16[160,128]{1,0:T(8,128)(2,1)S(1)} %get-tuple-element.25), channel_id=1, source_target_pairs={{0,2},{1,3},{2,0},{3,1},{4,6},{5,7},{6,4},{7,5},{8,10},{9,11},{10,... | collective-permute-start | bytes 122888 | tf_op jit(solution)/shard_map/ppermute | solution.py:386
  8.4 0.3 %collective-permute-start.4 = (bf16[160,128]{1,0:T(8,128)(2,1)S(1)}, bf16[160,128]{1,0:T(8,128)(2,1)S(1)}, u32[]{:S(2)}, u32[]{:S(2)}) collective-permute-start(bf16[160,128]{1,0:T(8,128)(2,1)S(1)} %get-tuple-element.26), channel_id=1, source_target_pairs={{0,16},{1,17},{2,18},{3,19},{4,20},{5,21},{6,22},{7,23},{8,24},{9,... | collective-permute-start | bytes 122888 | tf_op jit(solution)/shard_map/ppermute | solution.py:387
  8.7 2.1 %collective-permute-start.2 = (bf16[2,160,128]{2,1,0:T(8,128)(2,1)S(1)}, bf16[2,160,128]{2,1,0:T(8,128)(2,1)S(1)}, u32[]{:S(2)}, u32[]{:S(2)}) collective-permute-start(bf16[2,160,128]{2,1,0:T(8,128)(2,1)S(1)} %get-tuple-element.24), channel_id=1, source_target_pairs={{0,1},{1,0},{2,3},{3,2},{4,5},{5,4},{6,7},{7,6},{8,9},{9,8},{10,11... | collective-permute-start | bytes 245768 | tf_op jit(solution)/shard_map/ppermute | solution.py:391
  10.9 1.7 %collective-permute-done.3.xb_ref = bf16[160,128]{1,0:T(8,128)(2,1)S(1)} collective-permute-done((bf16[160,128]{1,0:T(8,128)(2,1)S(1)}, bf16[160,128]{1,0:T(8,128)(2,1)S(1)}, u32[]{:S(2)}, u32[]{:S(2)}) %collective-permute-start.3) | collective-permute-done | bytes 40992 | tf_op jit(solution)/shard_map/ppermute | solution.py:386
  12.6 0.0 collective-permute-done.4.xa_ref
  12.6 0.1 shard_map.31
  12.7 2.2 %collective-permute-start.5 = (bf16[80,128]{1,0:T(8,128)(2,1)S(1)}, bf16[80,128]{1,0:T(8,128)(2,1)S(1)}, u32[]{:S(2)}, u32[]{:S(2)}) collective-permute-start(bf16[80,128]{1,0:T(8,128)(2,1)S(1)} %shard_map.31), channel_id=1, source_target_pairs={{0,1},{1,0},{2,3},{3,2},{4,5},{5,4},{6,7},{7,6},{8,9},{9,8},{10,11... | collective-permute-start | bytes 61448 | tf_op jit(solution)/shard_map/ppermute | solution.py:391
  14.8 2.8 %shard_map.32 = (bf16[6,2,4,128,128]{4,3,2,1,0:T(8,128)(2,1)}, bf16[6,4,128,128]{3,2,1,0:T(8,128)(2,1)S(1)}, bf16[128,128]{1,0:T(8,128)(2,1)S(1)}, f32[32,256]{1,0:T(8,128)S(1)}) custom-call(bf16[160,128]{1,0:T(8,128)(2,1)S(1)} %collective-permute-done.3.xb_ref, bf16[160,128]{1,0:T(8,128)(2,1)S(1)} %collective-permute-done.4.xa_ref, ...), custom_call_target="tpu_custom_call" | custom-call | flops 1000000000 | bytes 4000000 | tf_op jit(solution)/shard_map/pallas_call | solution.py:404
  17.6 0.4 %collective-permute-done.5.h_ref = bf16[80,128]{1,0:T(8,128)(2,1)S(1)} collective-permute-done((bf16[80,128]{1,0:T(8,128)(2,1)S(1)}, bf16[80,128]{1,0:T(8,128)(2,1)S(1)}, u32[]{:S(2)}, u32[]{:S(2)}) %collective-permute-start.5) | collective-permute-done | bytes 20512 | tf_op jit(solution)/shard_map/ppermute | solution.py:391
  18.0 0.0 collective-permute-done.2.z_ref
  18.0 1.8 %shard_map.33 = bf16[6,2,4,128,128]{4,3,2,1,0:T(8,128)(2,1)} custom-call(bf16[2,160,128]{2,1,0:T(8,128)(2,1)S(1)} %collective-permute-done.2.z_ref, bf16[80,128]{1,0:T(8,128)(2,1)S(1)} %collective-permute-done.5.h_ref, bf16[6,4,128,128]{3,2,1,0:T(8,128)(2,1)S(1)} %get-tuple-element.27.f_ref, ...), custom_call_target="tpu_custom_call", output_to_operand_aliasing={{}: (6, {})} | custom-call | tf_op jit(solution)/shard_map/pallas_call | solution.py:419
Async XLA Ops:
  0.8 5.6 %collective-permute-start = (bf16[6,16,128]{2,1,0:T(8,128)(2,1)S(1)}, bf16[6,16,128]{2,1,0:T(8,128)(2,1)S(1)}, u32[]{:S(2)}, u32[]{:S(2)}) collective-permute-start(bf16[6,16,128]{2,1,0:T(8,128)(2,1)S(1)} %get-tuple-element.18), channel_id=1, source_target_pairs={{0,2},{1,3},{2,0},{3,1},{4,6},{5,7},{6,4},{7,5},{8,10},{9,11},{10,... | collective-permute-start | bytes 73736 | tf_op jit(solution)/shard_map/ppermute | solution.py:387
  1.0 5.8 %collective-permute-start.1 = (bf16[6,16,128]{2,1,0:T(8,128)(2,1)S(1)}, bf16[6,16,128]{2,1,0:T(8,128)(2,1)S(1)}, u32[]{:S(2)}, u32[]{:S(2)}) collective-permute-start(bf16[6,16,128]{2,1,0:T(8,128)(2,1)S(1)} %get-tuple-element.19), channel_id=1, source_target_pairs={{0,16},{1,17},{2,4},{3,5},{4,2},{5,3},{6,8},{7,9},{8,6},{9,7},{10,... | collective-permute-start | bytes 73736 | tf_op jit(solution)/shard_map/ppermute | solution.py:386
  6.9 5.6 %collective-permute-start.3 = (bf16[160,128]{1,0:T(8,128)(2,1)S(1)}, bf16[160,128]{1,0:T(8,128)(2,1)S(1)}, u32[]{:S(2)}, u32[]{:S(2)}) collective-permute-start(bf16[160,128]{1,0:T(8,128)(2,1)S(1)} %get-tuple-element.25), channel_id=1, source_target_pairs={{0,2},{1,3},{2,0},{3,1},{4,6},{5,7},{6,4},{7,5},{8,10},{9,11},{10,... | collective-permute-start | bytes 122888 | tf_op jit(solution)/shard_map/ppermute | solution.py:386
  8.4 4.1 %collective-permute-start.4 = (bf16[160,128]{1,0:T(8,128)(2,1)S(1)}, bf16[160,128]{1,0:T(8,128)(2,1)S(1)}, u32[]{:S(2)}, u32[]{:S(2)}) collective-permute-start(bf16[160,128]{1,0:T(8,128)(2,1)S(1)} %get-tuple-element.26), channel_id=1, source_target_pairs={{0,16},{1,17},{2,18},{3,19},{4,20},{5,21},{6,22},{7,23},{8,24},{9,... | collective-permute-start | bytes 122888 | tf_op jit(solution)/shard_map/ppermute | solution.py:387
  8.7 9.3 %collective-permute-start.2 = (bf16[2,160,128]{2,1,0:T(8,128)(2,1)S(1)}, bf16[2,160,128]{2,1,0:T(8,128)(2,1)S(1)}, u32[]{:S(2)}, u32[]{:S(2)}) collective-permute-start(bf16[2,160,128]{2,1,0:T(8,128)(2,1)S(1)} %get-tuple-element.24), channel_id=1, source_target_pairs={{0,1},{1,0},{2,3},{3,2},{4,5},{5,4},{6,7},{7,6},{8,9},{9,8},{10,11... | collective-permute-start | bytes 245768 | tf_op jit(solution)/shard_map/ppermute | solution.py:391
  12.7 5.3 %collective-permute-start.5 = (bf16[80,128]{1,0:T(8,128)(2,1)S(1)}, bf16[80,128]{1,0:T(8,128)(2,1)S(1)}, u32[]{:S(2)}, u32[]{:S(2)}) collective-permute-start(bf16[80,128]{1,0:T(8,128)(2,1)S(1)} %shard_map.31), channel_id=1, source_target_pairs={{0,1},{1,0},{2,3},{3,2},{4,5},{5,4},{6,7},{7,6},{8,9},{9,8},{10,11... | collective-permute-start | bytes 61448 | tf_op jit(solution)/shard_map/ppermute | solution.py:391

commit v9 on v8

--- a/solution.py
+++ b/solution.py
@@ -142,7 +142,7 @@
     tables.wait()
 
 
-def sides_kernel(ya_ref, yb_ref, s_ref, l_ref, r_ref, _, a_ref, b_ref, z_ref):
+def sides_kernel(ya_ref, yb_ref, s_ref, l_ref, r_ref, _, a_ref, b_ref):
     odd = lax.axis_index("gx") % 2 == 1
     top, bottom = low_high(ya_ref[...], yb_ref[...], "gy")
     left, right = pack_sides([jnp.concatenate([top[s], bottom[s]], 0) for s in range(6)])
@@ -150,6 +150,10 @@
     right = jnp.concatenate([right[:16], r_ref[...], right[16:]], 0)
     a_ref[...] = jnp.where(odd, left, right)
     b_ref[...] = jnp.where(odd, right, left)
+
+
+def tall_kernel(ya_ref, yb_ref, s_ref, z_ref):
+    top, bottom = low_high(ya_ref[:2], yb_ref[:2], "gy")
     for s in range(2):
         z_ref[s] = jnp.concatenate([top[s], s_ref[s], bottom[s]], 0)
 
@@ -454,15 +458,23 @@
         compiler_params=params(8),
         cost_estimate=pl.CostEstimate(flops=0, bytes_accessed=2 * 10**6, transcendentals=0),
     )(pixels, pltpu.with_memory_space_constraint(table, pltpu.HBM))
-    xa, xb, z = pl.pallas_call(
+    xa, xb = pl.pallas_call(
         sides_kernel,
-        out_shape=(side, side, shaped(2, 160, 128)),
+        out_shape=(side, side),
         in_specs=[VMEM] * 6,
-        out_specs=(VMEM,) * 3,
+        out_specs=(VMEM,) * 2,
         compiler_params=params(8),
     )(ya, yb, sections, left, right, table)
     xa, xb = exchange(xa, xb, "gx")
-    z = other(z)
+    z = other(
+        pl.pallas_call(
+            tall_kernel,
+            out_shape=shaped(2, 160, 128),
+            in_specs=[VMEM] * 3,
+            out_specs=VMEM,
+            compiler_params=params(8),
+        )(ya, yb, sections)
+    )
     sides = pl.pallas_call(
         halo_kernel,
         out_shape=shaped(80, 128),

time: 20.1 us -> 20 us (level)
  no operation moved by 1% of the time
where the time goes in v9:
time: 20 us; the launch traced here: 19.8 us
  starting transfers between devices  10.4 us (52%)
  Pallas kernels  6.86 us (34%)
  waiting for transfers between devices  2.44 us (12%)
    ppermute x2, starting transfers between devices, exchange(): value_b = lax.ppermute(value_b, AXES, pairs(1))  5.54 us
    ppermute x2, starting transfers between devices, other(): return lax.ppermute(value, 'gz', [(0, 1), (1, 0)])  4.4 us
    pallas_call x1, Pallas kernels, compute(): pl.pallas_call(own_kernel, out_shape=(shaped(6, 2, 4, 128, 128), shaped(6...  2.78 us
    ppermute x2, waiting for transfers between devices, exchange(): value_b = lax.ppermute(value_b, AXES, pairs(1))  2.06 us
    pallas_call x1, Pallas kernels, compute(): pl.pallas_call(rest_kernel, out_shape=shaped(6, 2, 4, 128, 128), in_specs...  1.78 us
    pallas_call x1, Pallas kernels, local(): pl.pallas_call(stage_kernel, out_shape=(shaped(*sections.shape), shaped(*...  1.31 us
    pallas_call x1, Pallas kernels, local(): pl.pallas_call(first_kernel, out_shape=(rows, rows), in_specs=[HBM], out_...  0.77 us
    ppermute x2, starting transfers between devices, exchange(): return (lax.ppermute(value_a, AXES, pairs(0)), value_b)  0.47 us
  transfers between devices with their start and end apart: 6, of which 3 were waited for; matrix products, arithmetic and copies ran while one was open for 0% of the time, Pallas kernels for 21%

profile of v9, /device:TPU:98, one launch (start us, length us, event | category | flops | bytes accessed | tf_op | source)
XLA Modules:
  0.0 19.8 jit_solution(12124643473971334958)
XLA Ops:
  0.0 0.8 %shard_map.28 = (bf16[6,16,128]{2,1,0:T(8,128)(2,1)S(1)}, bf16[6,16,128]{2,1,0:T(8,128)(2,1)S(1)}) custom-call(bf16[6,128,128]{2,1,0:T(8,128)(2,1)} %s_hbm.3), custom_call_target="tpu_custom_call" | custom-call | tf_op jit(solution)/shard_map/pallas_call | solution.py:443
  0.8 0.2 collective-permute-start
  1.0 4.0 %collective-permute-start.1 = (bf16[6,16,128]{2,1,0:T(8,128)(2,1)S(1)}, bf16[6,16,128]{2,1,0:T(8,128)(2,1)S(1)}, u32[]{:S(2)}, u32[]{:S(2)}) collective-permute-start(bf16[6,16,128]{2,1,0:T(8,128)(2,1)S(1)} %get-tuple-element.18), channel_id=1, source_target_pairs={{0,16},{1,17},{2,4},{3,5},{4,2},{5,3},{6,8},{7,9},{8,6},{9,7},{10,... | collective-permute-start | bytes 73736 | tf_op jit(solution)/shard_map/ppermute | solution.py:390
  5.0 1.3 %shard_map.29 = (bf16[6,128,128]{2,1,0:T(8,128)(2,1)S(1)}, bf16[3648,128]{1,0:T(8,128)(2,1)S(1)}, bf16[128,128]{1,0:T(8,128)(2,1)S(1)}, bf16[128,128]{1,0:T(8,128)(2,1)S(1)}) custom-call(bf16[6,128,128]{2,1,0:T(8,128)(2,1)} %s_hbm.3, bf16[3648,128]{1,0:T(8,128)(2,1)} %constant.2.clone.t_hbm), custom_call_target="tpu_custom_call" | custom-call | bytes 2000000 | tf_op jit(solution)/shard_map/pallas_call | solution.py:452
  6.3 0.0 collective-permute-done.ya_ref
  6.3 0.5 %collective-permute-done.1.yb_ref = bf16[6,16,128]{2,1,0:T(8,128)(2,1)S(1)} collective-permute-done((bf16[6,16,128]{2,1,0:T(8,128)(2,1)S(1)}, bf16[6,16,128]{2,1,0:T(8,128)(2,1)S(1)}, u32[]{:S(2)}, u32[]{:S(2)}) %collective-permute-start.1) | collective-permute-done | bytes 24608 | tf_op jit(solution)/shard_map/ppermute | solution.py:390
  6.8 0.1 shard_map.31
  6.9 1.5 %collective-permute-start.3 = (bf16[160,128]{1,0:T(8,128)(2,1)S(1)}, bf16[160,128]{1,0:T(8,128)(2,1)S(1)}, u32[]{:S(2)}, u32[]{:S(2)}) collective-permute-start(bf16[160,128]{1,0:T(8,128)(2,1)S(1)} %get-tuple-element.23), channel_id=1, source_target_pairs={{0,2},{1,3},{2,0},{3,1},{4,6},{5,7},{6,4},{7,5},{8,10},{9,11},{10,... | collective-permute-start | bytes 122888 | tf_op jit(solution)/shard_map/ppermute | solution.py:390
  8.4 0.3 %collective-permute-start.4 = (bf16[160,128]{1,0:T(8,128)(2,1)S(1)}, bf16[160,128]{1,0:T(8,128)(2,1)S(1)}, u32[]{:S(2)}, u32[]{:S(2)}) collective-permute-start(bf16[160,128]{1,0:T(8,128)(2,1)S(1)} %get-tuple-element.24), channel_id=1, source_target_pairs={{0,16},{1,17},{2,18},{3,19},{4,20},{5,21},{6,22},{7,23},{8,24},{9,... | collective-permute-start | bytes 122888 | tf_op jit(solution)/shard_map/ppermute | solution.py:391
  8.7 2.2 %collective-permute-start.2 = (bf16[2,160,128]{2,1,0:T(8,128)(2,1)S(1)}, bf16[2,160,128]{2,1,0:T(8,128)(2,1)S(1)}, u32[]{:S(2)}, u32[]{:S(2)}) collective-permute-start(bf16[2,160,128]{2,1,0:T(8,128)(2,1)S(1)} %shard_map.30), channel_id=1, source_target_pairs={{0,1},{1,0},{2,3},{3,2},{4,5},{5,4},{6,7},{7,6},{8,9},{9,8},{10,11... | collective-permute-start | bytes 245768 | tf_op jit(solution)/shard_map/ppermute | solution.py:395
  11.0 1.6 %collective-permute-done.3.xb_ref = bf16[160,128]{1,0:T(8,128)(2,1)S(1)} collective-permute-done((bf16[160,128]{1,0:T(8,128)(2,1)S(1)}, bf16[160,128]{1,0:T(8,128)(2,1)S(1)}, u32[]{:S(2)}, u32[]{:S(2)}) %collective-permute-start.3) | collective-permute-done | bytes 40992 | tf_op jit(solution)/shard_map/ppermute | solution.py:390
  12.6 0.0 collective-permute-done.4.xa_ref
  12.6 0.1 shard_map.32
  12.6 2.2 %collective-permute-start.5 = (bf16[80,128]{1,0:T(8,128)(2,1)S(1)}, bf16[80,128]{1,0:T(8,128)(2,1)S(1)}, u32[]{:S(2)}, u32[]{:S(2)}) collective-permute-start(bf16[80,128]{1,0:T(8,128)(2,1)S(1)} %shard_map.32), channel_id=1, source_target_pairs={{0,1},{1,0},{2,3},{3,2},{4,5},{5,4},{6,7},{7,6},{8,9},{9,8},{10,11... | collective-permute-start | bytes 61448 | tf_op jit(solution)/shard_map/ppermute | solution.py:395
  14.8 2.8 %shard_map.33 = (bf16[6,2,4,128,128]{4,3,2,1,0:T(8,128)(2,1)}, bf16[6,4,128,128]{3,2,1,0:T(8,128)(2,1)S(1)}, bf16[128,128]{1,0:T(8,128)(2,1)S(1)}, f32[32,256]{1,0:T(8,128)S(1)}) custom-call(bf16[160,128]{1,0:T(8,128)(2,1)S(1)} %collective-permute-done.3.xb_ref, bf16[160,128]{1,0:T(8,128)(2,1)S(1)} %collective-permute-done.4.xa_ref, ...), custom_call_target="tpu_custom_call" | custom-call | flops 1000000000 | bytes 4000000 | tf_op jit(solution)/shard_map/pallas_call | solution.py:408
  17.6 0.4 %collective-permute-done.5.h_ref = bf16[80,128]{1,0:T(8,128)(2,1)S(1)} collective-permute-done((bf16[80,128]{1,0:T(8,128)(2,1)S(1)}, bf16[80,128]{1,0:T(8,128)(2,1)S(1)}, u32[]{:S(2)}, u32[]{:S(2)}) %collective-permute-start.5) | collective-permute-done | bytes 20512 | tf_op jit(solution)/shard_map/ppermute | solution.py:395
  18.0 0.0 collective-permute-done.2.z_ref
  18.0 1.8 %shard_map.34 = bf16[6,2,4,128,128]{4,3,2,1,0:T(8,128)(2,1)} custom-call(bf16[2,160,128]{2,1,0:T(8,128)(2,1)S(1)} %collective-permute-done.2.z_ref, bf16[80,128]{1,0:T(8,128)(2,1)S(1)} %collective-permute-done.5.h_ref, bf16[6,4,128,128]{3,2,1,0:T(8,128)(2,1)S(1)} %get-tuple-element.25.f_ref, ...), custom_call_target="tpu_custom_call", output_to_operand_aliasing={{}: (6, {})} | custom-call | tf_op jit(solution)/shard_map/pallas_call | solution.py:423
  (1 shorter events, 0.0 us)
Async XLA Ops:
  0.8 5.6 %collective-permute-start = (bf16[6,16,128]{2,1,0:T(8,128)(2,1)S(1)}, bf16[6,16,128]{2,1,0:T(8,128)(2,1)S(1)}, u32[]{:S(2)}, u32[]{:S(2)}) collective-permute-start(bf16[6,16,128]{2,1,0:T(8,128)(2,1)S(1)} %get-tuple-element.17), channel_id=1, source_target_pairs={{0,2},{1,3},{2,0},{3,1},{4,6},{5,7},{6,4},{7,5},{8,10},{9,11},{10,... | collective-permute-start | bytes 73736 | tf_op jit(solution)/shard_map/ppermute | solution.py:391
  1.0 5.8 %collective-permute-start.1 = (bf16[6,16,128]{2,1,0:T(8,128)(2,1)S(1)}, bf16[6,16,128]{2,1,0:T(8,128)(2,1)S(1)}, u32[]{:S(2)}, u32[]{:S(2)}) collective-permute-start(bf16[6,16,128]{2,1,0:T(8,128)(2,1)S(1)} %get-tuple-element.18), channel_id=1, source_target_pairs={{0,16},{1,17},{2,4},{3,5},{4,2},{5,3},{6,8},{7,9},{8,6},{9,7},{10,... | collective-permute-start | bytes 73736 | tf_op jit(solution)/shard_map/ppermute | solution.py:390
  6.9 5.6 %collective-permute-start.3 = (bf16[160,128]{1,0:T(8,128)(2,1)S(1)}, bf16[160,128]{1,0:T(8,128)(2,1)S(1)}, u32[]{:S(2)}, u32[]{:S(2)}) collective-permute-start(bf16[160,128]{1,0:T(8,128)(2,1)S(1)} %get-tuple-element.23), channel_id=1, source_target_pairs={{0,2},{1,3},{2,0},{3,1},{4,6},{5,7},{6,4},{7,5},{8,10},{9,11},{10,... | collective-permute-start | bytes 122888 | tf_op jit(solution)/shard_map/ppermute | solution.py:390
  8.4 4.1 %collective-permute-start.4 = (bf16[160,128]{1,0:T(8,128)(2,1)S(1)}, bf16[160,128]{1,0:T(8,128)(2,1)S(1)}, u32[]{:S(2)}, u32[]{:S(2)}) collective-permute-start(bf16[160,128]{1,0:T(8,128)(2,1)S(1)} %get-tuple-element.24), channel_id=1, source_target_pairs={{0,16},{1,17},{2,18},{3,19},{4,20},{5,21},{6,22},{7,23},{8,24},{9,... | collective-permute-start | bytes 122888 | tf_op jit(solution)/shard_map/ppermute | solution.py:391
  8.7 9.3 %collective-permute-start.2 = (bf16[2,160,128]{2,1,0:T(8,128)(2,1)S(1)}, bf16[2,160,128]{2,1,0:T(8,128)(2,1)S(1)}, u32[]{:S(2)}, u32[]{:S(2)}) collective-permute-start(bf16[2,160,128]{2,1,0:T(8,128)(2,1)S(1)} %shard_map.30), channel_id=1, source_target_pairs={{0,1},{1,0},{2,3},{3,2},{4,5},{5,4},{6,7},{7,6},{8,9},{9,8},{10,11... | collective-permute-start | bytes 245768 | tf_op jit(solution)/shard_map/ppermute | solution.py:395
  12.6 5.3 %collective-permute-start.5 = (bf16[80,128]{1,0:T(8,128)(2,1)S(1)}, bf16[80,128]{1,0:T(8,128)(2,1)S(1)}, u32[]{:S(2)}, u32[]{:S(2)}) collective-permute-start(bf16[80,128]{1,0:T(8,128)(2,1)S(1)} %shard_map.32), channel_id=1, source_target_pairs={{0,1},{1,0},{2,3},{3,2},{4,5},{5,4},{6,7},{7,6},{8,9},{9,8},{10,11... | collective-permute-start | bytes 61448 | tf_op jit(solution)/shard_map/ppermute | solution.py:395
